TPU v7x, 32 devices: a whole 2x2x4 slice. The times are simulated.
32 devices in a mesh: lat: 4 (over z), lon: 8 (over y, x, core).
Axes of the slice: x: 2, y: 2, z: 4, core: 2. Of those that a mesh axis runs over, the one named last changes fastest.
Arguments:
- tracers: float32 [2, 48, 512, 1024], P(None, None, 'lat', 'lon'), may hold values from -6 to 6
- east_courant: float32 [48, 512, 1024], P(None, 'lat', 'lon'), may hold values from -0.4 to 0.4
- north_courant: float32 [48, 512, 1024], P(None, 'lat', 'lon'), may hold values from -0.4 to 0.4
- diffusivity: float32 [48, 512, 1024], P(None, 'lat', 'lon'), may hold values from 0.05 to 20
- land_sea: int32 [512, 1024], P('lat', 'lon'), may hold values 0 or 1
- fluxes: float32 [6, 262144], P(None, ('lat', 'lon')), may hold values from -6 to 6
- source_cell: int32 [32, 4, 6144], P(('lat', 'lon')), may hold values from 0 to 8191, as said below
- link_weight: float32 [32, 4, 6144], P(('lat', 'lon')), may hold values from 0.05 to 0.3
- target_cell: int32 [32, 4, 6144], P(('lat', 'lon')), may hold values from 0 to 16383, as said below
Outputs:
- stepped: float32 [2, 48, 512, 1024], P(None, None, 'lat', 'lon')
Inputs may be any that keep to these rules, and one draw needn't show every extreme that they name: source_cell[s, n, c] lies in n * 2048 to (n+1) * 2048 - 1; several links may name the same cells. target_cell[d, n, c] has its row in (1 - n // 2) * 64 to that plus 128 // 2 - 1 and its column in (1 - n % 2) * 64 to that plus 128 // 2 - 1.
All inputs are finite; a program needn't handle non-finite values. No bound on the sum of `land_sea` on one device may be relied on, other than what follows from the above.
Results may differ from a plain program's by a relative error of at most 0.00005.
Values sent between devices are 32-bit elements; how exact they have to be, the bound alone decides.
No kernel may reach another device: no remote copies, remote signals or barrier semaphores. Data moves between devices by JAX's collectives and lax.ppermute only.
A program may use at most 192 MiB of HBM per device.

v0:
```python
import functools

import jax
import jax.numpy as jnp
from jax import lax
from jax.experimental import pallas as pl
from jax.experimental.pallas import tpu as pltpu
from jax.sharding import PartitionSpec as P

F32 = jnp.float32
BF16 = jnp.bfloat16
LANES = 128
SUB = 8
TABLE_ROWS = 16


def lane_of(shape):
    return lax.broadcasted_iota(jnp.int32, shape, len(shape) - 1)


def prep_kernel(
    links,
    tracers,
    east_courant,
    north_last,
    fluxes,
    source,
    weight,
    east_msg,
    west_msg,
    north_msg,
    south_msg,
    corner_msg,
    own_msg,
):
    step = pl.program_id(0)
    steps = pl.num_programs(0)
    levels = tracers.shape[1]
    block = tracers.shape[2]
    rows_all = steps * block
    lane = lane_of((SUB, LANES))
    pair = lane // 2
    half = levels // 2
    for rb in range(block // SUB):
        at = pl.ds(rb * SUB, SUB)
        for t in range(2):
            tail = jnp.zeros((SUB, LANES), F32)
            head = jnp.zeros((SUB, LANES), F32)
            for k in range(levels):
                moved = pltpu.roll(tracers[t, k, at, :], 2 * k + 2, 1)
                tail = jnp.where(pair == k, moved, tail)
                head = jnp.where(pair == k + 1, moved, head)
            for j in range(half):
                moved = pltpu.roll(east_courant[t * half + j, at, :], (2 * levels + j + 1) % LANES, 1)
                tail = jnp.where(lane == 2 * levels + j, moved, tail)
            start = pl.multiple_of(t * rows_all + step * block + rb * SUB, SUB)
            east_msg[pl.ds(start, SUB), :] = tail
            west_msg[pl.ds(start, SUB), :] = head

    @pl.when(step == 0)
    def _():
        quarter = fluxes.shape[1] // 4
        places = ((own_msg, 0), (east_msg, 2 * rows_all), (north_msg, 5 * levels), (corner_msg, 0))
        for n, (msg, base) in enumerate(places):
            for f in range(5):
                for u in range(TABLE_ROWS):
                    cut = pl.ds(n * quarter + u * LANES, LANES)
                    row = fluxes[f : f + 1, cut]
                    if f == 1:
                        row = row + fluxes[5:6, cut]
                    msg[pl.ds(base + f * TABLE_ROWS + u, 1), :] = row
            base = base + 5 * TABLE_ROWS
            for c in range(links // LANES):
                cut = pl.ds(c * LANES, LANES)
                msg[pl.ds(base + c, 1), :] = source[n : n + 1, cut].astype(F32)
                msg[pl.ds(base + links // LANES + c, 1), :] = weight[n : n + 1, cut]
        for t in range(2):
            for k in range(levels):
                south_msg[pl.ds(2 * (t * levels + k), 2), :] = tracers[t, k, 0:2, :]

    @pl.when(step == steps - 1)
    def _():
        for t in range(2):
            for k in range(levels):
                north_msg[pl.ds(2 * (t * levels + k), 2), :] = tracers[t, k, block - 2 : block, :]
        for k in range(levels):
            north_msg[pl.ds(4 * levels + k, 1), :] = north_last[k, SUB - 1 : SUB, :]


def prep(tracers, east_courant, north_courant, fluxes, source, weight):
    _, levels, rows, cols = tracers.shape
    links = source.shape[1]
    block = 16
    remap = 5 * TABLE_ROWS + 2 * (links // LANES)
    heights = (2 * rows + remap, 2 * rows, 5 * levels + remap, 4 * levels, remap, remap)
    whole = lambda shape: pl.BlockSpec(shape, lambda i: (0,) * len(shape))
    return pl.pallas_call(
        functools.partial(prep_kernel, links),
        grid=(rows // block,),
        in_specs=[
            pl.BlockSpec((2, levels, block, cols), lambda i: (0, 0, i, 0)),
            pl.BlockSpec((levels, block, cols), lambda i: (0, i, 0)),
            pl.BlockSpec((levels, SUB, cols), lambda i: (0, rows // SUB - 1, 0)),
            whole(fluxes.shape),
            whole(source.shape),
            whole(weight.shape),
        ],
        out_specs=[whole((h, LANES)) for h in heights],
        out_shape=[jax.ShapeDtypeStruct((h, LANES), F32) for h in heights],
        compiler_params=pltpu.CompilerParams(vmem_limit_bytes=32 << 20),
        name="prep",
    )(tracers, east_courant, north_courant, fluxes, source, weight)


def gather_links(msg, base, n, links, picked):
    rows = links // LANES
    for g in range(rows // SUB):
        cells = msg[pl.ds(base + 5 * TABLE_ROWS + g * SUB, SUB), :].astype(jnp.int32)
        weights = msg[pl.ds(base + 5 * TABLE_ROWS + rows + g * SUB, SUB), :]
        low = cells % LANES
        high = (cells // LANES) % TABLE_ROWS
        for f in range(5):
            total = jnp.zeros((SUB, LANES), F32)
            for u in range(TABLE_ROWS):
                row = jnp.broadcast_to(msg[pl.ds(base + f * TABLE_ROWS + u, 1), :], (SUB, LANES))
                found = jnp.take_along_axis(row, low, axis=1, mode="promise_in_bounds")
                total = jnp.where(high == u, found, total)
            picked[f, pl.ds(n * rows + g * SUB, SUB), :] = total * weights


def scatter_links(picked, target, n, links, rows, cols):
    half_rows = rows // 2
    half_cols = cols // 2
    count = links // LANES
    wide = 4 * half_cols
    short = half_rows // 4
    tall_iota = lax.broadcasted_iota(jnp.int32, (wide, LANES), 0)
    short_iota = lax.broadcasted_iota(jnp.int32, (short, LANES), 0)
    total = jnp.zeros((10 * short, wide), F32)
    group = 8
    for g in range(count // group):
        lefts = []
        rights = []
        for c in range(g * group, (g + 1) * group):
            cell = target[n : n + 1, c * LANES : (c + 1) * LANES]
            row = cell // cols - (1 - n // 2) * half_rows
            col = cell % cols - (1 - n % 2) * half_cols
            short_at = jnp.broadcast_to(row % short, (short, LANES)) == short_iota
            wide_at = jnp.broadcast_to(row // short * half_cols + col, (wide, LANES)) == tall_iota
            rights.append(jnp.where(wide_at, 1.0, 0.0).astype(BF16))
            pieces = []
            for f in range(5):
                value = picked[f, pl.ds(n * count + c, 1), :]
                high = value.astype(BF16).astype(F32)
                low = value - high
                for part in (high, low):
                    spread = jnp.broadcast_to(part, (short, LANES))
                    pieces.append(jnp.where(short_at, spread, 0.0).astype(BF16))
            lefts.append(jnp.concatenate(pieces, 0))
        left = jnp.concatenate(lefts, 1)
        right = jnp.concatenate(rights, 1)
        total = total + lax.dot_general(
            left, right, (((1,), (1,)), ((), ())), preferred_element_type=F32
        )
    return total


def main_kernel(
    links,
    chunk_rows,
    tables,
    tracers,
    east_courant,
    north_courant,
    diffusivity,
    land,
    target,
    own_tail,
    own_head,
    from_west,
    from_east,
    from_south,
    from_north,
    from_corner,
    own_remap,
    out,
    cells,
    east,
    north,
    diff,
    values,
    gains,
    flux,
    picked,
    surface,
    left_fix,
    right_fix,
    in_sem,
    out_sem,
):
    _, levels, rows, cols = tracers.shape
    chunks = rows // chunk_rows
    lane = lane_of((SUB, LANES))

    def loads(c):
        part = pl.ds(c * chunk_rows, chunk_rows)
        return [
            pltpu.make_async_copy(
                tracers.at[:, :, part, :],
                cells.at[:, :, pl.ds(SUB + c * chunk_rows, chunk_rows), :],
                in_sem.at[0, c],
            ),
            pltpu.make_async_copy(
                east_courant.at[:, part, :], east.at[:, part, :], in_sem.at[1, c]
            ),
            pltpu.make_async_copy(
                north_courant.at[:, part, :], north.at[:, part, :], in_sem.at[2, c]
            ),
            pltpu.make_async_copy(
                diffusivity.at[:, part, :], diff.at[:, part, :], in_sem.at[3, c]
            ),
        ]

    def store(c):
        part = pl.ds(c * chunk_rows, chunk_rows)
        return pltpu.make_async_copy(
            values.at[:, :, part, :], out.at[:, :, part, :], out_sem.at[c]
        )

    copies = [loads(c) for c in range(chunks)]
    for group in copies:
        for copy in group:
            copy.start()

    places = (
        (own_remap, 0),
        (from_west, 2 * rows),
        (from_south, 5 * levels),
        (from_corner, 0),
    )
    quads = []
    for n, (msg, base) in enumerate(places):
        gather_links(msg, base, n, links, picked)
        quads.append(scatter_links(picked, target, n, links, rows, cols))
    short = rows // 8
    for pair in range(2):
        left = quads[2 * pair + 1]
        right = quads[2 * pair]
        for f in range(5):
            at = 2 * f * short
            one = left[at : at + short] + left[at + short : at + 2 * short]
            two = right[at : at + short] + right[at + short : at + 2 * short]
            for g in range(4):
                half = slice(g // 2 * LANES, g // 2 * LANES + LANES)
                a = one[:, half]
                b = two[:, half]
                if g % 2:
                    a = pltpu.roll(a, LANES // 2, 1)
                else:
                    b = pltpu.roll(b, LANES // 2, 1)
                merged = jnp.where(lane_of((short, LANES)) < LANES // 2, a, b)
                base = (1 - pair) * (rows // 2) + g * short
                surface[f, base : base + short, :] = merged
    for rb in range(rows // SUB):
        at = pl.ds(rb * SUB, SUB)
        s3 = surface[3, at, :]
        s4 = surface[4, at, :]
        surface[3, at, :] = 2.0 * jnp.sqrt(s3 * s3 + s4 * s4)

    even = lane % 2 == 0
    half = levels // 2
    spread = 2 * levels + (lane // 2) % half
    lower = lane // 2 < half
    for rb in range(rows // SUB):
        at = pl.ds(rb * SUB, SUB)
        next_at = pl.ds(rows + rb * SUB, SUB)
        first = jnp.take_along_axis(from_west[at, :], spread, axis=1, mode="promise_in_bounds")
        second = jnp.take_along_axis(from_west[next_at, :], spread, axis=1, mode="promise_in_bounds")
        courant = jnp.where(lower, first, second)
        for t in range(2):
            place = pl.ds(t * rows + rb * SUB, SUB)
            head = own_head[place, :]
            gap = from_east[place, :] - head
            right_fix[t, at, :] = jnp.where(even, -gap, 7.0 * pltpu.roll(gap, 1, 1) - gap)
            west = from_west[place, :]
            west_face = 7.0 * (pltpu.roll(west, LANES - 1, 1) + pltpu.roll(head, LANES - 2, 1)) - (
                west + pltpu.roll(head, LANES - 3, 1)
            )
            left_fix[t, at, :] = jnp.where(even, courant * west_face, own_tail[place, :] - west)

    def halo_rows(k, carry):
        for t in range(2):
            unit = t * levels + k
            below = from_south[pl.ds(2 * unit, 2), :]
            cells[t, k, SUB - 2 : SUB, :] = below
            cells[t, k, SUB + rows : SUB + rows + 2, :] = from_north[pl.ds(2 * unit, 2), :]
            low_two = below[0:1]
            low_one = below[1:2]
            up_one = cells[t, k, SUB : SUB + 1, :]
            up_two = cells[t, k, SUB + 1 : SUB + 2, :]
            courant = from_south[pl.ds(4 * levels + k, 1), :]
            flux[t, k, SUB - 1 : SUB, :] = courant * (7.0 * (low_one + up_one) - (low_two + up_two))
        return carry

    for copy in copies[0]:
        copy.wait()
    lax.fori_loop(0, levels, halo_rows, 0)

    at_right = lane >= LANES - 2
    at_left = lane == 0
    at_last = lane == LANES - 1
    blocks = chunk_rows // SUB

    def advect(t, k, r0):
        here = cells[t, k, SUB + r0 : 2 * SUB + r0, :]
        up_one = pltpu.roll(here, LANES - 1, 1)
        up_two = pltpu.roll(here, LANES - 2, 1)
        low_one = pltpu.roll(here, 1, 1)
        fix_right = pltpu.roll(right_fix[t, r0 : r0 + SUB, :], (2 * LANES - 4 - 2 * k) % LANES, 1)
        fix_left = pltpu.roll(left_fix[t, r0 : r0 + SUB, :], (LANES - 1 - 2 * k) % LANES, 1)
        face = 7.0 * (here + up_one) - (low_one + up_two)
        face = face + jnp.where(at_right, fix_right, jnp.where(at_left, fix_left, 0.0))
        east_flux = east[k, r0 : r0 + SUB, :] * face
        west_flux = pltpu.roll(jnp.where(at_last, fix_left, east_flux), 1, 1)
        low_one = cells[t, k, SUB + r0 - 1 : 2 * SUB + r0 - 1, :]
        up_one = cells[t, k, SUB + r0 + 1 : 2 * SUB + r0 + 1, :]
        up_two = cells[t, k, SUB + r0 + 2 : 2 * SUB + r0 + 2, :]
        face = 7.0 * (here + up_one) - (low_one + up_two)
        north_flux = north[k, r0 : r0 + SUB, :] * face
        flux[t, k, SUB + r0 : 2 * SUB + r0, :] = north_flux
        south_flux = flux[t, k, SUB + r0 - 1 : 2 * SUB + r0 - 1, :]
        change = (east_flux - west_flux) + (north_flux - south_flux)
        return here - change * (1.0 / 12.0)

    for c in range(chunks):
        if c + 1 < chunks:
            for copy in copies[c + 1]:
                copy.wait()
        base = c * chunk_rows

        def forward(k, carry, last=False):
            new = []
            for i in range(blocks):
                r0 = base + i * SUB
                above, lead, heat, salt = carry[4 * i : 4 * i + 4]
                heat_in = advect(0, k, r0) + surface[2, r0 : r0 + SUB, :] * tables[0, k]
                salt_in = advect(1, k, r0)
                if last:
                    inverse = 1.0 / lead
                    below = above
                else:
                    below = diff[k, r0 : r0 + SUB, :] + surface[3, r0 : r0 + SUB, :] * tables[1, k]
                    pivot = lead + below
                    rough = pl.reciprocal(pivot, approx=True)
                    inverse = rough * (2.0 - pivot * rough)
                heat = (heat_in + above * heat) * inverse
                salt = (salt_in + above * salt) * inverse
                values[0, k, r0 : r0 + SUB, :] = heat
                values[1, k, r0 : r0 + SUB, :] = salt
                if not last:
                    gains[k, i * SUB : (i + 1) * SUB, :] = below * inverse
                    lead = 1.0 + below * (lead * inverse)
                new += [below, lead, heat, salt]
            return tuple(new)

        carry = []
        for i in range(blocks):
            r0 = base + i * SUB
            one = jnp.ones((SUB, LANES), F32)
            carry += [one, one, 0.5 * surface[0, r0 : r0 + SUB, :], 0.5 * surface[1, r0 : r0 + SUB, :]]
        carry = lax.fori_loop(0, levels - 1, forward, tuple(carry))
        carry = forward(levels - 1, carry, True)

        def finish(k, i, heat, salt):
            r0 = base + i * SUB
            wet = land[r0 : r0 + SUB, :] == 1
            values[0, k, r0 : r0 + SUB, :] = jnp.where(wet, heat, cells[0, k, SUB + r0 : 2 * SUB + r0, :])
            values[1, k, r0 : r0 + SUB, :] = jnp.where(wet, salt, cells[1, k, SUB + r0 : 2 * SUB + r0, :])

        def backward(step, carry):
            k = levels - 2 - step
            new = []
            for i in range(blocks):
                r0 = base + i * SUB
                heat, salt = carry[2 * i : 2 * i + 2]
                gain = gains[k, i * SUB : (i + 1) * SUB, :]
                heat = values[0, k, r0 : r0 + SUB, :] + gain * heat
                salt = values[1, k, r0 : r0 + SUB, :] + gain * salt
                finish(k, i, heat, salt)
                new += [heat, salt]
            return tuple(new)

        ends = []
        for i in range(blocks):
            heat, salt = carry[4 * i + 2 : 4 * i + 4]
            finish(levels - 1, i, heat, salt)
            ends += [heat, salt]
        lax.fori_loop(0, levels - 1, backward, tuple(ends))
        store(c).start()
    for c in range(chunks):
        store(c).wait()


def step_blocks(
    tracers, east_courant, north_courant, diffusivity, land, target, messages, chunk_rows=32
):
    _, levels, rows, cols = tracers.shape
    links = target.shape[1]
    depth = jnp.arange(levels, dtype=F32)
    decay = jnp.exp(-4.0 * depth / levels)
    absorb = decay - jnp.exp(-4.0 * (depth + 1.0) / levels)
    tables = jnp.stack([0.5 * absorb, decay])
    chunks = rows // chunk_rows
    hbm = pl.BlockSpec(memory_space=pl.ANY)
    vmem = pl.BlockSpec(memory_space=pltpu.VMEM)
    own_tail, own_head = messages[0], messages[1]
    return pl.pallas_call(
        functools.partial(main_kernel, links, chunk_rows),
        in_specs=[pl.BlockSpec(memory_space=pltpu.SMEM)] + [hbm] * 4 + [vmem] * 10,
        out_specs=hbm,
        out_shape=jax.ShapeDtypeStruct(tracers.shape, F32),
        scratch_shapes=[
            pltpu.VMEM((2, levels, rows + 2 * SUB, cols), F32),
            pltpu.VMEM((levels, rows, cols), F32),
            pltpu.VMEM((levels, rows, cols), F32),
            pltpu.VMEM((levels, rows, cols), F32),
            pltpu.VMEM((2, levels, rows, cols), F32),
            pltpu.VMEM((levels, chunk_rows, cols), F32),
            pltpu.VMEM((2, levels, rows + SUB, cols), F32),
            pltpu.VMEM((5, 4 * links // LANES, LANES), F32),
            pltpu.VMEM((5, rows, cols), F32),
            pltpu.VMEM((2, rows, cols), F32),
            pltpu.VMEM((2, rows, cols), F32),
            pltpu.SemaphoreType.DMA((4, chunks)),
            pltpu.SemaphoreType.DMA((chunks,)),
        ],
        compiler_params=pltpu.CompilerParams(vmem_limit_bytes=56 << 20),
        name="step",
    )(tables, tracers, east_courant, north_courant, diffusivity, land, target, *messages)


def ring(axis, by):
    length = lax.axis_size(axis)
    return [(i, (i + by) % length) for i in range(length)]


def line(axis, by):
    length = lax.axis_size(axis)
    return [(i, i + by) for i in range(length) if 0 <= i + by < length]


def diagonal():
    lats = lax.axis_size("lat")
    lons = lax.axis_size("lon")
    return [
        (i * lons + j, (i + 1) * lons + (j + 1) % lons) for i in range(lats - 1) for j in range(lons)
    ]


def local(
    tracers,
    east_courant,
    north_courant,
    diffusivity,
    land_sea,
    fluxes,
    source_cell,
    link_weight,
    target_cell,
):
    east, west, north, south, corner, own = prep(
        tracers, east_courant, north_courant, fluxes, source_cell[0], link_weight[0]
    )
    from_corner = lax.ppermute(corner, ("lat", "lon"), diagonal())
    from_west = lax.ppermute(east, "lon", ring("lon", 1))
    from_east = lax.ppermute(west, "lon", ring("lon", -1))
    from_south = lax.ppermute(north, "lat", line("lat", 1))
    from_north = lax.ppermute(south, "lat", line("lat", -1))
    messages = (east, west, from_west, from_east, from_south, from_north, from_corner, own)
    return step_blocks(
        tracers, east_courant, north_courant, diffusivity, land_sea, target_cell[0], messages
    )


def solution(mesh):
    in_specs = (
        P(None, None, "lat", "lon"),
        P(None, "lat", "lon"),
        P(None, "lat", "lon"),
        P(None, "lat", "lon"),
        P("lat", "lon"),
        P(None, ("lat", "lon")),
        P(("lat", "lon"), None, None),
        P(("lat", "lon"), None, None),
        P(("lat", "lon"), None, None),
    )
    out_specs = P(None, None, "lat", "lon")
    return jax.shard_map(local, mesh=mesh, in_specs=in_specs, out_specs=out_specs, check_vma=False)
```

profile of v0, /device:TPU:0, one launch (start us, length us, event | category | flops | bytes accessed | tf_op | source)
XLA Modules:
  0.0 82.4 jit_solution(9663180606097175462)
XLA Ops:
  0.0 2.8 %copy-done = f32[2,48,128,128]{3,2,1,0:T(8,128)S(1)} copy-done((f32[2,48,128,128]{3,2,1,0:T(8,128)S(1)}, f32[2,48,128,128]{3,2,1,0:T(8,128)}, u32[]{:S(2)}) %copy-start) | copy-done | bytes 6291480
  2.8 1.9 %copy-done.1 = f32[48,128,128]{2,1,0:T(8,128)S(1)} copy-done((f32[48,128,128]{2,1,0:T(8,128)S(1)}, f32[48,128,128]{2,1,0:T(8,128)}, u32[]{:S(2)}) %copy-start.1) | copy-done | bytes 3145752
  4.7 1.9 %copy-done.2 = f32[48,128,128]{2,1,0:T(8,128)S(1)} copy-done((f32[48,128,128]{2,1,0:T(8,128)S(1)}, f32[48,128,128]{2,1,0:T(8,128)}, u32[]{:S(2)}) %copy-start.2) | copy-done | bytes 3145752
  6.6 0.9 %copy-done.3 = f32[6,8192]{1,0:T(8,128)S(1)} copy-done((f32[6,8192]{1,0:T(8,128)S(1)}, f32[6,8192]{1,0:T(8,128)}, u32[]{:S(2)}) %copy-start.3) | copy-done | bytes 196632
  7.5 0.9 %copy-done.6 = s32[1,4,6144]{2,1,0:T(4,128)S(1)} copy-done((s32[1,4,6144]{2,1,0:T(4,128)S(1)}, s32[1,4,6144]{2,1,0:T(4,128)}, u32[]{:S(2)}) %copy-start.6) | copy-done | bytes 98328
  8.4 0.9 %copy-done.7 = f32[1,4,6144]{2,1,0:T(4,128)S(1)} copy-done((f32[1,4,6144]{2,1,0:T(4,128)S(1)}, f32[1,4,6144]{2,1,0:T(4,128)}, u32[]{:S(2)}) %copy-start.7) | copy-done | bytes 98328
  9.3 4.3 %prep.1 = (f32[432,128]{1,0:T(8,128)S(1)}, f32[256,128]{1,0:T(8,128)S(1)}, f32[416,128]{1,0:T(8,128)S(1)}, f32[192,128]{1,0:T(8,128)S(1)}, f32[176,128]{1,0:T(8,128)S(1)}, /*index=5*/f32[176,128]{1,0:T(8,128)S(1)}) custom-call(f32[2,48,128,128]{3,2,1,0:T(8,128)S(1)} %copy-done, f32[48,128,128]{2,1,0:T(8,128)S(1)} %copy-done.1, ...), custom_call_target="tpu_custom_call" | custom-call | tf_op jit(solution)/shard_map/prep/pallas_call | solution.py:97
  13.6 0.6 copy-done.8
  14.3 4.4 %collective-permute-start.4 = (f32[176,128]{1,0:T(8,128)S(1)}, f32[176,128]{1,0:T(8,128)S(1)}, u32[]{:S(2)}, u32[]{:S(2)}) collective-permute-start(f32[176,128]{1,0:T(8,128)S(1)} %get-tuple-element.15), channel_id=1, source_target_pairs={{0,9},{1,10},{2,11},{3,12},{4,13},{5,14},{6,15},{7,8},{8,17},{9,18... | collective-permute-start | bytes 270344 | tf_op jit(solution)/shard_map/ppermute | solution.py:474
  18.6 1.3 %collective-permute-start.3 = (f32[192,128]{1,0:T(8,128)S(1)}, f32[192,128]{1,0:T(8,128)S(1)}, u32[]{:S(2)}, u32[]{:S(2)}) collective-permute-start(f32[192,128]{1,0:T(8,128)S(1)} %get-tuple-element.14), channel_id=1, source_target_pairs={{8,0},{16,8},{24,16},{9,1},{17,9},{25,17},{10,2},{18,10},{26,18},{... | collective-permute-start | bytes 294920 | tf_op jit(solution)/shard_map/ppermute | solution.py:478
  19.9 2.7 %collective-permute-start.1 = (f32[256,128]{1,0:T(8,128)S(1)}, f32[256,128]{1,0:T(8,128)S(1)}, u32[]{:S(2)}, u32[]{:S(2)}) collective-permute-start(f32[256,128]{1,0:T(8,128)S(1)} %get-tuple-element.12.own_head), channel_id=1, source_target_pairs={{0,7},{1,0},{2,1},{3,2},{4,3},{5,4},{6,5},{7,6},{8,15},{9,8},{10,9... | collective-permute-start | bytes 393224 | tf_op jit(solution)/shard_map/ppermute | solution.py:476
  22.6 4.3 %collective-permute-start.2 = (f32[416,128]{1,0:T(8,128)S(1)}, f32[416,128]{1,0:T(8,128)S(1)}, u32[]{:S(2)}, u32[]{:S(2)}) collective-permute-start(f32[416,128]{1,0:T(8,128)S(1)} %get-tuple-element.13), channel_id=1, source_target_pairs={{0,8},{8,16},{16,24},{1,9},{9,17},{17,25},{2,10},{10,18},{18,26},{... | collective-permute-start | bytes 638984 | tf_op jit(solution)/shard_map/ppermute | solution.py:477
  26.9 0.1 collective-permute-start
  27.0 0.6 pad_maximum_fusion.tables
  27.6 0.0 collective-permute-done.4.from_corner
  27.6 0.0 collective-permute-done.3.from_north
  27.6 0.0 collective-permute-done.1.from_east
  27.6 0.0 copy-start.11
  27.6 2.9 %collective-permute-done.2.from_south = f32[416,128]{1,0:T(8,128)S(1)} collective-permute-done((f32[416,128]{1,0:T(8,128)S(1)}, f32[416,128]{1,0:T(8,128)S(1)}, u32[]{:S(2)}, u32[]{:S(2)}) %collective-permute-start.2) | collective-permute-done | bytes 213024 | tf_op jit(solution)/shard_map/ppermute | solution.py:477
  30.5 2.7 %collective-permute-done.from_west = f32[432,128]{1,0:T(8,128)S(1)} collective-permute-done((f32[432,128]{1,0:T(8,128)S(1)}, f32[432,128]{1,0:T(8,128)S(1)}, u32[]{:S(2)}, u32[]{:S(2)}) %collective-permute-start) | collective-permute-done | bytes 221216 | tf_op jit(solution)/shard_map/ppermute | solution.py:475
  33.2 0.0 copy-done.5
  33.2 0.0 copy-done.12
  33.3 0.6 copy-done.9
  33.9 48.5 %step.1 = f32[2,48,128,128]{3,2,1,0:T(8,128)} custom-call(f32[2,48]{1,0:T(2,128)} %pad_maximum_fusion.tables, f32[2,48,128,128]{3,2,1,0:T(8,128)} %tracers.3, f32[48,128,128]{2,1,0:T(8,128)} %east_courant.3, f32[48,128,128]{2,1,0:T(8,128)} %north_courant.1, f32[48,128,128]{2,1,0:T(8,128)} %diffusivity.1, s32[128,128]{1,0:T(8,128)} %land.1, ...), custom_call_target="tpu_custom_call" | custom-call | tf_op jit(solution)/shard_map/step/pallas_call | solution.py:417
  (18 shorter events, 0.0 us)
Async XLA Ops:
  0.0 2.8 %copy-start = (f32[2,48,128,128]{3,2,1,0:T(8,128)S(1)}, f32[2,48,128,128]{3,2,1,0:T(8,128)}, u32[]{:S(2)}) copy-start(f32[2,48,128,128]{3,2,1,0:T(8,128)} %tracers.3) | copy-start | bytes 18874372
  2.8 1.9 %copy-start.1 = (f32[48,128,128]{2,1,0:T(8,128)S(1)}, f32[48,128,128]{2,1,0:T(8,128)}, u32[]{:S(2)}) copy-start(f32[48,128,128]{2,1,0:T(8,128)} %east_courant.3) | copy-start | bytes 9437188
  4.7 1.9 %copy-start.2 = (f32[48,128,128]{2,1,0:T(8,128)S(1)}, f32[48,128,128]{2,1,0:T(8,128)}, u32[]{:S(2)}) copy-start(f32[48,128,128]{2,1,0:T(8,128)} %north_courant.1) | copy-start | bytes 9437188
  6.6 0.9 %copy-start.3 = (f32[6,8192]{1,0:T(8,128)S(1)}, f32[6,8192]{1,0:T(8,128)}, u32[]{:S(2)}) copy-start(f32[6,8192]{1,0:T(8,128)} %fluxes.1) | copy-start | bytes 589828
  7.5 0.9 %copy-start.6 = (s32[1,4,6144]{2,1,0:T(4,128)S(1)}, s32[1,4,6144]{2,1,0:T(4,128)}, u32[]{:S(2)}) copy-start(s32[1,4,6144]{2,1,0:T(4,128)} %param.15) | copy-start | bytes 294916
  8.4 0.9 %copy-start.7 = (f32[1,4,6144]{2,1,0:T(4,128)S(1)}, f32[1,4,6144]{2,1,0:T(4,128)}, u32[]{:S(2)}) copy-start(f32[1,4,6144]{2,1,0:T(4,128)} %param.16) | copy-start | bytes 294916
  13.6 0.6 copy-start.8
  14.3 19.0 %copy-start.4 = (f32[432,128]{1,0:T(8,128)}, f32[432,128]{1,0:T(8,128)S(1)}, u32[]{:S(2)}) copy-start(f32[432,128]{1,0:T(8,128)S(1)} %get-tuple-element.11.own_tail) | copy-start | bytes 663556
  14.3 19.0 %copy-start.5 = (f32[256,128]{1,0:T(8,128)}, f32[256,128]{1,0:T(8,128)S(1)}, u32[]{:S(2)}) copy-start(f32[256,128]{1,0:T(8,128)S(1)} %get-tuple-element.12.own_head) | copy-start | bytes 393220
  14.3 13.3 %collective-permute-start.4 = (f32[176,128]{1,0:T(8,128)S(1)}, f32[176,128]{1,0:T(8,128)S(1)}, u32[]{:S(2)}, u32[]{:S(2)}) collective-permute-start(f32[176,128]{1,0:T(8,128)S(1)} %get-tuple-element.15), channel_id=1, source_target_pairs={{0,9},{1,10},{2,11},{3,12},{4,13},{5,14},{6,15},{7,8},{8,17},{9,18... | collective-permute-start | bytes 270344 | tf_op jit(solution)/shard_map/ppermute | solution.py:474
  18.6 8.9 %collective-permute-start.3 = (f32[192,128]{1,0:T(8,128)S(1)}, f32[192,128]{1,0:T(8,128)S(1)}, u32[]{:S(2)}, u32[]{:S(2)}) collective-permute-start(f32[192,128]{1,0:T(8,128)S(1)} %get-tuple-element.14), channel_id=1, source_target_pairs={{8,0},{16,8},{24,16},{9,1},{17,9},{25,17},{10,2},{18,10},{26,18},{... | collective-permute-start | bytes 294920 | tf_op jit(solution)/shard_map/ppermute | solution.py:478
  19.9 7.7 %collective-permute-start.1 = (f32[256,128]{1,0:T(8,128)S(1)}, f32[256,128]{1,0:T(8,128)S(1)}, u32[]{:S(2)}, u32[]{:S(2)}) collective-permute-start(f32[256,128]{1,0:T(8,128)S(1)} %get-tuple-element.12.own_head), channel_id=1, source_target_pairs={{0,7},{1,0},{2,1},{3,2},{4,3},{5,4},{6,5},{7,6},{8,15},{9,8},{10,9... | collective-permute-start | bytes 393224 | tf_op jit(solution)/shard_map/ppermute | solution.py:476
  22.6 7.9 %collective-permute-start.2 = (f32[416,128]{1,0:T(8,128)S(1)}, f32[416,128]{1,0:T(8,128)S(1)}, u32[]{:S(2)}, u32[]{:S(2)}) collective-permute-start(f32[416,128]{1,0:T(8,128)S(1)} %get-tuple-element.13), channel_id=1, source_target_pairs={{0,8},{8,16},{16,24},{1,9},{9,17},{17,25},{2,10},{10,18},{18,26},{... | collective-permute-start | bytes 638984 | tf_op jit(solution)/shard_map/ppermute | solution.py:477
  26.9 6.3 %collective-permute-start = (f32[432,128]{1,0:T(8,128)S(1)}, f32[432,128]{1,0:T(8,128)S(1)}, u32[]{:S(2)}, u32[]{:S(2)}) collective-permute-start(f32[432,128]{1,0:T(8,128)S(1)} %get-tuple-element.11.own_tail), channel_id=1, source_target_pairs={{0,1},{1,2},{2,3},{3,4},{4,5},{5,6},{6,7},{7,0},{8,9},{9,10},{10,1... | collective-permute-start | bytes 663560 | tf_op jit(solution)/shard_map/ppermute | solution.py:475
  27.6 5.6 %copy-start.13 = (f32[176,128]{1,0:T(8,128)}, f32[176,128]{1,0:T(8,128)S(1)}, u32[]{:S(2)}) copy-start(f32[176,128]{1,0:T(8,128)S(1)} %collective-permute-done.4.from_corner) | copy-start | bytes 270340
  27.6 5.6 %copy-start.12 = (f32[192,128]{1,0:T(8,128)}, f32[192,128]{1,0:T(8,128)S(1)}, u32[]{:S(2)}) copy-start(f32[192,128]{1,0:T(8,128)S(1)} %collective-permute-done.3.from_north) | copy-start | bytes 294916
  27.6 5.6 %copy-start.11 = (f32[256,128]{1,0:T(8,128)}, f32[256,128]{1,0:T(8,128)S(1)}, u32[]{:S(2)}) copy-start(f32[256,128]{1,0:T(8,128)S(1)} %collective-permute-done.1.from_east) | copy-start | bytes 393220
  30.5 2.7 %copy-start.10 = (f32[416,128]{1,0:T(8,128)}, f32[416,128]{1,0:T(8,128)S(1)}, u32[]{:S(2)}) copy-start(f32[416,128]{1,0:T(8,128)S(1)} %collective-permute-done.2.from_south) | copy-start | bytes 638980
  33.2 0.7 copy-start.9
where the time goes:
time: 82.8 us; the launch traced here: 82.4 us
  Pallas kernels  52.8 us (64%)
  starting transfers between devices  12.7 us (15%)
  local copies, waits for them, and re-layouts  10.6 us (13%)
  waiting for transfers between devices  5.6 us (7%)
    pallas_call x1, Pallas kernels, step_blocks(): pl.pallas_call(functools.partial(main_kernel, links, chunk_rows), in_spec...  48.5 us
    unnamed x28, local copies, waits for them, and re-layouts  10.6 us
    ppermute x1, starting transfers between devices, local(): from_corner = lax.ppermute(corner, ('lat', 'lon'), diagonal())  4.36 us
    pallas_call x1, Pallas kernels, prep(): pl.pallas_call(functools.partial(prep_kernel, links), grid=(rows // block...  4.32 us
    ppermute x1, starting transfers between devices, local(): from_south = lax.ppermute(north, 'lat', line('lat', 1))  4.27 us
    ppermute x1, waiting for transfers between devices, local(): from_south = lax.ppermute(north, 'lat', line('lat', 1))  2.92 us
    ppermute x1, starting transfers between devices, local(): from_east = lax.ppermute(west, 'lon', ring('lon', -1))  2.69 us
    ppermute x1, waiting for transfers between devices, local(): from_west = lax.ppermute(east, 'lon', ring('lon', 1))  2.67 us
  transfers between devices with their start and end apart: 5, of which 2 were waited for; matrix products, arithmetic and copies ran while one was open for 1% of the time, Pallas kernels for 0%

commit v1 on v0

v1 whole, which is shorter than its diff:
```python
import functools

import jax
import jax.numpy as jnp
from jax import lax
from jax.experimental import pallas as pl
from jax.experimental.pallas import tpu as pltpu
from jax.sharding import PartitionSpec as P

F32 = jnp.float32
BF16 = jnp.bfloat16
LANES = 128
SUB = 8
TABLE_ROWS = 16
EDGE_VMEM = 60 << 20
COLUMN_VMEM = 8 << 20
STEP_VMEM = 24 << 20


def lane_of(shape):
    return lax.broadcasted_iota(jnp.int32, shape, len(shape) - 1)


def edge_kernel(
    links,
    tracers,
    north_courant,
    fluxes,
    source,
    weight,
    east_links,
    north_msg,
    south_msg,
    corner_msg,
    own_msg,
    first_rows,
    last_rows,
    last_north,
    flux_in,
    source_in,
    weight_in,
    sem,
):
    _, levels, rows, _ = tracers.shape
    copies = [
        pltpu.make_async_copy(fluxes, flux_in, sem.at[0]),
        pltpu.make_async_copy(source, source_in, sem.at[1]),
        pltpu.make_async_copy(weight, weight_in, sem.at[2]),
        pltpu.make_async_copy(tracers.at[:, :, pl.ds(0, SUB), :], first_rows, sem.at[3]),
        pltpu.make_async_copy(tracers.at[:, :, pl.ds(rows - SUB, SUB), :], last_rows, sem.at[4]),
        pltpu.make_async_copy(north_courant.at[:, pl.ds(rows - SUB, SUB), :], last_north, sem.at[5]),
    ]
    for copy in copies:
        copy.start()
    for copy in copies[:3]:
        copy.wait()
    quarter = fluxes.shape[1] // 4
    places = ((own_msg, 0), (east_links, 0), (north_msg, 5 * levels), (corner_msg, 0))
    for n, (msg, base) in enumerate(places):
        for f in range(5):
            for u in range(TABLE_ROWS):
                cut = pl.ds(n * quarter + u * LANES, LANES)
                row = flux_in[f : f + 1, cut]
                if f == 1:
                    row = row + flux_in[5:6, cut]
                msg[pl.ds(base + f * TABLE_ROWS + u, 1), :] = row
        base = base + 5 * TABLE_ROWS
        for c in range(links // LANES):
            cut = pl.ds(c * LANES, LANES)
            msg[pl.ds(base + c, 1), :] = source_in[n : n + 1, cut].astype(F32)
            msg[pl.ds(base + links // LANES + c, 1), :] = weight_in[n : n + 1, cut]
    for copy in copies[3:]:
        copy.wait()
    for t in range(2):
        for k in range(levels):
            at = pl.ds(2 * (t * levels + k), 2)
            south_msg[at, :] = first_rows[t, k, 0:2, :]
            north_msg[at, :] = last_rows[t, k, SUB - 2 : SUB, :]
    for k in range(levels):
        north_msg[pl.ds(4 * levels + k, 1), :] = last_north[k, SUB - 1 : SUB, :]


def edges(tracers, north_courant, fluxes, source, weight):
    _, levels, _, cols = tracers.shape
    links = source.shape[1]
    remap = remap_rows(links)
    heights = (remap, 5 * levels + remap, 4 * levels, remap, remap)
    hbm = pl.BlockSpec(memory_space=pl.ANY)
    vmem = pl.BlockSpec(memory_space=pltpu.VMEM)
    return pl.pallas_call(
        functools.partial(edge_kernel, links),
        in_specs=[hbm] * 5,
        out_specs=[vmem] * 5,
        out_shape=[jax.ShapeDtypeStruct((h, LANES), F32) for h in heights],
        scratch_shapes=[
            pltpu.VMEM((2, levels, SUB, cols), F32),
            pltpu.VMEM((2, levels, SUB, cols), F32),
            pltpu.VMEM((levels, SUB, cols), F32),
            pltpu.VMEM(fluxes.shape, F32),
            pltpu.VMEM(source.shape, jnp.int32),
            pltpu.VMEM(weight.shape, F32),
            pltpu.SemaphoreType.DMA((6,)),
        ],
        compiler_params=pltpu.CompilerParams(vmem_limit_bytes=EDGE_VMEM),
        name="edges",
    )(tracers, north_courant, fluxes, source, weight)


def column_kernel(tracers, east_courant, east_links, east_msg, west_msg):
    _, levels, rows, _ = tracers.shape
    lane = lane_of((SUB, LANES))
    pair = lane // 2
    half = levels // 2

    def block(rb, carry):
        at = pl.ds(pl.multiple_of(rb * SUB, SUB), SUB)
        for t in range(2):
            tail = jnp.zeros((SUB, LANES), F32)
            head = jnp.zeros((SUB, LANES), F32)
            for k in range(levels):
                moved = pltpu.roll(tracers[t, k, at, :], 2 * k + 2, 1)
                tail = jnp.where(pair == k, moved, tail)
                head = jnp.where(pair == k + 1, moved, head)
            for j in range(half):
                moved = pltpu.roll(east_courant[t * half + j, at, :], (2 * levels + j + 1) % LANES, 1)
                tail = jnp.where(lane == 2 * levels + j, moved, tail)
            place = pl.ds(pl.multiple_of(t * rows + rb * SUB, SUB), SUB)
            east_msg[place, :] = tail
            west_msg[place, :] = head
        return carry

    lax.fori_loop(0, rows // SUB, block, 0)
    east_msg[2 * rows :, :] = east_links[...]


def columns(tracers, east_courant, east_links):
    rows = tracers.shape[2]
    vmem = pl.BlockSpec(memory_space=pltpu.VMEM)
    return pl.pallas_call(
        column_kernel,
        in_specs=[vmem] * 3,
        out_specs=[vmem] * 2,
        out_shape=[
            jax.ShapeDtypeStruct((2 * rows + east_links.shape[0], LANES), F32),
            jax.ShapeDtypeStruct((2 * rows, LANES), F32),
        ],
        compiler_params=pltpu.CompilerParams(vmem_limit_bytes=COLUMN_VMEM),
        name="columns",
    )(tracers, east_courant, east_links)


def remap_rows(links):
    return 5 * TABLE_ROWS + 2 * (links // LANES)


def gather_links(msg, base, n, links, picked):
    rows = links // LANES
    for g in range(rows // SUB):
        cells = msg[pl.ds(base + 5 * TABLE_ROWS + g * SUB, SUB), :].astype(jnp.int32)
        weights = msg[pl.ds(base + 5 * TABLE_ROWS + rows + g * SUB, SUB), :]
        low = cells % LANES
        high = (cells // LANES) % TABLE_ROWS
        for f in range(5):
            total = jnp.zeros((SUB, LANES), F32)
            for u in range(TABLE_ROWS):
                row = jnp.broadcast_to(msg[pl.ds(base + f * TABLE_ROWS + u, 1), :], (SUB, LANES))
                found = jnp.take_along_axis(row, low, axis=1, mode="promise_in_bounds")
                total = jnp.where(high == u, found, total)
            picked[f, pl.ds(n * rows + g * SUB, SUB), :] = total * weights


def scatter_links(picked, target, n, links, rows, cols):
    half_rows = rows // 2
    half_cols = cols // 2
    count = links // LANES
    wide = 4 * half_cols
    short = half_rows // 4
    tall_iota = lax.broadcasted_iota(jnp.int32, (wide, LANES), 0)
    short_iota = lax.broadcasted_iota(jnp.int32, (short, LANES), 0)
    total = jnp.zeros((10 * short, wide), F32)
    group = 8
    for g in range(count // group):
        lefts = []
        rights = []
        for c in range(g * group, (g + 1) * group):
            cell = target[n : n + 1, c * LANES : (c + 1) * LANES]
            row = cell // cols - (1 - n // 2) * half_rows
            col = cell % cols - (1 - n % 2) * half_cols
            short_at = jnp.broadcast_to(row % short, (short, LANES)) == short_iota
            wide_at = jnp.broadcast_to(row // short * half_cols + col, (wide, LANES)) == tall_iota
            rights.append(jnp.where(wide_at, 1.0, 0.0).astype(BF16))
            pieces = []
            for f in range(5):
                value = picked[f, pl.ds(n * count + c, 1), :]
                high = value.astype(BF16).astype(F32)
                low = value - high
                for part in (high, low):
                    spread = jnp.broadcast_to(part, (short, LANES))
                    pieces.append(jnp.where(short_at, spread, 0.0).astype(BF16))
            lefts.append(jnp.concatenate(pieces, 0))
        left = jnp.concatenate(lefts, 1)
        right = jnp.concatenate(rights, 1)
        total = total + lax.dot_general(
            left, right, (((1,), (1,)), ((), ())), preferred_element_type=F32
        )
    return total


def remap_kernel(links, rows, cols, numbers, bases, target, *refs):
    count = len(numbers)
    quads = refs[count]
    picked = refs[count + 1]
    for i, (n, base) in enumerate(zip(numbers, bases)):
        gather_links(refs[i], base, n, links, picked)
        quads[i] = scatter_links(picked, target, n, links, rows, cols)


def remap(target, blocks, rows, cols):
    links = target.shape[1]
    numbers = tuple(n for n, _, _ in blocks)
    bases = tuple(base for _, _, base in blocks)
    vmem = pl.BlockSpec(memory_space=pltpu.VMEM)
    return pl.pallas_call(
        functools.partial(remap_kernel, links, rows, cols, numbers, bases),
        in_specs=[vmem] * (1 + len(blocks)),
        out_specs=vmem,
        out_shape=jax.ShapeDtypeStruct((len(blocks), 10 * rows // 8, 2 * cols), F32),
        scratch_shapes=[pltpu.VMEM((5, 4 * links // LANES, LANES), F32)],
        compiler_params=pltpu.CompilerParams(vmem_limit_bytes=16 << 20),
        name="remap",
    )(target, *[msg for _, msg, _ in blocks])


def main_kernel(
    links,
    chunk_rows,
    tables,
    tracers,
    east,
    north,
    diff,
    land,
    target,
    own_tail,
    own_head,
    from_west,
    from_east,
    from_south,
    from_north,
    earlier,
    out,
    values,
    gains,
    before,
    picked,
    surface,
    left_fix,
    right_fix,
    out_sem,
):
    _, levels, rows, cols = tracers.shape
    chunks = rows // chunk_rows
    lane = lane_of((SUB, LANES))
    sub = lax.broadcasted_iota(jnp.int32, (SUB, LANES), 0)

    def store(c):
        part = pl.ds(c * chunk_rows, chunk_rows)
        return pltpu.make_async_copy(
            values.at[:, :, part, :], out.at[:, :, part, :], out_sem.at[c]
        )

    gather_links(from_west, 2 * rows, 1, links, picked)
    eastern = scatter_links(picked, target, 1, links, rows, cols)
    quads = [earlier[0], eastern, earlier[1], earlier[2]]
    short = rows // 8
    for pair in range(2):
        left = quads[2 * pair + 1]
        right = quads[2 * pair]
        for f in range(5):
            at = 2 * f * short
            one = left[at : at + short] + left[at + short : at + 2 * short]
            two = right[at : at + short] + right[at + short : at + 2 * short]
            for g in range(4):
                half = slice(g // 2 * LANES, g // 2 * LANES + LANES)
                a = one[:, half]
                b = two[:, half]
                if g % 2:
                    a = pltpu.roll(a, LANES // 2, 1)
                else:
                    b = pltpu.roll(b, LANES // 2, 1)
                merged = jnp.where(lane_of((short, LANES)) < LANES // 2, a, b)
                base = (1 - pair) * (rows // 2) + g * short
                surface[f, base : base + short, :] = merged
    for rb in range(rows // SUB):
        at = pl.ds(rb * SUB, SUB)
        s3 = surface[3, at, :]
        s4 = surface[4, at, :]
        surface[3, at, :] = 2.0 * jnp.sqrt(s3 * s3 + s4 * s4)

    even = lane % 2 == 0
    half = levels // 2
    spread = 2 * levels + (lane // 2) % half
    lower = lane // 2 < half
    for rb in range(rows // SUB):
        at = pl.ds(rb * SUB, SUB)
        next_at = pl.ds(rows + rb * SUB, SUB)
        first = jnp.take_along_axis(from_west[at, :], spread, axis=1, mode="promise_in_bounds")
        second = jnp.take_along_axis(from_west[next_at, :], spread, axis=1, mode="promise_in_bounds")
        courant = jnp.where(lower, first, second)
        for t in range(2):
            place = pl.ds(t * rows + rb * SUB, SUB)
            head = own_head[place, :]
            gap = from_east[place, :] - head
            right_fix[t, at, :] = jnp.where(even, -gap, 7.0 * pltpu.roll(gap, 1, 1) - gap)
            west = from_west[place, :]
            west_face = 7.0 * (pltpu.roll(west, LANES - 1, 1) + pltpu.roll(head, LANES - 2, 1)) - (
                west + pltpu.roll(head, LANES - 3, 1)
            )
            left_fix[t, at, :] = jnp.where(even, courant * west_face, own_tail[place, :] - west)

    def south_face(k, carry):
        for t in range(2):
            unit = t * levels + k
            below = from_south[pl.ds(2 * unit, 2), :]
            inside = tracers[t, k, 0:2, :]
            courant = from_south[pl.ds(4 * levels + k, 1), :]
            face = 7.0 * (below[1:2] + inside[0:1]) - (below[0:1] + inside[1:2])
            before[t, k, 0:1, :] = courant * face
        return carry

    lax.fori_loop(0, levels, south_face, 0)

    at_right = lane >= LANES - 2
    at_left = lane == 0
    at_last = lane == LANES - 1
    blocks = chunk_rows // SUB

    def halo_row(msg, index):
        return jnp.broadcast_to(msg[pl.ds(index, 1), :], (SUB, LANES))

    def advect(t, k, base):
        unit = t * levels + k
        south = before[t, k]
        result = []
        for i in range(blocks):
            r0 = base + i * SUB
            here = tracers[t, k, r0 : r0 + SUB, :]
            up_one = pltpu.roll(here, LANES - 1, 1)
            up_two = pltpu.roll(here, LANES - 2, 1)
            low_one = pltpu.roll(here, 1, 1)
            fix_right = pltpu.roll(right_fix[t, r0 : r0 + SUB, :], (2 * LANES - 4 - 2 * k) % LANES, 1)
            fix_left = pltpu.roll(left_fix[t, r0 : r0 + SUB, :], (LANES - 1 - 2 * k) % LANES, 1)
            face = 7.0 * (here + up_one) - (low_one + up_two)
            face = face + jnp.where(at_right, fix_right, jnp.where(at_left, fix_left, 0.0))
            east_flux = east[k, r0 : r0 + SUB, :] * face
            west_flux = pltpu.roll(jnp.where(at_last, fix_left, east_flux), 1, 1)
            if r0 == 0:
                low_one = jnp.where(sub == 0, halo_row(from_south, 2 * unit + 1), pltpu.roll(here, 1, 0))
            else:
                low_one = tracers[t, k, r0 - 1 : r0 - 1 + SUB, :]
            if r0 + SUB == rows:
                near = halo_row(from_north, 2 * unit)
                far = halo_row(from_north, 2 * unit + 1)
                up_one = jnp.where(sub == SUB - 1, near, pltpu.roll(here, SUB - 1, 0))
                up_two = jnp.where(
                    sub == SUB - 1, far, jnp.where(sub == SUB - 2, near, pltpu.roll(here, SUB - 2, 0))
                )
            else:
                up_one = tracers[t, k, r0 + 1 : r0 + 1 + SUB, :]
                up_two = tracers[t, k, r0 + 2 : r0 + 2 + SUB, :]
            face = 7.0 * (here + up_one) - (low_one + up_two)
            north_flux = north[k, r0 : r0 + SUB, :] * face
            moved = pltpu.roll(north_flux, 1, 0)
            south_flux = jnp.where(sub == 0, south, moved)
            south = moved
            change = (east_flux - west_flux) + (north_flux - south_flux)
            result.append(here - change * (1.0 / 12.0))
        before[t, k] = south
        return result

    for c in range(chunks):
        base = c * chunk_rows

        def forward(k, carry, last=False):
            new = []
            heat_all = advect(0, k, base)
            salt_all = advect(1, k, base)
            for i in range(blocks):
                r0 = base + i * SUB
                above, lead, heat, salt = carry[4 * i : 4 * i + 4]
                heat_in = heat_all[i] + surface[2, r0 : r0 + SUB, :] * tables[0, k]
                salt_in = salt_all[i]
                if last:
                    inverse = 1.0 / lead
                    below = above
                else:
                    below = diff[k, r0 : r0 + SUB, :] + surface[3, r0 : r0 + SUB, :] * tables[1, k]
                    pivot = lead + below
                    rough = pl.reciprocal(pivot, approx=True)
                    inverse = rough * (2.0 - pivot * rough)
                heat = (heat_in + above * heat) * inverse
                salt = (salt_in + above * salt) * inverse
                values[0, k, r0 : r0 + SUB, :] = heat
                values[1, k, r0 : r0 + SUB, :] = salt
                if not last:
                    gains[k, i * SUB : (i + 1) * SUB, :] = below * inverse
                    lead = 1.0 + below * (lead * inverse)
                new += [below, lead, heat, salt]
            return tuple(new)

        carry = []
        for i in range(blocks):
            r0 = base + i * SUB
            one = jnp.ones((SUB, LANES), F32)
            carry += [one, one, 0.5 * surface[0, r0 : r0 + SUB, :], 0.5 * surface[1, r0 : r0 + SUB, :]]
        carry = lax.fori_loop(0, levels - 1, forward, tuple(carry))
        carry = forward(levels - 1, carry, True)

        def finish(k, i, heat, salt):
            r0 = base + i * SUB
            wet = land[r0 : r0 + SUB, :] == 1
            values[0, k, r0 : r0 + SUB, :] = jnp.where(wet, heat, tracers[0, k, r0 : r0 + SUB, :])
            values[1, k, r0 : r0 + SUB, :] = jnp.where(wet, salt, tracers[1, k, r0 : r0 + SUB, :])

        def backward(step, carry):
            k = levels - 2 - step
            new = []
            for i in range(blocks):
                r0 = base + i * SUB
                heat, salt = carry[2 * i : 2 * i + 2]
                gain = gains[k, i * SUB : (i + 1) * SUB, :]
                heat = values[0, k, r0 : r0 + SUB, :] + gain * heat
                salt = values[1, k, r0 : r0 + SUB, :] + gain * salt
                finish(k, i, heat, salt)
                new += [heat, salt]
            return tuple(new)

        ends = []
        for i in range(blocks):
            heat, salt = carry[4 * i + 2 : 4 * i + 4]
            finish(levels - 1, i, heat, salt)
            ends += [heat, salt]
        lax.fori_loop(0, levels - 1, backward, tuple(ends))
        store(c).start()
    for c in range(chunks):
        store(c).wait()


def step_blocks(
    tracers, east_courant, north_courant, diffusivity, land, target, messages, chunk_rows=64
):
    _, levels, rows, cols = tracers.shape
    links = target.shape[1]
    depth = jnp.arange(levels, dtype=F32)
    decay = jnp.exp(-4.0 * depth / levels)
    absorb = decay - jnp.exp(-4.0 * (depth + 1.0) / levels)
    tables = jnp.stack([0.5 * absorb, decay])
    chunks = rows // chunk_rows
    hbm = pl.BlockSpec(memory_space=pl.ANY)
    vmem = pl.BlockSpec(memory_space=pltpu.VMEM)
    return pl.pallas_call(
        functools.partial(main_kernel, links, chunk_rows),
        in_specs=[pl.BlockSpec(memory_space=pltpu.SMEM)] + [vmem] * (6 + len(messages)),
        out_specs=hbm,
        out_shape=jax.ShapeDtypeStruct(tracers.shape, F32),
        scratch_shapes=[
            pltpu.VMEM((2, levels, rows, cols), F32),
            pltpu.VMEM((levels, chunk_rows, cols), F32),
            pltpu.VMEM((2, levels, SUB, cols), F32),
            pltpu.VMEM((5, 4 * links // LANES, LANES), F32),
            pltpu.VMEM((5, rows, cols), F32),
            pltpu.VMEM((2, rows, cols), F32),
            pltpu.VMEM((2, rows, cols), F32),
            pltpu.SemaphoreType.DMA((chunks,)),
        ],
        compiler_params=pltpu.CompilerParams(vmem_limit_bytes=STEP_VMEM),
        name="step",
    )(tables, tracers, east_courant, north_courant, diffusivity, land, target, *messages)


def ring(axis, by):
    length = lax.axis_size(axis)
    return [(i, (i + by) % length) for i in range(length)]


def line(axis, by):
    length = lax.axis_size(axis)
    return [(i, i + by) for i in range(length) if 0 <= i + by < length]


def diagonal():
    lats = lax.axis_size("lat")
    lons = lax.axis_size("lon")
    return [
        (i * lons + j, (i + 1) * lons + (j + 1) % lons) for i in range(lats - 1) for j in range(lons)
    ]


def local(
    tracers,
    east_courant,
    north_courant,
    diffusivity,
    land_sea,
    fluxes,
    source_cell,
    link_weight,
    target_cell,
):
    _, levels, rows, cols = tracers.shape
    target = target_cell[0]
    east_links, north, south, corner, own = edges(
        tracers, north_courant, fluxes, source_cell[0], link_weight[0]
    )
    from_corner = lax.ppermute(corner, ("lat", "lon"), diagonal())
    from_south = lax.ppermute(north, "lat", line("lat", 1))
    from_north = lax.ppermute(south, "lat", line("lat", -1))
    east, west = columns(tracers, east_courant, east_links)
    from_west = lax.ppermute(east, "lon", ring("lon", 1))
    from_east = lax.ppermute(west, "lon", ring("lon", -1))
    earlier = remap(
        target, [(0, own, 0), (2, from_south, 5 * levels), (3, from_corner, 0)], rows, cols
    )
    messages = (east, west, from_west, from_east, from_south, from_north, earlier)
    return step_blocks(
        tracers, east_courant, north_courant, diffusivity, land_sea, target, messages
    )


def solution(mesh):
    in_specs = (
        P(None, None, "lat", "lon"),
        P(None, "lat", "lon"),
        P(None, "lat", "lon"),
        P(None, "lat", "lon"),
        P("lat", "lon"),
        P(None, ("lat", "lon")),
        P(("lat", "lon"), None, None),
        P(("lat", "lon"), None, None),
        P(("lat", "lon"), None, None),
    )
    out_specs = P(None, None, "lat", "lon")
    return jax.shard_map(local, mesh=mesh, in_specs=in_specs, out_specs=out_specs, check_vma=False)
```

time: 82.8 us -> 62 us (0.75)
  Pallas kernels: 52.8 us -> 39.3 us
  waiting for transfers between devices: 5.6 us -> 1.51 us
  local copies, waits for them, and re-layouts: 10.6 us -> 8.35 us
    pallas_call x1, Pallas kernels: 48.5 us -> 29 us  [step_blocks(): pl.pallas_call(functools.partial(main_kernel, links, chunk_rows), in_spec...]
    pallas_call x1 -> x3, Pallas kernels: 4.32 us -> 10.3 us  [the longest x1 4.37 us: remap(): pl.pallas_call(functools.partial(remap_kernel, links, rows, cols, numbers...]
    ppermute x1, waiting for transfers between devices: 2.92 us -> 0.01 us  [local(): from_south = lax.ppermute(north, 'lat', line('lat', 1))]
    unnamed x28 -> x22, local copies, waits for them, and re-layouts: 10.6 us -> 8.35 us
    ppermute x1, waiting for transfers between devices: 2.67 us -> 1.5 us  [local(): from_west = lax.ppermute(east, 'lon', ring('lon', 1))]
  transfers between devices with their start and end apart: 5 -> 5, of which waited for: 2 -> 1; matrix products, arithmetic and copies ran while one was open for 1% -> 0% of each run, Pallas kernels for 0% -> 13%
where the time goes in v1:
time: 62 us; the launch traced here: 61.7 us
  Pallas kernels  39.3 us (63%)
  starting transfers between devices  12.4 us (20%)
  local copies, waits for them, and re-layouts  8.35 us (13%)
  waiting for transfers between devices  1.51 us (2%)
    pallas_call x1, Pallas kernels, step_blocks(): pl.pallas_call(functools.partial(main_kernel, links, chunk_rows), in_spec...  29 us
    unnamed x22, local copies, waits for them, and re-layouts  8.35 us
    ppermute x1, starting transfers between devices, local(): from_south = lax.ppermute(north, 'lat', line('lat', 1))  4.56 us
    ppermute x1, starting transfers between devices, local(): from_corner = lax.ppermute(corner, ('lat', 'lon'), diagonal())  4.38 us
    pallas_call x1, Pallas kernels, remap(): pl.pallas_call(functools.partial(remap_kernel, links, rows, cols, numbers...  4.37 us
    pallas_call x1, Pallas kernels, columns(): pl.pallas_call(column_kernel, in_specs=[vmem] * 3, out_specs=[vmem] * 2,...  3.53 us
    pallas_call x1, Pallas kernels, edges(): pl.pallas_call(functools.partial(edge_kernel, links), in_specs=[hbm] * 5,...  2.4 us
    ppermute x1, starting transfers between devices, local(): from_east = lax.ppermute(west, 'lon', ring('lon', -1))  2.13 us
  transfers between devices with their start and end apart: 5, of which 1 were waited for; matrix products, arithmetic and copies ran while one was open for 0% of the time, Pallas kernels for 13%

profile of v1, /device:TPU:0, one launch (start us, length us, event | category | flops | bytes accessed | tf_op | source)
XLA Modules:
  0.0 61.7 jit_solution(2756618299344822640)
XLA Ops:
  0.0 2.4 %edges.1 = (f32[176,128]{1,0:T(8,128)}, f32[416,128]{1,0:T(8,128)}, f32[192,128]{1,0:T(8,128)}, f32[176,128]{1,0:T(8,128)}, f32[176,128]{1,0:T(8,128)}) custom-call(f32[2,48,128,128]{3,2,1,0:T(8,128)} %tracers.5, f32[48,128,128]{2,1,0:T(8,128)} %north.1, f32[6,8192]{1,0:T(8,128)} %fluxes.1, s32[4,6144]{1,0:T(4,128)} %bitcast.7, f32[4,6144]{1,0:T(4,128)} %bitcast.8), custom_call_target="tpu_custom_call" | custom-call | tf_op jit(solution)/shard_map/edges/pallas_call | solution.py:90
  2.4 4.4 %collective-permute-start.4 = (f32[176,128]{1,0:T(8,128)}, f32[176,128]{1,0:T(8,128)S(1)}, u32[]{:S(2)}, u32[]{:S(2)}) collective-permute-start(f32[176,128]{1,0:T(8,128)} %get-tuple-element.18), channel_id=1, source_target_pairs={{0,9},{1,10},{2,11},{3,12},{4,13},{5,14},{6,15},{7,8},{8,17},{9,18... | collective-permute-start | bytes 270344 | tf_op jit(solution)/shard_map/ppermute | solution.py:515
  6.8 1.3 %collective-permute-start.3 = (f32[192,128]{1,0:T(8,128)}, f32[192,128]{1,0:T(8,128)S(1)}, u32[]{:S(2)}, u32[]{:S(2)}) collective-permute-start(f32[192,128]{1,0:T(8,128)} %get-tuple-element.16), channel_id=1, source_target_pairs={{8,0},{16,8},{24,16},{9,1},{17,9},{25,17},{10,2},{18,10},{26,18},{... | collective-permute-start | bytes 294920 | tf_op jit(solution)/shard_map/ppermute | solution.py:517
  8.1 4.6 %collective-permute-start.2 = (f32[416,128]{1,0:T(8,128)}, f32[416,128]{1,0:T(8,128)S(1)}, u32[]{:S(2)}, u32[]{:S(2)}) collective-permute-start(f32[416,128]{1,0:T(8,128)} %get-tuple-element.15), channel_id=1, source_target_pairs={{0,8},{8,16},{16,24},{1,9},{9,17},{17,25},{2,10},{10,18},{18,26},{... | collective-permute-start | bytes 638984 | tf_op jit(solution)/shard_map/ppermute | solution.py:516
  12.7 0.0 copy-start
  12.7 2.8 %copy-done = f32[2,48,128,128]{3,2,1,0:T(8,128)S(1)} copy-done((f32[2,48,128,128]{3,2,1,0:T(8,128)S(1)}, f32[2,48,128,128]{3,2,1,0:T(8,128)}, u32[]{:S(2)}) %copy-start) | copy-done | bytes 6291480
  15.5 1.9 %copy-done.1 = f32[48,128,128]{2,1,0:T(8,128)S(1)} copy-done((f32[48,128,128]{2,1,0:T(8,128)S(1)}, f32[48,128,128]{2,1,0:T(8,128)}, u32[]{:S(2)}) %copy-start.1) | copy-done | bytes 3145752
  17.3 0.9 %copy-done.7 = f32[176,128]{1,0:T(8,128)S(1)} copy-done((f32[176,128]{1,0:T(8,128)S(1)}, f32[176,128]{1,0:T(8,128)}, u32[]{:S(2)}) %copy-start.7) | copy-done | bytes 90136
  18.2 3.5 %columns.1 = (f32[432,128]{1,0:T(8,128)S(1)}, f32[256,128]{1,0:T(8,128)S(1)}) custom-call(f32[2,48,128,128]{3,2,1,0:T(8,128)S(1)} %copy-done, f32[48,128,128]{2,1,0:T(8,128)S(1)} %copy-done.1, f32[176,128]{1,0:T(8,128)S(1)} %copy-done.7), custom_call_target="tpu_custom_call" | custom-call | tf_op jit(solution)/shard_map/columns/pallas_call | solution.py:139
  21.8 2.1 %collective-permute-start.1 = (f32[256,128]{1,0:T(8,128)S(1)}, f32[256,128]{1,0:T(8,128)S(1)}, u32[]{:S(2)}, u32[]{:S(2)}) collective-permute-start(f32[256,128]{1,0:T(8,128)S(1)} %get-tuple-element.14.own_head), channel_id=1, source_target_pairs={{0,7},{1,0},{2,1},{3,2},{4,3},{5,4},{6,5},{7,6},{8,15},{9,8},{10,9... | collective-permute-start | bytes 393224 | tf_op jit(solution)/shard_map/ppermute | solution.py:520
  23.9 0.0 collective-permute-start
  23.9 0.0 collective-permute-done.4.refs_2_
  23.9 0.0 collective-permute-done.2.refs_1_.from_south
  24.0 0.0 copy-done.5
  24.0 0.0 copy-start.6
  24.0 0.9 %copy-done.6 = f32[176,128]{1,0:T(8,128)S(1)} copy-done((f32[176,128]{1,0:T(8,128)S(1)}, f32[176,128]{1,0:T(8,128)}, u32[]{:S(2)}) %copy-start.6) | copy-done | bytes 90136
  24.9 4.4 %remap.1.earlier = f32[3,160,256]{2,1,0:T(8,128)S(1)} custom-call(s32[4,6144]{1,0:T(4,128)S(1)} %bitcast.5, f32[176,128]{1,0:T(8,128)S(1)} %copy-done.6, f32[416,128]{1,0:T(8,128)S(1)} %collective-permute-done.2.refs_1_.from_south, f32[176,128]{1,0:T(8,128)S(1)} %collective-permute-done.4.refs_2_), custom_call_target="tpu_custom_call" | custom-call | tf_op jit(solution)/shard_map/remap/pallas_call | solution.py:223
  29.2 0.0 collective-permute-done.3.from_north
  29.2 0.0 collective-permute-done.1.from_east
  29.3 1.5 %collective-permute-done.from_west = f32[432,128]{1,0:T(8,128)S(1)} collective-permute-done((f32[432,128]{1,0:T(8,128)S(1)}, f32[432,128]{1,0:T(8,128)S(1)}, u32[]{:S(2)}, u32[]{:S(2)}) %collective-permute-start) | collective-permute-done | bytes 221216 | tf_op jit(solution)/shard_map/ppermute | solution.py:519
  30.8 0.0 copy-done.8
  30.8 0.0 copy-start.4
  30.8 1.9 %copy-done.4 = f32[48,128,128]{2,1,0:T(8,128)S(1)} copy-done((f32[48,128,128]{2,1,0:T(8,128)S(1)}, f32[48,128,128]{2,1,0:T(8,128)}, u32[]{:S(2)}) %copy-start.4) | copy-done | bytes 3145752
  32.7 29.0 %step.1 = f32[2,48,128,128]{3,2,1,0:T(8,128)} custom-call(f32[2,48]{1,0:T(2,128)S(1)} %pad_maximum_fusion.tables, f32[2,48,128,128]{3,2,1,0:T(8,128)S(1)} %bitcast.4, f32[48,128,128]{2,1,0:T(8,128)S(1)} %copy-done.2, f32[48,128,128]{2,1,0:T(8,128)S(1)} %copy-done.3, f32[48,128,128]{2,1,0:T(8,128)S(1)} %copy-done.4, s32[128,128]{1,0:T(8,128)S(1)} %copy-done.8, ...), custom_call_target="tpu_custom_call" | custom-call | tf_op jit(solution)/shard_map/step/pallas_call | solution.py:461
  (15 shorter events, 0.0 us)
Async XLA Ops:
  0.0 24.0 %copy-start.5 = (s32[1,4,6144]{2,1,0:T(4,128)S(1)}, s32[1,4,6144]{2,1,0:T(4,128)}, u32[]{:S(2)}) copy-start(s32[1,4,6144]{2,1,0:T(4,128)} %param.17) | copy-start | bytes 294916
  0.0 30.8 %slice-start = ((s8[6291456]{0:T(1024)(128)(4,1)}), s8[2097152]{0:T(1024)(128)(4,1)S(1)}, s32[]{:S(2)}) async-start(s8[6291456]{0:T(1024)(128)(4,1)} %bitcast.3), calls=%async_computation | async-start | bytes 4194304
  0.0 30.8 %copy-start.8 = (s32[128,128]{1,0:T(8,128)S(1)}, s32[128,128]{1,0:T(8,128)}, u32[]{:S(2)}) copy-start(s32[128,128]{1,0:T(8,128)} %land.1) | copy-start | bytes 196612
  2.4 21.5 %collective-permute-start.4 = (f32[176,128]{1,0:T(8,128)}, f32[176,128]{1,0:T(8,128)S(1)}, u32[]{:S(2)}, u32[]{:S(2)}) collective-permute-start(f32[176,128]{1,0:T(8,128)} %get-tuple-element.18), channel_id=1, source_target_pairs={{0,9},{1,10},{2,11},{3,12},{4,13},{5,14},{6,15},{7,8},{8,17},{9,18... | collective-permute-start | bytes 270344 | tf_op jit(solution)/shard_map/ppermute | solution.py:515
  6.8 22.4 %collective-permute-start.3 = (f32[192,128]{1,0:T(8,128)}, f32[192,128]{1,0:T(8,128)S(1)}, u32[]{:S(2)}, u32[]{:S(2)}) collective-permute-start(f32[192,128]{1,0:T(8,128)} %get-tuple-element.16), channel_id=1, source_target_pairs={{8,0},{16,8},{24,16},{9,1},{17,9},{25,17},{10,2},{18,10},{26,18},{... | collective-permute-start | bytes 294920 | tf_op jit(solution)/shard_map/ppermute | solution.py:517
  8.1 15.9 %collective-permute-start.2 = (f32[416,128]{1,0:T(8,128)}, f32[416,128]{1,0:T(8,128)S(1)}, u32[]{:S(2)}, u32[]{:S(2)}) collective-permute-start(f32[416,128]{1,0:T(8,128)} %get-tuple-element.15), channel_id=1, source_target_pairs={{0,8},{8,16},{16,24},{1,9},{9,17},{17,25},{2,10},{10,18},{18,26},{... | collective-permute-start | bytes 638984 | tf_op jit(solution)/shard_map/ppermute | solution.py:516
  12.7 2.8 %copy-start = (f32[2,48,128,128]{3,2,1,0:T(8,128)S(1)}, f32[2,48,128,128]{3,2,1,0:T(8,128)}, u32[]{:S(2)}) copy-start(f32[2,48,128,128]{3,2,1,0:T(8,128)} %tracers.5) | copy-start | bytes 18874372
  15.4 1.9 %copy-start.1 = (f32[48,128,128]{2,1,0:T(8,128)S(1)}, f32[48,128,128]{2,1,0:T(8,128)}, u32[]{:S(2)}) copy-start(f32[48,128,128]{2,1,0:T(8,128)} %east.1) | copy-start | bytes 9437188
  17.3 0.9 %copy-start.7 = (f32[176,128]{1,0:T(8,128)S(1)}, f32[176,128]{1,0:T(8,128)}, u32[]{:S(2)}) copy-start(f32[176,128]{1,0:T(8,128)} %get-tuple-element.12.east_links) | copy-start | bytes 270340
  18.2 12.5 %slice-start.1 = ((s8[6291456]{0:T(1024)(128)(4,1)}), s8[4194304]{0:T(1024)(128)(4,1)S(1)}, s32[]{:S(2)}) async-start(s8[6291456]{0:T(1024)(128)(4,1)} %bitcast.3), calls=%async_computation.1 | async-start | bytes 8388608
  18.2 12.5 %copy-start.2 = (f32[48,128,128]{2,1,0:T(8,128)S(1)}, f32[48,128,128]{2,1,0:T(8,128)}, u32[]{:S(2)}) copy-start(f32[48,128,128]{2,1,0:T(8,128)} %east.1) | copy-start | bytes 9437188
  18.2 12.6 %copy-start.3 = (f32[48,128,128]{2,1,0:T(8,128)S(1)}, f32[48,128,128]{2,1,0:T(8,128)}, u32[]{:S(2)}) copy-start(f32[48,128,128]{2,1,0:T(8,128)} %north.1) | copy-start | bytes 9437188
  21.8 7.5 %collective-permute-start.1 = (f32[256,128]{1,0:T(8,128)S(1)}, f32[256,128]{1,0:T(8,128)S(1)}, u32[]{:S(2)}, u32[]{:S(2)}) collective-permute-start(f32[256,128]{1,0:T(8,128)S(1)} %get-tuple-element.14.own_head), channel_id=1, source_target_pairs={{0,7},{1,0},{2,1},{3,2},{4,3},{5,4},{6,5},{7,6},{8,15},{9,8},{10,9... | collective-permute-start | bytes 393224 | tf_op jit(solution)/shard_map/ppermute | solution.py:520
  23.9 6.9 %collective-permute-start = (f32[432,128]{1,0:T(8,128)S(1)}, f32[432,128]{1,0:T(8,128)S(1)}, u32[]{:S(2)}, u32[]{:S(2)}) collective-permute-start(f32[432,128]{1,0:T(8,128)S(1)} %get-tuple-element.13.own_tail), channel_id=1, source_target_pairs={{0,1},{1,2},{2,3},{3,4},{4,5},{5,6},{6,7},{7,0},{8,9},{9,10},{10,1... | collective-permute-start | bytes 663560 | tf_op jit(solution)/shard_map/ppermute | solution.py:519
  24.0 0.9 %copy-start.6 = (f32[176,128]{1,0:T(8,128)S(1)}, f32[176,128]{1,0:T(8,128)}, u32[]{:S(2)}) copy-start(f32[176,128]{1,0:T(8,128)} %get-tuple-element.17.refs_0_) | copy-start | bytes 270340
  30.8 1.9 %copy-start.4 = (f32[48,128,128]{2,1,0:T(8,128)S(1)}, f32[48,128,128]{2,1,0:T(8,128)}, u32[]{:S(2)}) copy-start(f32[48,128,128]{2,1,0:T(8,128)} %diff.1) | copy-start | bytes 9437188

commit v2 on v1

v2 whole, which is shorter than its diff:
```python
import functools

import jax
import jax.numpy as jnp
import numpy as np
from jax import lax
from jax.experimental import pallas as pl
from jax.experimental.pallas import tpu as pltpu
from jax.sharding import PartitionSpec as P

F32 = jnp.float32
BF16 = jnp.bfloat16
LANES = 128
SUB = 8
TABLE_ROWS = 16
PARTS = 4
PACK = 16
LEVELS = 6
FORWARD = 4
BACKWARD = 4


def lane_of(shape):
    return lax.broadcasted_iota(jnp.int32, shape, len(shape) - 1)


def remap_rows(links):
    return 5 * TABLE_ROWS + 2 * (links // LANES)


def load_kernel(
    links,
    tracers,
    east_courant,
    north_courant,
    fluxes,
    source,
    weight,
    cells,
    east,
    own,
    east_msg,
    west_msg,
    north_msg,
    south_msg,
    corner_msg,
    own_msg,
    flux_in,
    source_in,
    weight_in,
    last_north,
    sem,
):
    _, levels, rows, _ = tracers.shape
    part = levels // PARTS
    half = levels // 2
    small = [
        pltpu.make_async_copy(fluxes, flux_in, sem.at[0]),
        pltpu.make_async_copy(source, source_in, sem.at[1]),
        pltpu.make_async_copy(weight, weight_in, sem.at[2]),
        pltpu.make_async_copy(north_courant.at[:, pl.ds(rows - SUB, SUB), :], last_north, sem.at[3]),
    ]
    large = []
    for q in range(PARTS):
        at = pl.ds(q * part, part)
        large.append(
            [
                pltpu.make_async_copy(tracers.at[0, at], cells.at[0, at], sem.at[4 + 3 * q]),
                pltpu.make_async_copy(tracers.at[1, at], cells.at[1, at], sem.at[5 + 3 * q]),
                pltpu.make_async_copy(east_courant.at[at], east.at[at], sem.at[6 + 3 * q]),
            ]
        )
    for copy in small:
        copy.start()
    for group in large:
        for copy in group:
            copy.start()
    for copy in small:
        copy.wait()
    quarter = fluxes.shape[1] // 4
    places = ((own_msg, 0), (east_msg, 2 * rows), (north_msg, 5 * levels), (corner_msg, 0))
    for n, (msg, base) in enumerate(places):
        for f in range(5):
            for u in range(TABLE_ROWS):
                cut = pl.ds(n * quarter + u * LANES, LANES)
                row = flux_in[f : f + 1, cut]
                if f == 1:
                    row = row + flux_in[5:6, cut]
                msg[pl.ds(base + f * TABLE_ROWS + u, 1), :] = row
        base = base + 5 * TABLE_ROWS
        for c in range(links // LANES):
            cut = pl.ds(c * LANES, LANES)
            msg[pl.ds(base + c, 1), :] = source_in[n : n + 1, cut].astype(F32)
            msg[pl.ds(base + links // LANES + c, 1), :] = weight_in[n : n + 1, cut]
    for k in range(levels):
        north_msg[pl.ds(4 * levels + k, 1), :] = last_north[k, SUB - 1 : SUB, :]

    lane = lane_of((SUB, LANES))
    group = lane // 4
    for q in range(PARTS):
        for copy in large[q]:
            copy.wait()
        side = q * part // half
        offset = q * part % half

        def pack(rb, carry):
            at = pl.ds(pl.multiple_of(rb * SUB, SUB), SUB)
            for slot, ref in ((side, cells.at[0]), (2 + side, cells.at[1]), (4 + side, east)):
                packed = own[slot, at, :] if offset else jnp.zeros((SUB, LANES), F32)
                for j in range(part):
                    moved = pltpu.roll(ref[q * part + j, at, :], 4 * (offset + j) + 2, 1)
                    packed = jnp.where(group == offset + j, moved, packed)
                own[slot, at, :] = packed
            return carry

        lax.fori_loop(0, rows // SUB, pack, 0, unroll=PACK)
        for t in range(2):
            for k in range(q * part, (q + 1) * part):
                at = pl.ds(2 * (t * levels + k), 2)
                south_msg[at, :] = cells[t, k, 0:2, :]
                north_msg[at, :] = cells[t, k, rows - 2 : rows, :]

    early = lane % 4 < 2
    spare = lane >= 2 * levels
    last_column = (4 * lane + 1) % LANES

    def messages(rb, carry):
        at = pl.ds(pl.multiple_of(rb * SUB, SUB), SUB)
        for t in range(2):
            first = own[2 * t, at, :]
            second = own[2 * t + 1, at, :]
            courant = jnp.take_along_axis(own[4 + t, at, :], last_column, axis=1, mode="promise_in_bounds")
            tails = jnp.where(early, first, pltpu.roll(second, 2, 1))
            place = pl.ds(pl.multiple_of(t * rows + rb * SUB, SUB), SUB)
            east_msg[place, :] = jnp.where(spare, courant, tails)
            west_msg[place, :] = jnp.where(early, pltpu.roll(first, LANES - 2, 1), second)
        return carry

    lax.fori_loop(0, rows // SUB, messages, 0, unroll=4)


def in_hbm(*arrays):
    return [pltpu.with_memory_space_constraint(a, pltpu.HBM) for a in arrays]


def load(tracers, east_courant, north_courant, fluxes, source, weight):
    _, levels, rows, cols = tracers.shape
    links = source.shape[1]
    remap = remap_rows(links)
    hbm = pl.BlockSpec(memory_space=pltpu.HBM)
    vmem = pl.BlockSpec(memory_space=pltpu.VMEM)
    shapes = [
        tracers.shape,
        east_courant.shape,
        (6, rows, cols),
        (2 * rows + remap, LANES),
        (2 * rows, LANES),
        (5 * levels + remap, LANES),
        (4 * levels, LANES),
        (remap, LANES),
        (remap, LANES),
    ]
    return pl.pallas_call(
        functools.partial(load_kernel, links),
        in_specs=[hbm] * 6,
        out_specs=[vmem] * len(shapes),
        out_shape=[pltpu.VMEM(shape, F32) for shape in shapes],
        scratch_shapes=[
            pltpu.VMEM(fluxes.shape, F32),
            pltpu.VMEM(source.shape, jnp.int32),
            pltpu.VMEM(weight.shape, F32),
            pltpu.VMEM((levels, SUB, cols), F32),
            pltpu.SemaphoreType.DMA((4 + 3 * PARTS,)),
        ],
        compiler_params=pltpu.CompilerParams(vmem_limit_bytes=16 << 20),
        name="load",
    )(*in_hbm(tracers, east_courant, north_courant, fluxes, source, weight))


def stencil_weights(cols):
    i = lax.broadcasted_iota(jnp.int32, (2 * cols, 2 * cols), 0) % cols
    j = lax.broadcasted_iota(jnp.int32, (2 * cols, 2 * cols), 1)
    face = j % cols - j // cols
    gap = i - face
    near = (gap == 0) | (gap == 1)
    far = (gap == -1) | (gap == 2)
    return jnp.where(near, 7.0, jnp.where(far, -1.0, 0.0)).astype(BF16)


def interior_kernel(
    cells,
    east,
    north_courant,
    diffusivity,
    from_south,
    from_north,
    advected,
    diff,
    weights,
    north,
    sem,
):
    _, levels, rows, cols = cells.shape
    weights[...] = stencil_weights(cols)
    part = levels // PARTS
    sub = lax.broadcasted_iota(jnp.int32, (SUB, LANES), 0)
    blocks = rows // SUB
    copies = []
    for q in range(PARTS):
        at = pl.ds(q * part, part)
        copies.append(pltpu.make_async_copy(north_courant.at[at], north.at[at], sem.at[q]))
    last = pltpu.make_async_copy(diffusivity, diff, sem.at[PARTS])
    for copy in copies:
        copy.start()
    last.start()

    def halo_row(msg, index):
        return jnp.broadcast_to(msg[pl.ds(index, 1), :], (SUB, LANES))

    def level(k, carry):
        west_courant = [pltpu.roll(east[k, i * SUB : (i + 1) * SUB, :], 1, 1) for i in range(blocks)]
        for t in range(2):
            unit = t * levels + k
            whole = cells[t, k]
            high = whole.astype(BF16)
            low = (whole - high.astype(F32)).astype(BF16)
            faces = jnp.dot(
                jnp.concatenate([high, low], 1), weights[...], preferred_element_type=F32
            )
            below = from_south[pl.ds(2 * unit, 2), :]
            inside = cells[t, k, 0:2, :]
            courant = from_south[pl.ds(4 * levels + k, 1), :]
            south = courant * (7.0 * (below[1:2] + inside[0:1]) - (below[0:1] + inside[1:2]))
            south = jnp.broadcast_to(south, (SUB, LANES))
            for i in range(blocks):
                r0 = i * SUB
                here = cells[t, k, r0 : r0 + SUB, :]
                east_flux = east[k, r0 : r0 + SUB, :] * faces[r0 : r0 + SUB, :cols]
                west_flux = west_courant[i] * faces[r0 : r0 + SUB, cols:]
                if i == 0:
                    low_one = jnp.where(
                        sub == 0, halo_row(from_south, 2 * unit + 1), pltpu.roll(here, 1, 0)
                    )
                else:
                    low_one = cells[t, k, r0 - 1 : r0 - 1 + SUB, :]
                if i == blocks - 1:
                    near = halo_row(from_north, 2 * unit)
                    far = halo_row(from_north, 2 * unit + 1)
                    up_one = jnp.where(sub == SUB - 1, near, pltpu.roll(here, SUB - 1, 0))
                    up_two = pltpu.roll(here, SUB - 2, 0)
                    up_two = jnp.where(
                        sub == SUB - 1, far, jnp.where(sub == SUB - 2, near, up_two)
                    )
                else:
                    up_one = cells[t, k, r0 + 1 : r0 + 1 + SUB, :]
                    up_two = cells[t, k, r0 + 2 : r0 + 2 + SUB, :]
                face = 7.0 * (here + up_one) - (low_one + up_two)
                north_flux = north[k, r0 : r0 + SUB, :] * face
                moved = pltpu.roll(north_flux, 1, 0)
                south_flux = jnp.where(sub == 0, south, moved)
                south = moved
                change = (east_flux - west_flux) + (north_flux - south_flux)
                advected[t, k, r0 : r0 + SUB, :] = here - change * (1.0 / 12.0)
        return carry

    for q in range(PARTS):
        copies[q].wait()
        lax.fori_loop(q * part, (q + 1) * part, level, 0, unroll=LEVELS)
    last.wait()


def interior(cells, east, north_courant, diffusivity, from_south, from_north):
    _, levels, rows, cols = cells.shape
    hbm = pl.BlockSpec(memory_space=pltpu.HBM)
    vmem = pl.BlockSpec(memory_space=pltpu.VMEM)
    return pl.pallas_call(
        interior_kernel,
        in_specs=[vmem] * 2 + [hbm] * 2 + [vmem] * 2,
        out_specs=[vmem] * 2,
        out_shape=[pltpu.VMEM(cells.shape, F32), pltpu.VMEM(diffusivity.shape, F32)],
        scratch_shapes=[
            pltpu.VMEM((2 * cols, 2 * cols), BF16),
            pltpu.VMEM(north_courant.shape, F32),
            pltpu.SemaphoreType.DMA((PARTS + 1,)),
        ],
        compiler_params=pltpu.CompilerParams(vmem_limit_bytes=16 << 20),
        name="interior",
    )(cells, east, *in_hbm(north_courant, diffusivity), from_south, from_north)


def gather_links(msg, base, n, links, picked):
    rows = links // LANES
    for g in range(rows // SUB):
        cells = msg[pl.ds(base + 5 * TABLE_ROWS + g * SUB, SUB), :].astype(jnp.int32)
        weights = msg[pl.ds(base + 5 * TABLE_ROWS + rows + g * SUB, SUB), :]
        low = cells % LANES
        high = (cells // LANES) % TABLE_ROWS
        for f in range(5):
            total = jnp.zeros((SUB, LANES), F32)
            for u in range(TABLE_ROWS):
                row = jnp.broadcast_to(msg[pl.ds(base + f * TABLE_ROWS + u, 1), :], (SUB, LANES))
                found = jnp.take_along_axis(row, low, axis=1, mode="promise_in_bounds")
                total = jnp.where(high == u, found, total)
            picked[f, pl.ds(n * rows + g * SUB, SUB), :] = total * weights


def scatter_links(picked, target, n, links, rows, cols):
    half_rows = rows // 2
    half_cols = cols // 2
    count = links // LANES
    wide = 4 * half_cols
    short = half_rows // 4
    tall_iota = lax.broadcasted_iota(jnp.int32, (wide, LANES), 0)
    short_iota = lax.broadcasted_iota(jnp.int32, (short, LANES), 0)
    total = jnp.zeros((10 * short, wide), F32)
    group = 8
    for g in range(count // group):
        lefts = []
        rights = []
        for c in range(g * group, (g + 1) * group):
            cell = target[n : n + 1, c * LANES : (c + 1) * LANES]
            row = cell // cols - (1 - n // 2) * half_rows
            col = cell % cols - (1 - n % 2) * half_cols
            short_at = jnp.broadcast_to(row % short, (short, LANES)) == short_iota
            wide_at = jnp.broadcast_to(row // short * half_cols + col, (wide, LANES)) == tall_iota
            rights.append(jnp.where(wide_at, 1.0, 0.0).astype(BF16))
            pieces = []
            for f in range(5):
                value = picked[f, pl.ds(n * count + c, 1), :]
                high = value.astype(BF16).astype(F32)
                low = value - high
                for part in (high, low):
                    spread = jnp.broadcast_to(part, (short, LANES))
                    pieces.append(jnp.where(short_at, spread, 0.0).astype(BF16))
            lefts.append(jnp.concatenate(pieces, 0))
        left = jnp.concatenate(lefts, 1)
        right = jnp.concatenate(rights, 1)
        total = total + lax.dot_general(
            left, right, (((1,), (1,)), ((), ())), preferred_element_type=F32
        )
    return total


def remap_kernel(links, rows, cols, numbers, bases, target, *refs):
    count = len(numbers)
    quads = refs[count]
    picked = refs[count + 1]
    for i, (n, base) in enumerate(zip(numbers, bases)):
        gather_links(refs[i], base, n, links, picked)
        quads[i] = scatter_links(picked, target, n, links, rows, cols)


def remap(target, blocks, rows, cols):
    links = target.shape[1]
    numbers = tuple(n for n, _, _ in blocks)
    bases = tuple(base for _, _, base in blocks)
    vmem = pl.BlockSpec(memory_space=pltpu.VMEM)
    return pl.pallas_call(
        functools.partial(remap_kernel, links, rows, cols, numbers, bases),
        in_specs=[vmem] * (1 + len(blocks)),
        out_specs=vmem,
        out_shape=jax.ShapeDtypeStruct((len(blocks), 10 * rows // 8, 2 * cols), F32),
        scratch_shapes=[pltpu.VMEM((5, 4 * links // LANES, LANES), F32)],
        compiler_params=pltpu.CompilerParams(vmem_limit_bytes=16 << 20),
        name="remap",
    )(target, *[msg for _, msg, _ in blocks])


def main_kernel(
    links,
    chunk_rows,
    tables,
    cells,
    advected,
    diff,
    land,
    target,
    own,
    from_west,
    from_east,
    earlier,
    out,
    values,
    gains,
    picked,
    surface,
    fix,
    out_sem,
):
    _, levels, rows, cols = cells.shape
    chunks = rows // chunk_rows
    lane = lane_of((SUB, LANES))

    def store(c):
        part = pl.ds(c * chunk_rows, chunk_rows)
        return pltpu.make_async_copy(
            values.at[:, :, part, :], out.at[:, :, part, :], out_sem.at[c]
        )

    gather_links(from_west, 2 * rows, 1, links, picked)
    eastern = scatter_links(picked, target, 1, links, rows, cols)
    quads = [earlier[0], eastern, earlier[1], earlier[2]]
    short = rows // 8
    for pair in range(2):
        left = quads[2 * pair + 1]
        right = quads[2 * pair]
        for f in range(5):
            at = 2 * f * short
            one = left[at : at + short] + left[at + short : at + 2 * short]
            two = right[at : at + short] + right[at + short : at + 2 * short]
            for g in range(4):
                half = slice(g // 2 * LANES, g // 2 * LANES + LANES)
                a = one[:, half]
                b = two[:, half]
                if g % 2:
                    a = pltpu.roll(a, LANES // 2, 1)
                else:
                    b = pltpu.roll(b, LANES // 2, 1)
                merged = jnp.where(lane_of((short, LANES)) < LANES // 2, a, b)
                base = (1 - pair) * (rows // 2) + g * short
                surface[f, base : base + short, :] = merged
    for rb in range(rows // SUB):
        at = pl.ds(rb * SUB, SUB)
        s3 = surface[3, at, :]
        s4 = surface[4, at, :]
        surface[3, at, :] = 2.0 * jnp.sqrt(s3 * s3 + s4 * s4)

    half = levels // 2
    place_in_group = lane % 4
    spread = (2 * levels + lane // 4) % LANES
    for side in range(2):

        def mend(rb, carry):
            at = pl.ds(pl.multiple_of(rb * SUB, SUB), SUB)
            msg_at = pl.ds(pl.multiple_of(side * rows + rb * SUB, SUB), SUB)
            courant = own[4 + side, at, :]
            courant_before = pltpu.roll(courant, 1, 1)
            west_courant = jnp.take_along_axis(
                from_west[msg_at, :], spread, axis=1, mode="promise_in_bounds"
            )
            for t in range(2):
                msg_at = pl.ds(pl.multiple_of(t * rows + rb * SUB, SUB), SUB)
                west = from_west[msg_at, :]
                right = from_east[msg_at, :]
                if side:
                    west = pltpu.roll(west, LANES - 2, 1)
                    right = pltpu.roll(right, LANES - 2, 1)
                inner = own[2 * t + side, at, :]
                inner_next = pltpu.roll(inner, LANES - 1, 1)
                west_one = pltpu.roll(west, 1, 1)
                west_two = pltpu.roll(west, 2, 1)
                product = courant * right
                second = courant * (7.0 * pltpu.roll(right, 1, 1)) - product + pltpu.roll(product, 1, 1)
                third = (
                    courant_before * (7.0 * inner - inner_next)
                    - courant * west_one
                    - west_courant * (7.0 * (west_one + inner) - (west_two + inner_next))
                )
                fourth = courant_before * west_two
                change = jnp.where(
                    place_in_group < 2,
                    jnp.where(place_in_group == 0, -product, second),
                    jnp.where(place_in_group == 2, third, fourth),
                )
                fix[t, side, at, :] = change * (-1.0 / 12.0)
            return carry

        lax.fori_loop(0, rows // SUB, mend, 0, unroll=4)

    at_edge = (lane >= LANES - 2) | (lane < 2)
    blocks = chunk_rows // SUB

    def advect(t, k, base):
        side = k // half
        shift = (2 * LANES - 2 - 4 * (k % half)) % LANES
        result = []
        for i in range(blocks):
            at = pl.ds(base + i * SUB, SUB)
            edge = pltpu.roll(fix[t, side, at, :], shift, 1)
            result.append(advected[t, k, at, :] + jnp.where(at_edge, edge, 0.0))
        return result

    for c in range(chunks):
        base = c * chunk_rows

        def forward(k, carry, last=False):
            new = []
            heat_all = advect(0, k, base)
            salt_all = advect(1, k, base)
            for i in range(blocks):
                r0 = base + i * SUB
                above, lead, heat, salt = carry[4 * i : 4 * i + 4]
                heat_in = heat_all[i] + surface[2, r0 : r0 + SUB, :] * tables[0, k]
                salt_in = salt_all[i]
                if last:
                    inverse = 1.0 / lead
                    below = above
                else:
                    below = diff[k, r0 : r0 + SUB, :] + surface[3, r0 : r0 + SUB, :] * tables[1, k]
                    pivot = lead + below
                    rough = pl.reciprocal(pivot, approx=True)
                    inverse = rough * (2.0 - pivot * rough)
                heat = (heat_in + above * heat) * inverse
                salt = (salt_in + above * salt) * inverse
                values[0, k, r0 : r0 + SUB, :] = heat
                values[1, k, r0 : r0 + SUB, :] = salt
                if not last:
                    gains[k, i * SUB : (i + 1) * SUB, :] = below * inverse
                    lead = 1.0 + below * (lead * inverse)
                new += [below, lead, heat, salt]
            return tuple(new)

        carry = []
        for i in range(blocks):
            r0 = base + i * SUB
            one = jnp.ones((SUB, LANES), F32)
            carry += [one, one, 0.5 * surface[0, r0 : r0 + SUB, :], 0.5 * surface[1, r0 : r0 + SUB, :]]
        spare = (levels - 1) % FORWARD
        carry = lax.fori_loop(0, levels - 1 - spare, forward, tuple(carry), unroll=FORWARD)
        for k in range(levels - 1 - spare, levels - 1):
            carry = forward(k, carry)
        carry = forward(levels - 1, carry, True)

        def finish(k, i, heat, salt):
            r0 = base + i * SUB
            wet = land[r0 : r0 + SUB, :] == 1
            values[0, k, r0 : r0 + SUB, :] = jnp.where(wet, heat, cells[0, k, r0 : r0 + SUB, :])
            values[1, k, r0 : r0 + SUB, :] = jnp.where(wet, salt, cells[1, k, r0 : r0 + SUB, :])

        def backward(step, carry):
            k = levels - 2 - step
            new = []
            for i in range(blocks):
                r0 = base + i * SUB
                heat, salt = carry[2 * i : 2 * i + 2]
                gain = gains[k, i * SUB : (i + 1) * SUB, :]
                heat = values[0, k, r0 : r0 + SUB, :] + gain * heat
                salt = values[1, k, r0 : r0 + SUB, :] + gain * salt
                finish(k, i, heat, salt)
                new += [heat, salt]
            return tuple(new)

        ends = []
        for i in range(blocks):
            heat, salt = carry[4 * i + 2 : 4 * i + 4]
            finish(levels - 1, i, heat, salt)
            ends += [heat, salt]
        spare = (levels - 1) % BACKWARD
        carry = lax.fori_loop(0, levels - 1 - spare, backward, tuple(ends), unroll=BACKWARD)
        for k in range(levels - 1 - spare, levels - 1):
            carry = backward(k, carry)
        store(c).start()
    for c in range(chunks):
        store(c).wait()


def step(cells, advected, diff, land, target, own, from_west, from_east, earlier, chunk_rows=64):
    _, levels, rows, cols = cells.shape
    links = target.shape[1]
    depth = np.arange(levels)
    decay = np.exp(-4.0 * depth / levels)
    absorb = decay - np.exp(-4.0 * (depth + 1.0) / levels)
    tables = jnp.asarray(np.stack([0.5 * absorb, decay]), F32)
    chunks = rows // chunk_rows
    hbm = pl.BlockSpec(memory_space=pl.ANY)
    vmem = pl.BlockSpec(memory_space=pltpu.VMEM)
    return pl.pallas_call(
        functools.partial(main_kernel, links, chunk_rows),
        in_specs=[pl.BlockSpec(memory_space=pltpu.SMEM)] + [vmem] * 9,
        out_specs=hbm,
        out_shape=jax.ShapeDtypeStruct(cells.shape, F32),
        scratch_shapes=[
            pltpu.VMEM((2, levels, rows, cols), F32),
            pltpu.VMEM((levels, chunk_rows, cols), F32),
            pltpu.VMEM((5, 4 * links // LANES, LANES), F32),
            pltpu.VMEM((5, rows, cols), F32),
            pltpu.VMEM((2, 2, rows, cols), F32),
            pltpu.SemaphoreType.DMA((chunks,)),
        ],
        compiler_params=pltpu.CompilerParams(vmem_limit_bytes=16 << 20),
        name="step",
    )(tables, cells, advected, diff, land, target, own, from_west, from_east, earlier)


def ring(axis, by):
    length = lax.axis_size(axis)
    return [(i, (i + by) % length) for i in range(length)]


def line(axis, by):
    length = lax.axis_size(axis)
    return [(i, i + by) for i in range(length) if 0 <= i + by < length]


def diagonal():
    lats = lax.axis_size("lat")
    lons = lax.axis_size("lon")
    return [
        (i * lons + j, (i + 1) * lons + (j + 1) % lons) for i in range(lats - 1) for j in range(lons)
    ]


def local(
    tracers,
    east_courant,
    north_courant,
    diffusivity,
    land_sea,
    fluxes,
    source_cell,
    link_weight,
    target_cell,
):
    _, levels, rows, cols = tracers.shape
    target = target_cell[0]
    cells, east, own, to_east, to_west, to_north, to_south, corner, own_links = load(
        tracers, east_courant, north_courant, fluxes, source_cell[0], link_weight[0]
    )
    from_corner = lax.ppermute(corner, ("lat", "lon"), diagonal())
    from_south = lax.ppermute(to_north, "lat", line("lat", 1))
    from_north = lax.ppermute(to_south, "lat", line("lat", -1))
    from_west = lax.ppermute(to_east, "lon", ring("lon", 1))
    from_east = lax.ppermute(to_west, "lon", ring("lon", -1))
    advected, diff = interior(cells, east, north_courant, diffusivity, from_south, from_north)
    earlier = remap(
        target, [(0, own_links, 0), (2, from_south, 5 * levels), (3, from_corner, 0)], rows, cols
    )
    return step(cells, advected, diff, land_sea, target, own, from_west, from_east, earlier)


def solution(mesh):
    in_specs = (
        P(None, None, "lat", "lon"),
        P(None, "lat", "lon"),
        P(None, "lat", "lon"),
        P(None, "lat", "lon"),
        P("lat", "lon"),
        P(None, ("lat", "lon")),
        P(("lat", "lon"), None, None),
        P(("lat", "lon"), None, None),
        P(("lat", "lon"), None, None),
    )
    out_specs = P(None, None, "lat", "lon")
    return jax.shard_map(local, mesh=mesh, in_specs=in_specs, out_specs=out_specs, check_vma=False)
```

time: 62 us -> 42 us (0.68)
  the two profiles are of different devices: /device:TPU:0 before, /device:TPU:8 now
where the time goes in v2:
time: 42 us; the launch traced here: 41.8 us
  Pallas kernels  25.6 us (61%)
  starting transfers between devices  10.4 us (25%)
  waiting for transfers between devices  5.55 us (13%)
    pallas_call x1, Pallas kernels, step(): pl.pallas_call(functools.partial(main_kernel, links, chunk_rows), in_spec...  10.2 us
    pallas_call x1, Pallas kernels, interior(): pl.pallas_call(interior_kernel, in_specs=[vmem] * 2 + [hbm] * 2 + [vmem]...  5.87 us
    ppermute x1, waiting for transfers between devices, local(): from_corner = lax.ppermute(corner, ('lat', 'lon'), diagonal())  5.54 us
    pallas_call x1, Pallas kernels, load(): pl.pallas_call(functools.partial(load_kernel, links), in_specs=[hbm] * 6,...  5.22 us
    pallas_call x1, Pallas kernels, remap(): pl.pallas_call(functools.partial(remap_kernel, links, rows, cols, numbers...  4.37 us
    ppermute x1, starting transfers between devices, local(): from_south = lax.ppermute(to_north, 'lat', line('lat', 1))  3.49 us
    ppermute x1, starting transfers between devices, local(): from_east = lax.ppermute(to_west, 'lon', ring('lon', -1))  2.39 us
    ppermute x1, starting transfers between devices, local(): from_north = lax.ppermute(to_south, 'lat', line('lat', -1))  2.35 us
  transfers between devices with their start and end apart: 5, of which 1 were waited for; matrix products, arithmetic and copies ran while one was open for 0% of the time, Pallas kernels for 24%

profile of v2, /device:TPU:8, one launch (start us, length us, event | category | flops | bytes accessed | tf_op | source)
XLA Modules:
  0.0 41.8 jit_solution(3944716919881594446)
XLA Ops:
  0.0 0.0 copy-start
  0.0 5.2 %load.1 = (f32[2,48,128,128]{3,2,1,0:T(8,128)S(1)}, f32[48,128,128]{2,1,0:T(8,128)S(1)}, f32[6,128,128]{2,1,0:T(8,128)S(1)}, f32[432,128]{1,0:T(8,128)S(1)}, f32...) custom-call(f32[2,48,128,128]{3,2,1,0:T(8,128)} %tracers.1, ...), custom_call_target="tpu_custom_call" | custom-call | tf_op jit(solution)/shard_map/load/pallas_call | solution.py:163
  5.2 0.1 collective-permute-start.2
  5.3 3.5 %collective-permute-start = (f32[416,128]{1,0:T(8,128)S(1)}, f32[416,128]{1,0:T(8,128)S(1)}, u32[]{:S(2)}, u32[]{:S(2)}) collective-permute-start(f32[416,128]{1,0:T(8,128)S(1)} %get-tuple-element.18), channel_id=1, source_target_pairs={{0,8},{8,16},{16,24},{1,9},{9,17},{17,25},{2,10},{10,18},{18,26},{... | collective-permute-start | bytes 638984 | tf_op jit(solution)/shard_map/ppermute | solution.py:620
  8.8 2.4 %collective-permute-start.3 = (f32[256,128]{1,0:T(8,128)S(1)}, f32[256,128]{1,0:T(8,128)S(1)}, u32[]{:S(2)}, u32[]{:S(2)}) collective-permute-start(f32[256,128]{1,0:T(8,128)S(1)} %get-tuple-element.24), channel_id=1, source_target_pairs={{0,7},{1,0},{2,1},{3,2},{4,3},{5,4},{6,5},{7,6},{8,15},{9,8},{10,9... | collective-permute-start | bytes 393224 | tf_op jit(solution)/shard_map/ppermute | solution.py:623
  11.2 2.4 %collective-permute-start.1 = (f32[192,128]{1,0:T(8,128)S(1)}, f32[192,128]{1,0:T(8,128)S(1)}, u32[]{:S(2)}, u32[]{:S(2)}) collective-permute-start(f32[192,128]{1,0:T(8,128)S(1)} %get-tuple-element.19), channel_id=1, source_target_pairs={{8,0},{16,8},{24,16},{9,1},{17,9},{25,17},{10,2},{18,10},{26,18},{... | collective-permute-start | bytes 294920 | tf_op jit(solution)/shard_map/ppermute | solution.py:621
  13.5 2.1 %collective-permute-start.4 = (f32[176,128]{1,0:T(8,128)S(1)}, f32[176,128]{1,0:T(8,128)S(1)}, u32[]{:S(2)}, u32[]{:S(2)}) collective-permute-start(f32[176,128]{1,0:T(8,128)S(1)} %get-tuple-element.26), channel_id=1, source_target_pairs={{0,9},{1,10},{2,11},{3,12},{4,13},{5,14},{6,15},{7,8},{8,17},{9,18... | collective-permute-start | bytes 270344 | tf_op jit(solution)/shard_map/ppermute | solution.py:619
  15.7 5.5 %collective-permute-done.4.refs_2_ = f32[176,128]{1,0:T(8,128)S(1)} collective-permute-done((f32[176,128]{1,0:T(8,128)S(1)}, f32[176,128]{1,0:T(8,128)S(1)}, u32[]{:S(2)}, u32[]{:S(2)}) %collective-permute-start.4) | collective-permute-done | bytes 90144 | tf_op jit(solution)/shard_map/ppermute | solution.py:619
  21.2 0.0 collective-permute-done.from_south.refs_1_
  21.2 0.0 copy-done
  21.2 4.4 %remap.1.earlier = f32[3,160,256]{2,1,0:T(8,128)S(1)} custom-call(s32[4,6144]{1,0:T(4,128)S(1)} %bitcast.3, f32[176,128]{1,0:T(8,128)S(1)} %get-tuple-element.25.refs_0_, f32[416,128]{1,0:T(8,128)S(1)} %collective-permute-done.from_south.refs_1_, f32[176,128]{1,0:T(8,128)S(1)} %collective-permute-done.4.refs_2_), custom_call_target="tpu_custom_call" | custom-call | tf_op jit(solution)/shard_map/remap/pallas_call | solution.py:358
  25.6 0.0 collective-permute-done.1.from_north
  25.6 0.0 copy-start.1
  25.6 0.0 copy-start.2
  25.6 5.9 %interior.1 = (f32[2,48,128,128]{3,2,1,0:T(8,128)S(1)}, f32[48,128,128]{2,1,0:T(8,128)S(1)}) custom-call(f32[2,48,128,128]{3,2,1,0:T(8,128)S(1)} %get-tuple-element.16.cells, f32[48,128,128]{2,1,0:T(8,128)S(1)} %get-tuple-element.17.east, f32[48,128,128]{2,1,0:T(8,128)} %north_courant.3, f32[48,128,128]{2,1,0:T(8,128)} %diffusivity.1, ...), custom_call_target="tpu_custom_call" | custom-call | tf_op jit(solution)/shard_map/interior/pallas_call | solution.py:276
  31.5 0.0 collective-permute-done.3.from_east
  31.5 0.0 collective-permute-done.2.from_west
  31.5 0.0 copy-done.1
  31.5 0.0 copy-done.2
  31.5 10.2 %step.1 = f32[2,48,128,128]{3,2,1,0:T(8,128)} custom-call(f32[2,48]{1,0:T(2,128)S(1)} %copy-done.2, f32[2,48,128,128]{3,2,1,0:T(8,128)S(1)} %get-tuple-element.16.cells, f32[2,48,128,128]{3,2,1,0:T(8,128)S(1)} %get-tuple-element.20.advected, f32[48,128,128]{2,1,0:T(8,128)S(1)} %get-tuple-element.21.diff, s32[128,128]{1,0:T(8,128)S(1)} %copy-done.1, ...), custom_call_target="tpu_custom_call" | custom-call | tf_op jit(solution)/shard_map/step/pallas_call | solution.py:567
Async XLA Ops:
  0.0 21.2 %copy-start = (s32[1,4,6144]{2,1,0:T(4,128)S(1)}, s32[1,4,6144]{2,1,0:T(4,128)}, u32[]{:S(2)}) copy-start(s32[1,4,6144]{2,1,0:T(4,128)} %param.18) | copy-start | bytes 294916
  5.2 26.3 %collective-permute-start.2 = (f32[432,128]{1,0:T(8,128)S(1)}, f32[432,128]{1,0:T(8,128)S(1)}, u32[]{:S(2)}, u32[]{:S(2)}) collective-permute-start(f32[432,128]{1,0:T(8,128)S(1)} %get-tuple-element.23), channel_id=1, source_target_pairs={{0,1},{1,2},{2,3},{3,4},{4,5},{5,6},{6,7},{7,0},{8,9},{9,10},{10,1... | collective-permute-start | bytes 663560 | tf_op jit(solution)/shard_map/ppermute | solution.py:622
  5.3 15.9 %collective-permute-start = (f32[416,128]{1,0:T(8,128)S(1)}, f32[416,128]{1,0:T(8,128)S(1)}, u32[]{:S(2)}, u32[]{:S(2)}) collective-permute-start(f32[416,128]{1,0:T(8,128)S(1)} %get-tuple-element.18), channel_id=1, source_target_pairs={{0,8},{8,16},{16,24},{1,9},{9,17},{17,25},{2,10},{10,18},{18,26},{... | collective-permute-start | bytes 638984 | tf_op jit(solution)/shard_map/ppermute | solution.py:620
  8.8 22.7 %collective-permute-start.3 = (f32[256,128]{1,0:T(8,128)S(1)}, f32[256,128]{1,0:T(8,128)S(1)}, u32[]{:S(2)}, u32[]{:S(2)}) collective-permute-start(f32[256,128]{1,0:T(8,128)S(1)} %get-tuple-element.24), channel_id=1, source_target_pairs={{0,7},{1,0},{2,1},{3,2},{4,3},{5,4},{6,5},{7,6},{8,15},{9,8},{10,9... | collective-permute-start | bytes 393224 | tf_op jit(solution)/shard_map/ppermute | solution.py:623
  11.2 14.4 %collective-permute-start.1 = (f32[192,128]{1,0:T(8,128)S(1)}, f32[192,128]{1,0:T(8,128)S(1)}, u32[]{:S(2)}, u32[]{:S(2)}) collective-permute-start(f32[192,128]{1,0:T(8,128)S(1)} %get-tuple-element.19), channel_id=1, source_target_pairs={{8,0},{16,8},{24,16},{9,1},{17,9},{25,17},{10,2},{18,10},{26,18},{... | collective-permute-start | bytes 294920 | tf_op jit(solution)/shard_map/ppermute | solution.py:621
  13.5 7.6 %collective-permute-start.4 = (f32[176,128]{1,0:T(8,128)S(1)}, f32[176,128]{1,0:T(8,128)S(1)}, u32[]{:S(2)}, u32[]{:S(2)}) collective-permute-start(f32[176,128]{1,0:T(8,128)S(1)} %get-tuple-element.26), channel_id=1, source_target_pairs={{0,9},{1,10},{2,11},{3,12},{4,13},{5,14},{6,15},{7,8},{8,17},{9,18... | collective-permute-start | bytes 270344 | tf_op jit(solution)/shard_map/ppermute | solution.py:619
  25.6 5.9 %copy-start.1 = (s32[128,128]{1,0:T(8,128)S(1)}, s32[128,128]{1,0:T(8,128)}, u32[]{:S(2)}) copy-start(s32[128,128]{1,0:T(8,128)} %land.1) | copy-start | bytes 196612
  25.6 5.9 %copy-start.2 = (f32[2,48]{1,0:T(2,128)S(1)}, f32[2,48]{1,0:T(2,128)}, u32[]{:S(2)}) copy-start(f32[2,48]{1,0:T(2,128)} %constant.2.clone.tables) | copy-start | bytes 1156

commit v3 on v2

--- a/solution.py
+++ b/solution.py
@@ -45,13 +45,18 @@
     south_msg,
     corner_msg,
     own_msg,
+    own_rows,
     flux_in,
     source_in,
     weight_in,
+    first_north,
     last_north,
     sem,
 ):
     _, levels, rows, _ = tracers.shape
+    lat = lax.axis_index("lat")
+    has_north = (lat < lax.axis_size("lat") - 1).astype(F32)
+    has_south = (lat > 0).astype(F32)
     part = levels // PARTS
     half = levels // 2
     small = [
@@ -59,6 +64,7 @@
         pltpu.make_async_copy(source, source_in, sem.at[1]),
         pltpu.make_async_copy(weight, weight_in, sem.at[2]),
         pltpu.make_async_copy(north_courant.at[:, pl.ds(rows - SUB, SUB), :], last_north, sem.at[3]),
+        pltpu.make_async_copy(north_courant.at[:, pl.ds(0, SUB), :], first_north, sem.at[4 + 3 * PARTS]),
     ]
     large = []
     for q in range(PARTS):
@@ -91,9 +97,13 @@
         for c in range(links // LANES):
             cut = pl.ds(c * LANES, LANES)
             msg[pl.ds(base + c, 1), :] = source_in[n : n + 1, cut].astype(F32)
-            msg[pl.ds(base + links // LANES + c, 1), :] = weight_in[n : n + 1, cut]
+            row = weight_in[n : n + 1, cut]
+            msg[pl.ds(base + links // LANES + c, 1), :] = row * has_north if n >= 2 else row
     for k in range(levels):
-        north_msg[pl.ds(4 * levels + k, 1), :] = last_north[k, SUB - 1 : SUB, :]
+        north_msg[pl.ds(4 * levels + k, 1), :] = last_north[k, SUB - 1 : SUB, :] * has_north
+        own_rows[pl.ds(k, 1), :] = first_north[k, 0:1, :]
+        own_rows[pl.ds(levels + k, 1), :] = last_north[k, SUB - 2 : SUB - 1, :]
+        own_rows[pl.ds(2 * levels + k, 1), :] = last_north[k, SUB - 1 : SUB, :]
 
     lane = lane_of((SUB, LANES))
     group = lane // 4
@@ -116,9 +126,13 @@
         lax.fori_loop(0, rows // SUB, pack, 0, unroll=PACK)
         for t in range(2):
             for k in range(q * part, (q + 1) * part):
-                at = pl.ds(2 * (t * levels + k), 2)
-                south_msg[at, :] = cells[t, k, 0:2, :]
-                north_msg[at, :] = cells[t, k, rows - 2 : rows, :]
+                for j in range(2):
+                    at = pl.ds((2 * t + j) * levels + k, 1)
+                    low = cells[t, k, j : j + 1, :]
+                    high = cells[t, k, rows - 2 + j : rows - 1 + j, :]
+                    south_msg[at, :] = low * has_south
+                    north_msg[at, :] = high * has_north
+                    own_rows[pl.ds((3 + 2 * t + j) * levels + k, 1), :] = low
 
     early = lane % 4 < 2
     spare = lane >= 2 * levels
@@ -159,6 +173,7 @@
         (4 * levels, LANES),
         (remap, LANES),
         (remap, LANES),
+        (7 * levels, LANES),
     ]
     return pl.pallas_call(
         functools.partial(load_kernel, links),
@@ -170,7 +185,8 @@
             pltpu.VMEM(source.shape, jnp.int32),
             pltpu.VMEM(weight.shape, F32),
             pltpu.VMEM((levels, SUB, cols), F32),
-            pltpu.SemaphoreType.DMA((4 + 3 * PARTS,)),
+            pltpu.VMEM((levels, SUB, cols), F32),
+            pltpu.SemaphoreType.DMA((5 + 3 * PARTS,)),
         ],
         compiler_params=pltpu.CompilerParams(vmem_limit_bytes=16 << 20),
         name="load",
@@ -192,8 +208,6 @@
     east,
     north_courant,
     diffusivity,
-    from_south,
-    from_north,
     advected,
     diff,
     weights,
@@ -214,43 +228,28 @@
         copy.start()
     last.start()
 
-    def halo_row(msg, index):
-        return jnp.broadcast_to(msg[pl.ds(index, 1), :], (SUB, LANES))
-
     def level(k, carry):
         west_courant = [pltpu.roll(east[k, i * SUB : (i + 1) * SUB, :], 1, 1) for i in range(blocks)]
         for t in range(2):
-            unit = t * levels + k
             whole = cells[t, k]
             high = whole.astype(BF16)
             low = (whole - high.astype(F32)).astype(BF16)
             faces = jnp.dot(
                 jnp.concatenate([high, low], 1), weights[...], preferred_element_type=F32
             )
-            below = from_south[pl.ds(2 * unit, 2), :]
-            inside = cells[t, k, 0:2, :]
-            courant = from_south[pl.ds(4 * levels + k, 1), :]
-            south = courant * (7.0 * (below[1:2] + inside[0:1]) - (below[0:1] + inside[1:2]))
-            south = jnp.broadcast_to(south, (SUB, LANES))
+            south = jnp.zeros((SUB, LANES), F32)
             for i in range(blocks):
                 r0 = i * SUB
                 here = cells[t, k, r0 : r0 + SUB, :]
                 east_flux = east[k, r0 : r0 + SUB, :] * faces[r0 : r0 + SUB, :cols]
                 west_flux = west_courant[i] * faces[r0 : r0 + SUB, cols:]
                 if i == 0:
-                    low_one = jnp.where(
-                        sub == 0, halo_row(from_south, 2 * unit + 1), pltpu.roll(here, 1, 0)
-                    )
+                    low_one = jnp.where(sub == 0, 0.0, pltpu.roll(here, 1, 0))
                 else:
                     low_one = cells[t, k, r0 - 1 : r0 - 1 + SUB, :]
                 if i == blocks - 1:
-                    near = halo_row(from_north, 2 * unit)
-                    far = halo_row(from_north, 2 * unit + 1)
-                    up_one = jnp.where(sub == SUB - 1, near, pltpu.roll(here, SUB - 1, 0))
-                    up_two = pltpu.roll(here, SUB - 2, 0)
-                    up_two = jnp.where(
-                        sub == SUB - 1, far, jnp.where(sub == SUB - 2, near, up_two)
-                    )
+                    up_one = jnp.where(sub == SUB - 1, 0.0, pltpu.roll(here, SUB - 1, 0))
+                    up_two = jnp.where(sub >= SUB - 2, 0.0, pltpu.roll(here, SUB - 2, 0))
                 else:
                     up_one = cells[t, k, r0 + 1 : r0 + 1 + SUB, :]
                     up_two = cells[t, k, r0 + 2 : r0 + 2 + SUB, :]
@@ -269,13 +268,13 @@
     last.wait()
 
 
-def interior(cells, east, north_courant, diffusivity, from_south, from_north):
+def interior(cells, east, north_courant, diffusivity):
     _, levels, rows, cols = cells.shape
     hbm = pl.BlockSpec(memory_space=pltpu.HBM)
     vmem = pl.BlockSpec(memory_space=pltpu.VMEM)
     return pl.pallas_call(
         interior_kernel,
-        in_specs=[vmem] * 2 + [hbm] * 2 + [vmem] * 2,
+        in_specs=[vmem] * 2 + [hbm] * 2,
         out_specs=[vmem] * 2,
         out_shape=[pltpu.VMEM(cells.shape, F32), pltpu.VMEM(diffusivity.shape, F32)],
         scratch_shapes=[
@@ -285,7 +284,7 @@
         ],
         compiler_params=pltpu.CompilerParams(vmem_limit_bytes=16 << 20),
         name="interior",
-    )(cells, east, *in_hbm(north_courant, diffusivity), from_south, from_north)
+    )(cells, east, *in_hbm(north_courant, diffusivity))
 
 
 def gather_links(msg, base, n, links, picked):
@@ -378,6 +377,9 @@
     own,
     from_west,
     from_east,
+    own_rows,
+    from_south,
+    from_north,
     earlier,
     out,
     values,
@@ -385,16 +387,18 @@
     picked,
     surface,
     fix,
+    row_fix,
     out_sem,
 ):
     _, levels, rows, cols = cells.shape
     chunks = rows // chunk_rows
     lane = lane_of((SUB, LANES))
 
-    def store(c):
+    def store(c, q):
         part = pl.ds(c * chunk_rows, chunk_rows)
+        at = pl.ds(q * (levels // PARTS), levels // PARTS)
         return pltpu.make_async_copy(
-            values.at[:, :, part, :], out.at[:, :, part, :], out_sem.at[c]
+            values.at[:, at, part, :], out.at[:, at, part, :], out_sem.at[c, q]
         )
 
     gather_links(from_west, 2 * rows, 1, links, picked)
@@ -467,8 +471,31 @@
 
         lax.fori_loop(0, rows // SUB, mend, 0, unroll=4)
 
+    def plane(msg, p):
+        return msg[p * levels : (p + 1) * levels, :]
+
+    for t in range(2):
+        inner_one = plane(own_rows, 3 + 2 * t)
+        inner_two = plane(own_rows, 4 + 2 * t)
+        below_two = plane(from_south, 2 * t)
+        below_one = plane(from_south, 2 * t + 1)
+        above_one = plane(from_north, 2 * t)
+        above_two = plane(from_north, 2 * t + 1)
+        first = plane(own_rows, 0) * below_one
+        entering = plane(from_south, 4) * (7.0 * (below_one + inner_one) - (below_two + inner_two))
+        last = plane(own_rows, 1) * above_one
+        top = plane(own_rows, 2) * (7.0 * above_one - above_two)
+        for p, change in enumerate((-first - entering, first, -last, top + last)):
+            row_fix[t, p] = change * (-1.0 / 12.0)
+
     at_edge = (lane >= LANES - 2) | (lane < 2)
+    sub = lax.broadcasted_iota(jnp.int32, (SUB, LANES), 0)
     blocks = chunk_rows // SUB
+
+    def row_pair(t, k, p, at):
+        one = jnp.broadcast_to(row_fix[t, p, pl.ds(k, 1), :], (SUB, LANES))
+        two = jnp.broadcast_to(row_fix[t, p + 1, pl.ds(k, 1), :], (SUB, LANES))
+        return jnp.where(sub == at, one, jnp.where(sub == at + 1, two, 0.0))
 
     def advect(t, k, base):
         side = k // half
@@ -477,7 +504,12 @@
         for i in range(blocks):
             at = pl.ds(base + i * SUB, SUB)
             edge = pltpu.roll(fix[t, side, at, :], shift, 1)
-            result.append(advected[t, k, at, :] + jnp.where(at_edge, edge, 0.0))
+            value = advected[t, k, at, :] + jnp.where(at_edge, edge, 0.0)
+            if base + i * SUB == 0:
+                value = value + row_pair(t, k, 0, 0)
+            if base + (i + 1) * SUB == rows:
+                value = value + row_pair(t, k, 2, SUB - 2)
+            result.append(value)
         return result
 
     for c in range(chunks):
@@ -545,16 +577,22 @@
             heat, salt = carry[4 * i + 2 : 4 * i + 4]
             finish(levels - 1, i, heat, salt)
             ends += [heat, salt]
-        spare = (levels - 1) % BACKWARD
-        carry = lax.fori_loop(0, levels - 1 - spare, backward, tuple(ends), unroll=BACKWARD)
-        for k in range(levels - 1 - spare, levels - 1):
-            carry = backward(k, carry)
-        store(c).start()
+        carry = backward(0, tuple(ends))
+        done = 1
+        for q in reversed(range(PARTS)):
+            until = levels - 1 - q * (levels // PARTS)
+            while (until - done) % BACKWARD:
+                carry = backward(done, carry)
+                done += 1
+            carry = lax.fori_loop(done, until, backward, carry, unroll=BACKWARD)
+            done = until
+            store(c, q).start()
     for c in range(chunks):
-        store(c).wait()
-
-
-def step(cells, advected, diff, land, target, own, from_west, from_east, earlier, chunk_rows=64):
+        for q in range(PARTS):
+            store(c, q).wait()
+
+
+def step(cells, advected, diff, land, target, messages, chunk_rows=64):
     _, levels, rows, cols = cells.shape
     links = target.shape[1]
     depth = np.arange(levels)
@@ -566,7 +604,7 @@
     vmem = pl.BlockSpec(memory_space=pltpu.VMEM)
     return pl.pallas_call(
         functools.partial(main_kernel, links, chunk_rows),
-        in_specs=[pl.BlockSpec(memory_space=pltpu.SMEM)] + [vmem] * 9,
+        in_specs=[pl.BlockSpec(memory_space=pltpu.SMEM)] + [vmem] * (5 + len(messages)),
         out_specs=hbm,
         out_shape=jax.ShapeDtypeStruct(cells.shape, F32),
         scratch_shapes=[
@@ -575,28 +613,24 @@
             pltpu.VMEM((5, 4 * links // LANES, LANES), F32),
             pltpu.VMEM((5, rows, cols), F32),
             pltpu.VMEM((2, 2, rows, cols), F32),
-            pltpu.SemaphoreType.DMA((chunks,)),
+            pltpu.VMEM((2, 4, levels, cols), F32),
+            pltpu.SemaphoreType.DMA((chunks, PARTS)),
         ],
         compiler_params=pltpu.CompilerParams(vmem_limit_bytes=16 << 20),
         name="step",
-    )(tables, cells, advected, diff, land, target, own, from_west, from_east, earlier)
+    )(tables, cells, advected, diff, land, target, *messages)
 
 
 def ring(axis, by):
     length = lax.axis_size(axis)
     return [(i, (i + by) % length) for i in range(length)]
-
-
-def line(axis, by):
-    length = lax.axis_size(axis)
-    return [(i, i + by) for i in range(length) if 0 <= i + by < length]
 
 
 def diagonal():
     lats = lax.axis_size("lat")
     lons = lax.axis_size("lon")
     return [
-        (i * lons + j, (i + 1) * lons + (j + 1) % lons) for i in range(lats - 1) for j in range(lons)
+        (i * lons + j, (i + 1) % lats * lons + (j + 1) % lons) for i in range(lats) for j in range(lons)
     ]
 
 
@@ -613,19 +647,20 @@
 ):
     _, levels, rows, cols = tracers.shape
     target = target_cell[0]
-    cells, east, own, to_east, to_west, to_north, to_south, corner, own_links = load(
+    cells, east, own, to_east, to_west, to_north, to_south, corner, own_links, own_rows = load(
         tracers, east_courant, north_courant, fluxes, source_cell[0], link_weight[0]
     )
     from_corner = lax.ppermute(corner, ("lat", "lon"), diagonal())
-    from_south = lax.ppermute(to_north, "lat", line("lat", 1))
-    from_north = lax.ppermute(to_south, "lat", line("lat", -1))
+    from_south = lax.ppermute(to_north, "lat", ring("lat", 1))
+    from_north = lax.ppermute(to_south, "lat", ring("lat", -1))
     from_west = lax.ppermute(to_east, "lon", ring("lon", 1))
     from_east = lax.ppermute(to_west, "lon", ring("lon", -1))
-    advected, diff = interior(cells, east, north_courant, diffusivity, from_south, from_north)
+    advected, diff = interior(cells, east, north_courant, diffusivity)
     earlier = remap(
         target, [(0, own_links, 0), (2, from_south, 5 * levels), (3, from_corner, 0)], rows, cols
     )
-    return step(cells, advected, diff, land_sea, target, own, from_west, from_east, earlier)
+    messages = (own, from_west, from_east, own_rows, from_south, from_north, earlier)
+    return step(cells, advected, diff, land_sea, target, messages)
 
 
 def solution(mesh):

time: 42 us -> 36.8 us (0.88)
  the two profiles are of different devices: /device:TPU:8 before, /device:TPU:0 now
where the time goes in v3:
time: 36.8 us; the launch traced here: 36.7 us
  Pallas kernels  25.4 us (69%)
  starting transfers between devices  7.75 us (21%)
  waiting for transfers between devices  3.25 us (9%)
    pallas_call x1, Pallas kernels, step(): pl.pallas_call(functools.partial(main_kernel, links, chunk_rows), in_spec...  9.9 us
    pallas_call x1, Pallas kernels, interior(): pl.pallas_call(interior_kernel, in_specs=[vmem] * 2 + [hbm] * 2, out_spec...  5.77 us
    pallas_call x1, Pallas kernels, load(): pl.pallas_call(functools.partial(load_kernel, links), in_specs=[hbm] * 6,...  5.36 us
    pallas_call x1, Pallas kernels, remap(): pl.pallas_call(functools.partial(remap_kernel, links, rows, cols, numbers...  4.38 us
    ppermute x1, waiting for transfers between devices, local(): from_corner = lax.ppermute(corner, ('lat', 'lon'), diagonal())  3.23 us
    ppermute x1, starting transfers between devices, local(): from_south = lax.ppermute(to_north, 'lat', ring('lat', 1))  2.64 us
    ppermute x1, starting transfers between devices, local(): from_north = lax.ppermute(to_south, 'lat', ring('lat', -1))  2.31 us
    ppermute x1, starting transfers between devices, local(): from_east = lax.ppermute(to_west, 'lon', ring('lon', -1))  2.3 us
  transfers between devices with their start and end apart: 5, of which 1 were waited for; matrix products, arithmetic and copies ran while one was open for 0% of the time, Pallas kernels for 28%

profile of v3, /device:TPU:0, one launch (start us, length us, event | category | flops | bytes accessed | tf_op | source)
XLA Modules:
  0.0 36.7 jit_solution(9428812620939967096)
XLA Ops:
  0.0 5.4 %load.1 = (f32[2,48,128,128]{3,2,1,0:T(8,128)S(1)}, f32[48,128,128]{2,1,0:T(8,128)S(1)}, f32[6,128,128]{2,1,0:T(8,128)S(1)}, f32[432,128]{1,0:T(8,128)S(1)}, f32...) custom-call(f32[2,48,128,128]{3,2,1,0:T(8,128)} %tracers.1, ...), custom_call_target="tpu_custom_call" | custom-call | tf_op jit(solution)/shard_map/load/pallas_call | solution.py:178
  5.4 0.5 %collective-permute-start = (f32[432,128]{1,0:T(8,128)S(1)}, f32[432,128]{1,0:T(8,128)S(1)}, u32[]{:S(2)}, u32[]{:S(2)}) collective-permute-start(f32[432,128]{1,0:T(8,128)S(1)} %get-tuple-element.22), channel_id=1, source_target_pairs={{0,1},{1,2},{2,3},{3,4},{4,5},{5,6},{6,7},{7,0},{8,9},{9,10},{10,1... | collective-permute-start | bytes 663560 | tf_op jit(solution)/shard_map/ppermute | solution.py:656
  5.9 2.6 %collective-permute-start.2 = (f32[416,128]{1,0:T(8,128)S(1)}, f32[416,128]{1,0:T(8,128)S(1)}, u32[]{:S(2)}, u32[]{:S(2)}) collective-permute-start(f32[416,128]{1,0:T(8,128)S(1)} %get-tuple-element.25), channel_id=1, source_target_pairs={{0,8},{8,16},{16,24},{24,0},{1,9},{9,17},{17,25},{25,1},{2,10},{10... | collective-permute-start | bytes 638984 | tf_op jit(solution)/shard_map/ppermute | solution.py:654
  8.5 2.3 %collective-permute-start.1 = (f32[256,128]{1,0:T(8,128)S(1)}, f32[256,128]{1,0:T(8,128)S(1)}, u32[]{:S(2)}, u32[]{:S(2)}) collective-permute-start(f32[256,128]{1,0:T(8,128)S(1)} %get-tuple-element.23), channel_id=1, source_target_pairs={{0,7},{1,0},{2,1},{3,2},{4,3},{5,4},{6,5},{7,6},{8,15},{9,8},{10,9... | collective-permute-start | bytes 393224 | tf_op jit(solution)/shard_map/ppermute | solution.py:657
  10.8 2.3 %collective-permute-start.3 = (f32[192,128]{1,0:T(8,128)S(1)}, f32[192,128]{1,0:T(8,128)S(1)}, u32[]{:S(2)}, u32[]{:S(2)}) collective-permute-start(f32[192,128]{1,0:T(8,128)S(1)} %get-tuple-element.26), channel_id=1, source_target_pairs={{0,24},{8,0},{16,8},{24,16},{1,25},{9,1},{17,9},{25,17},{2,26},{10... | collective-permute-start | bytes 294920 | tf_op jit(solution)/shard_map/ppermute | solution.py:655
  13.1 0.0 collective-permute-start.4
  13.1 0.0 copy-start
  13.1 0.0 copy-start.1
  13.1 0.0 copy-start.2
  13.1 5.8 %interior.1 = (f32[2,48,128,128]{3,2,1,0:T(8,128)S(1)}, f32[48,128,128]{2,1,0:T(8,128)S(1)}) custom-call(f32[2,48,128,128]{3,2,1,0:T(8,128)S(1)} %get-tuple-element.17.cells, f32[48,128,128]{2,1,0:T(8,128)S(1)} %get-tuple-element.18.east, f32[48,128,128]{2,1,0:T(8,128)} %north_courant.3, f32[48,128,128]{2,1,0:T(8,128)} %diffusivity.1), custom_call_target="tpu_custom_call" | custom-call | tf_op jit(solution)/shard_map/interior/pallas_call | solution.py:275
  18.9 3.2 %collective-permute-done.4.refs_2_ = f32[176,128]{1,0:T(8,128)S(1)} collective-permute-done((f32[176,128]{1,0:T(8,128)S(1)}, f32[176,128]{1,0:T(8,128)S(1)}, u32[]{:S(2)}, u32[]{:S(2)}) %collective-permute-start.4) | collective-permute-done | bytes 90144 | tf_op jit(solution)/shard_map/ppermute | solution.py:653
  22.1 0.0 collective-permute-done.2.refs_1_.from_south
  22.1 0.0 copy-done
  22.2 4.4 %remap.1.earlier = f32[3,160,256]{2,1,0:T(8,128)S(1)} custom-call(s32[4,6144]{1,0:T(4,128)S(1)} %bitcast.3, f32[176,128]{1,0:T(8,128)S(1)} %get-tuple-element.27.refs_0_, f32[416,128]{1,0:T(8,128)S(1)} %collective-permute-done.2.refs_1_.from_south, f32[176,128]{1,0:T(8,128)S(1)} %collective-permute-done.4.refs_2_), custom_call_target="tpu_custom_call" | custom-call | tf_op jit(solution)/shard_map/remap/pallas_call | solution.py:357
  26.5 0.0 collective-permute-done.3.from_north
  26.6 0.0 collective-permute-done.1.from_east
  26.6 0.0 collective-permute-done.from_west
  26.6 0.0 copy-done.1
  26.6 0.0 copy-done.2
  26.6 9.9 %step.1 = f32[2,48,128,128]{3,2,1,0:T(8,128)} custom-call(f32[2,48]{1,0:T(2,128)S(1)} %copy-done.2, f32[2,48,128,128]{3,2,1,0:T(8,128)S(1)} %get-tuple-element.17.cells, f32[2,48,128,128]{3,2,1,0:T(8,128)S(1)} %get-tuple-element.19.advected, f32[48,128,128]{2,1,0:T(8,128)S(1)} %get-tuple-element.20.diff, s32[128,128]{1,0:T(8,128)S(1)} %copy-done.1, ...), custom_call_target="tpu_custom_call" | custom-call | tf_op jit(solution)/shard_map/step/pallas_call | solution.py:605
Async XLA Ops:
  5.4 21.2 %collective-permute-start = (f32[432,128]{1,0:T(8,128)S(1)}, f32[432,128]{1,0:T(8,128)S(1)}, u32[]{:S(2)}, u32[]{:S(2)}) collective-permute-start(f32[432,128]{1,0:T(8,128)S(1)} %get-tuple-element.22), channel_id=1, source_target_pairs={{0,1},{1,2},{2,3},{3,4},{4,5},{5,6},{6,7},{7,0},{8,9},{9,10},{10,1... | collective-permute-start | bytes 663560 | tf_op jit(solution)/shard_map/ppermute | solution.py:656
  5.9 16.3 %collective-permute-start.2 = (f32[416,128]{1,0:T(8,128)S(1)}, f32[416,128]{1,0:T(8,128)S(1)}, u32[]{:S(2)}, u32[]{:S(2)}) collective-permute-start(f32[416,128]{1,0:T(8,128)S(1)} %get-tuple-element.25), channel_id=1, source_target_pairs={{0,8},{8,16},{16,24},{24,0},{1,9},{9,17},{17,25},{25,1},{2,10},{10... | collective-permute-start | bytes 638984 | tf_op jit(solution)/shard_map/ppermute | solution.py:654
  8.5 18.0 %collective-permute-start.1 = (f32[256,128]{1,0:T(8,128)S(1)}, f32[256,128]{1,0:T(8,128)S(1)}, u32[]{:S(2)}, u32[]{:S(2)}) collective-permute-start(f32[256,128]{1,0:T(8,128)S(1)} %get-tuple-element.23), channel_id=1, source_target_pairs={{0,7},{1,0},{2,1},{3,2},{4,3},{5,4},{6,5},{7,6},{8,15},{9,8},{10,9... | collective-permute-start | bytes 393224 | tf_op jit(solution)/shard_map/ppermute | solution.py:657
  10.8 15.7 %collective-permute-start.3 = (f32[192,128]{1,0:T(8,128)S(1)}, f32[192,128]{1,0:T(8,128)S(1)}, u32[]{:S(2)}, u32[]{:S(2)}) collective-permute-start(f32[192,128]{1,0:T(8,128)S(1)} %get-tuple-element.26), channel_id=1, source_target_pairs={{0,24},{8,0},{16,8},{24,16},{1,25},{9,1},{17,9},{25,17},{2,26},{10... | collective-permute-start | bytes 294920 | tf_op jit(solution)/shard_map/ppermute | solution.py:655
  13.1 9.0 %collective-permute-start.4 = (f32[176,128]{1,0:T(8,128)S(1)}, f32[176,128]{1,0:T(8,128)S(1)}, u32[]{:S(2)}, u32[]{:S(2)}) collective-permute-start(f32[176,128]{1,0:T(8,128)S(1)} %get-tuple-element.28), channel_id=1, source_target_pairs={{0,9},{1,10},{2,11},{3,12},{4,13},{5,14},{6,15},{7,8},{8,17},{9,18... | collective-permute-start | bytes 270344 | tf_op jit(solution)/shard_map/ppermute | solution.py:653
  13.1 9.0 %copy-start = (s32[1,4,6144]{2,1,0:T(4,128)S(1)}, s32[1,4,6144]{2,1,0:T(4,128)}, u32[]{:S(2)}) copy-start(s32[1,4,6144]{2,1,0:T(4,128)} %param.18) | copy-start | bytes 294916
  13.1 13.4 %copy-start.1 = (s32[128,128]{1,0:T(8,128)S(1)}, s32[128,128]{1,0:T(8,128)}, u32[]{:S(2)}) copy-start(s32[128,128]{1,0:T(8,128)} %land.1) | copy-start | bytes 196612
  13.1 13.5 %copy-start.2 = (f32[2,48]{1,0:T(2,128)S(1)}, f32[2,48]{1,0:T(2,128)}, u32[]{:S(2)}) copy-start(f32[2,48]{1,0:T(2,128)} %constant.2.clone.tables) | copy-start | bytes 1156

commit v4 on v3

--- a/solution.py
+++ b/solution.py
@@ -309,10 +309,11 @@
     count = links // LANES
     wide = 4 * half_cols
     short = half_rows // 4
-    tall_iota = lax.broadcasted_iota(jnp.int32, (wide, LANES), 0)
+    tall_iota = lax.broadcasted_iota(jnp.int32, (wide, LANES), 0).astype(jnp.int16)
     short_iota = lax.broadcasted_iota(jnp.int32, (short, LANES), 0)
-    total = jnp.zeros((10 * short, wide), F32)
-    group = 8
+    ones = jnp.ones((wide, LANES), BF16)
+    total = jnp.zeros((wide, 10 * short), F32)
+    group = count
     for g in range(count // group):
         lefts = []
         rights = []
@@ -321,8 +322,9 @@
             row = cell // cols - (1 - n // 2) * half_rows
             col = cell % cols - (1 - n % 2) * half_cols
             short_at = jnp.broadcast_to(row % short, (short, LANES)) == short_iota
-            wide_at = jnp.broadcast_to(row // short * half_cols + col, (wide, LANES)) == tall_iota
-            rights.append(jnp.where(wide_at, 1.0, 0.0).astype(BF16))
+            place = (row // short * half_cols + col).astype(jnp.int16)
+            wide_at = jnp.broadcast_to(place, (wide, LANES)) == tall_iota
+            rights.append(jnp.where(wide_at, ones, jnp.zeros_like(ones)))
             pieces = []
             for f in range(5):
                 value = picked[f, pl.ds(n * count + c, 1), :]
@@ -335,56 +337,53 @@
         left = jnp.concatenate(lefts, 1)
         right = jnp.concatenate(rights, 1)
         total = total + lax.dot_general(
-            left, right, (((1,), (1,)), ((), ())), preferred_element_type=F32
+            right, left, (((1,), (1,)), ((), ())), preferred_element_type=F32
         )
-    return total
+    return total.T
 
 
 def remap_kernel(links, rows, cols, numbers, bases, target, *refs):
     count = len(numbers)
-    quads = refs[count]
-    picked = refs[count + 1]
+    quads, picked = refs[-2:]
     for i, (n, base) in enumerate(zip(numbers, bases)):
         gather_links(refs[i], base, n, links, picked)
         quads[i] = scatter_links(picked, target, n, links, rows, cols)
 
 
-def remap(target, blocks, rows, cols):
+def remap(target, blocks, rows, cols, after=()):
     links = target.shape[1]
     numbers = tuple(n for n, _, _ in blocks)
     bases = tuple(base for _, _, base in blocks)
     vmem = pl.BlockSpec(memory_space=pltpu.VMEM)
     return pl.pallas_call(
         functools.partial(remap_kernel, links, rows, cols, numbers, bases),
-        in_specs=[vmem] * (1 + len(blocks)),
+        in_specs=[vmem] * (1 + len(blocks)) + [pl.BlockSpec(memory_space=pl.ANY)] * len(after),
         out_specs=vmem,
         out_shape=jax.ShapeDtypeStruct((len(blocks), 10 * rows // 8, 2 * cols), F32),
         scratch_shapes=[pltpu.VMEM((5, 4 * links // LANES, LANES), F32)],
         compiler_params=pltpu.CompilerParams(vmem_limit_bytes=16 << 20),
         name="remap",
-    )(target, *[msg for _, msg, _ in blocks])
+    )(target, *[msg for _, msg, _ in blocks], *after)
 
 
 def main_kernel(
-    links,
     chunk_rows,
     tables,
     cells,
     advected,
     diff,
     land,
-    target,
     own,
     from_west,
     from_east,
     own_rows,
     from_south,
     from_north,
-    earlier,
+    upper,
+    lower,
     out,
     values,
     gains,
-    picked,
     surface,
     fix,
     row_fix,
@@ -401,9 +400,7 @@
             values.at[:, at, part, :], out.at[:, at, part, :], out_sem.at[c, q]
         )
 
-    gather_links(from_west, 2 * rows, 1, links, picked)
-    eastern = scatter_links(picked, target, 1, links, rows, cols)
-    quads = [earlier[0], eastern, earlier[1], earlier[2]]
+    quads = [upper[0], upper[1], lower[0], lower[1]]
     short = rows // 8
     for pair in range(2):
         left = quads[2 * pair + 1]
@@ -592,9 +589,8 @@
             store(c, q).wait()
 
 
-def step(cells, advected, diff, land, target, messages, chunk_rows=64):
+def step(cells, advected, diff, land, messages, chunk_rows=64):
     _, levels, rows, cols = cells.shape
-    links = target.shape[1]
     depth = np.arange(levels)
     decay = np.exp(-4.0 * depth / levels)
     absorb = decay - np.exp(-4.0 * (depth + 1.0) / levels)
@@ -603,14 +599,13 @@
     hbm = pl.BlockSpec(memory_space=pl.ANY)
     vmem = pl.BlockSpec(memory_space=pltpu.VMEM)
     return pl.pallas_call(
-        functools.partial(main_kernel, links, chunk_rows),
-        in_specs=[pl.BlockSpec(memory_space=pltpu.SMEM)] + [vmem] * (5 + len(messages)),
+        functools.partial(main_kernel, chunk_rows),
+        in_specs=[pl.BlockSpec(memory_space=pltpu.SMEM)] + [vmem] * (4 + len(messages)),
         out_specs=hbm,
         out_shape=jax.ShapeDtypeStruct(cells.shape, F32),
         scratch_shapes=[
             pltpu.VMEM((2, levels, rows, cols), F32),
             pltpu.VMEM((levels, chunk_rows, cols), F32),
-            pltpu.VMEM((5, 4 * links // LANES, LANES), F32),
             pltpu.VMEM((5, rows, cols), F32),
             pltpu.VMEM((2, 2, rows, cols), F32),
             pltpu.VMEM((2, 4, levels, cols), F32),
@@ -618,7 +613,7 @@
         ],
         compiler_params=pltpu.CompilerParams(vmem_limit_bytes=16 << 20),
         name="step",
-    )(tables, cells, advected, diff, land, target, *messages)
+    )(tables, cells, advected, diff, land, *messages)
 
 
 def ring(axis, by):
@@ -656,11 +651,10 @@
     from_west = lax.ppermute(to_east, "lon", ring("lon", 1))
     from_east = lax.ppermute(to_west, "lon", ring("lon", -1))
     advected, diff = interior(cells, east, north_courant, diffusivity)
-    earlier = remap(
-        target, [(0, own_links, 0), (2, from_south, 5 * levels), (3, from_corner, 0)], rows, cols
-    )
-    messages = (own, from_west, from_east, own_rows, from_south, from_north, earlier)
-    return step(cells, advected, diff, land_sea, target, messages)
+    upper = remap(target, [(0, own_links, 0), (1, from_west, 2 * rows)], rows, cols)
+    lower = remap(target, [(2, from_south, 5 * levels), (3, from_corner, 0)], rows, cols, [upper])
+    messages = (own, from_west, from_east, own_rows, from_south, from_north, upper, lower)
+    return step(cells, advected, diff, land_sea, messages)
 
 
 def solution(mesh):

time: 36.8 us -> 32.8 us (0.89)
  waiting for transfers between devices: 3.25 us -> 0.52 us
  Pallas kernels: 25.4 us -> 24.3 us
    ppermute x1, waiting for transfers between devices: 3.23 us -> 0.5 us  [local(): from_corner = lax.ppermute(corner, ('lat', 'lon'), diagonal())]
    pallas_call x1, Pallas kernels: 9.9 us -> 8.17 us  [step(): pl.pallas_call(functools.partial(main_kernel, chunk_rows), in_specs=[pl.B...]
    pallas_call x1 -> x2, Pallas kernels: 4.38 us -> 4.65 us  [remap(): pl.pallas_call(functools.partial(remap_kernel, links, rows, cols, numbers...]
  transfers between devices with their start and end apart: 5 -> 5, of which waited for: 1 -> 1; matrix products, arithmetic and copies ran while one was open for 0% -> 0% of each run, Pallas kernels for 28% -> 33%
where the time goes in v4:
time: 32.8 us; the launch traced here: 32.7 us
  Pallas kernels  24.3 us (74%)
  starting transfers between devices  7.75 us (24%)
  waiting for transfers between devices  0.52 us (2%)
    pallas_call x1, Pallas kernels, step(): pl.pallas_call(functools.partial(main_kernel, chunk_rows), in_specs=[pl.B...  8.17 us
    pallas_call x1, Pallas kernels, interior(): pl.pallas_call(interior_kernel, in_specs=[vmem] * 2 + [hbm] * 2, out_spec...  6.13 us
    pallas_call x1, Pallas kernels, load(): pl.pallas_call(functools.partial(load_kernel, links), in_specs=[hbm] * 6,...  5.34 us
    pallas_call x2, Pallas kernels, remap(): pl.pallas_call(functools.partial(remap_kernel, links, rows, cols, numbers...  4.65 us
    ppermute x1, starting transfers between devices, local(): from_south = lax.ppermute(to_north, 'lat', ring('lat', 1))  2.64 us
    ppermute x1, starting transfers between devices, local(): from_north = lax.ppermute(to_south, 'lat', ring('lat', -1))  2.31 us
    ppermute x1, starting transfers between devices, local(): from_east = lax.ppermute(to_west, 'lon', ring('lon', -1))  2.3 us
  transfers between devices with their start and end apart: 5, of which 1 were waited for; matrix products, arithmetic and copies ran while one was open for 0% of the time, Pallas kernels for 33%

profile of v4, /device:TPU:0, one launch (start us, length us, event | category | flops | bytes accessed | tf_op | source)
XLA Modules:
  0.0 32.7 jit_solution(9244591893121921634)
XLA Ops:
  0.0 5.3 %load.1 = (f32[2,48,128,128]{3,2,1,0:T(8,128)S(1)}, f32[48,128,128]{2,1,0:T(8,128)S(1)}, f32[6,128,128]{2,1,0:T(8,128)S(1)}, f32[432,128]{1,0:T(8,128)S(1)}, f32...) custom-call(f32[2,48,128,128]{3,2,1,0:T(8,128)} %tracers.1, ...), custom_call_target="tpu_custom_call" | custom-call | tf_op jit(solution)/shard_map/load/pallas_call | solution.py:178
  5.4 0.5 %collective-permute-start = (f32[432,128]{1,0:T(8,128)S(1)}, f32[432,128]{1,0:T(8,128)S(1)}, u32[]{:S(2)}, u32[]{:S(2)}) collective-permute-start(f32[432,128]{1,0:T(8,128)S(1)} %get-tuple-element.22), channel_id=1, source_target_pairs={{0,1},{1,2},{2,3},{3,4},{4,5},{5,6},{6,7},{7,0},{8,9},{9,10},{10,1... | collective-permute-start | bytes 663560 | tf_op jit(solution)/shard_map/ppermute | solution.py:651
  5.9 2.6 %collective-permute-start.2 = (f32[416,128]{1,0:T(8,128)S(1)}, f32[416,128]{1,0:T(8,128)S(1)}, u32[]{:S(2)}, u32[]{:S(2)}) collective-permute-start(f32[416,128]{1,0:T(8,128)S(1)} %get-tuple-element.25), channel_id=1, source_target_pairs={{0,8},{8,16},{16,24},{24,0},{1,9},{9,17},{17,25},{25,1},{2,10},{10... | collective-permute-start | bytes 638984 | tf_op jit(solution)/shard_map/ppermute | solution.py:649
  8.5 2.3 %collective-permute-start.1 = (f32[256,128]{1,0:T(8,128)S(1)}, f32[256,128]{1,0:T(8,128)S(1)}, u32[]{:S(2)}, u32[]{:S(2)}) collective-permute-start(f32[256,128]{1,0:T(8,128)S(1)} %get-tuple-element.23), channel_id=1, source_target_pairs={{0,7},{1,0},{2,1},{3,2},{4,3},{5,4},{6,5},{7,6},{8,15},{9,8},{10,9... | collective-permute-start | bytes 393224 | tf_op jit(solution)/shard_map/ppermute | solution.py:652
  10.8 2.3 %collective-permute-start.3 = (f32[192,128]{1,0:T(8,128)S(1)}, f32[192,128]{1,0:T(8,128)S(1)}, u32[]{:S(2)}, u32[]{:S(2)}) collective-permute-start(f32[192,128]{1,0:T(8,128)S(1)} %get-tuple-element.26), channel_id=1, source_target_pairs={{0,24},{8,0},{16,8},{24,16},{1,25},{9,1},{17,9},{25,17},{2,26},{10... | collective-permute-start | bytes 294920 | tf_op jit(solution)/shard_map/ppermute | solution.py:650
  13.1 0.0 collective-permute-start.4
  13.1 0.0 copy-start
  13.1 0.0 copy-start.1
  13.1 0.0 copy-start.2
  13.1 6.1 %interior.1 = (f32[2,48,128,128]{3,2,1,0:T(8,128)S(1)}, f32[48,128,128]{2,1,0:T(8,128)S(1)}) custom-call(f32[2,48,128,128]{3,2,1,0:T(8,128)S(1)} %get-tuple-element.17.cells, f32[48,128,128]{2,1,0:T(8,128)S(1)} %get-tuple-element.18.east, f32[48,128,128]{2,1,0:T(8,128)} %north_courant.3, f32[48,128,128]{2,1,0:T(8,128)} %diffusivity.1), custom_call_target="tpu_custom_call" | custom-call | tf_op jit(solution)/shard_map/interior/pallas_call | solution.py:275
  19.3 0.0 collective-permute-done.refs_1_.from_west
  19.3 0.0 copy-done
  19.3 2.3 %remap.2.refs_2_.upper = f32[2,160,256]{2,1,0:T(8,128)S(1)} custom-call(s32[4,6144]{1,0:T(4,128)S(1)} %bitcast.3, f32[176,128]{1,0:T(8,128)S(1)} %get-tuple-element.27.refs_0_, f32[432,128]{1,0:T(8,128)S(1)} %collective-permute-done.refs_1_.from_west), custom_call_target="tpu_custom_call" | custom-call | tf_op jit(solution)/shard_map/remap/pallas_call | solution.py:358
  21.6 0.5 %collective-permute-done.4.refs_1_ = f32[176,128]{1,0:T(8,128)S(1)} collective-permute-done((f32[176,128]{1,0:T(8,128)S(1)}, f32[176,128]{1,0:T(8,128)S(1)}, u32[]{:S(2)}, u32[]{:S(2)}) %collective-permute-start.4) | collective-permute-done | bytes 90144 | tf_op jit(solution)/shard_map/ppermute | solution.py:648
  22.1 0.0 collective-permute-done.2.refs_0_.from_south
  22.1 2.3 %remap.3.lower = f32[2,160,256]{2,1,0:T(8,128)S(1)} custom-call(s32[4,6144]{1,0:T(4,128)S(1)} %bitcast.4, f32[416,128]{1,0:T(8,128)S(1)} %collective-permute-done.2.refs_0_.from_south, f32[176,128]{1,0:T(8,128)S(1)} %collective-permute-done.4.refs_1_, f32[2,160,256]{2,1,0:T(8,128)S(1)} %remap.2.refs_2_.upper), custom_call_target="tpu_custom_call" | custom-call | tf_op jit(solution)/shard_map/remap/pallas_call | solution.py:358
  24.4 0.0 collective-permute-done.3.from_north
  24.5 0.0 collective-permute-done.1.from_east
  24.5 0.0 copy-done.1
  24.5 0.0 copy-done.2
  24.5 8.2 %step.1 = f32[2,48,128,128]{3,2,1,0:T(8,128)} custom-call(f32[2,48]{1,0:T(2,128)S(1)} %copy-done.2, f32[2,48,128,128]{3,2,1,0:T(8,128)S(1)} %get-tuple-element.17.cells, f32[2,48,128,128]{3,2,1,0:T(8,128)S(1)} %get-tuple-element.19.advected, f32[48,128,128]{2,1,0:T(8,128)S(1)} %get-tuple-element.20.diff, s32[128,128]{1,0:T(8,128)S(1)} %copy-done.1, ...), custom_call_target="tpu_custom_call" | custom-call | tf_op jit(solution)/shard_map/step/pallas_call | solution.py:601
Async XLA Ops:
  5.4 13.9 %collective-permute-start = (f32[432,128]{1,0:T(8,128)S(1)}, f32[432,128]{1,0:T(8,128)S(1)}, u32[]{:S(2)}, u32[]{:S(2)}) collective-permute-start(f32[432,128]{1,0:T(8,128)S(1)} %get-tuple-element.22), channel_id=1, source_target_pairs={{0,1},{1,2},{2,3},{3,4},{4,5},{5,6},{6,7},{7,0},{8,9},{9,10},{10,1... | collective-permute-start | bytes 663560 | tf_op jit(solution)/shard_map/ppermute | solution.py:651
  5.9 16.3 %collective-permute-start.2 = (f32[416,128]{1,0:T(8,128)S(1)}, f32[416,128]{1,0:T(8,128)S(1)}, u32[]{:S(2)}, u32[]{:S(2)}) collective-permute-start(f32[416,128]{1,0:T(8,128)S(1)} %get-tuple-element.25), channel_id=1, source_target_pairs={{0,8},{8,16},{16,24},{24,0},{1,9},{9,17},{17,25},{25,1},{2,10},{10... | collective-permute-start | bytes 638984 | tf_op jit(solution)/shard_map/ppermute | solution.py:649
  8.5 16.0 %collective-permute-start.1 = (f32[256,128]{1,0:T(8,128)S(1)}, f32[256,128]{1,0:T(8,128)S(1)}, u32[]{:S(2)}, u32[]{:S(2)}) collective-permute-start(f32[256,128]{1,0:T(8,128)S(1)} %get-tuple-element.23), channel_id=1, source_target_pairs={{0,7},{1,0},{2,1},{3,2},{4,3},{5,4},{6,5},{7,6},{8,15},{9,8},{10,9... | collective-permute-start | bytes 393224 | tf_op jit(solution)/shard_map/ppermute | solution.py:652
  10.8 13.7 %collective-permute-start.3 = (f32[192,128]{1,0:T(8,128)S(1)}, f32[192,128]{1,0:T(8,128)S(1)}, u32[]{:S(2)}, u32[]{:S(2)}) collective-permute-start(f32[192,128]{1,0:T(8,128)S(1)} %get-tuple-element.26), channel_id=1, source_target_pairs={{0,24},{8,0},{16,8},{24,16},{1,25},{9,1},{17,9},{25,17},{2,26},{10... | collective-permute-start | bytes 294920 | tf_op jit(solution)/shard_map/ppermute | solution.py:650
  13.1 9.0 %collective-permute-start.4 = (f32[176,128]{1,0:T(8,128)S(1)}, f32[176,128]{1,0:T(8,128)S(1)}, u32[]{:S(2)}, u32[]{:S(2)}) collective-permute-start(f32[176,128]{1,0:T(8,128)S(1)} %get-tuple-element.28), channel_id=1, source_target_pairs={{0,9},{1,10},{2,11},{3,12},{4,13},{5,14},{6,15},{7,8},{8,17},{9,18... | collective-permute-start | bytes 270344 | tf_op jit(solution)/shard_map/ppermute | solution.py:648
  13.1 6.2 %copy-start = (s32[1,4,6144]{2,1,0:T(4,128)S(1)}, s32[1,4,6144]{2,1,0:T(4,128)}, u32[]{:S(2)}) copy-start(s32[1,4,6144]{2,1,0:T(4,128)} %param.18) | copy-start | bytes 294916
  13.1 11.4 %copy-start.1 = (s32[128,128]{1,0:T(8,128)S(1)}, s32[128,128]{1,0:T(8,128)}, u32[]{:S(2)}) copy-start(s32[128,128]{1,0:T(8,128)} %land.1) | copy-start | bytes 196612
  13.1 11.4 %copy-start.2 = (f32[2,48]{1,0:T(2,128)S(1)}, f32[2,48]{1,0:T(2,128)}, u32[]{:S(2)}) copy-start(f32[2,48]{1,0:T(2,128)} %constant.2.clone.tables) | copy-start | bytes 1156

commit v5 on v4

--- a/solution.py
+++ b/solution.py
@@ -15,9 +15,9 @@
 TABLE_ROWS = 16
 PARTS = 4
 PACK = 16
-LEVELS = 6
-FORWARD = 4
-BACKWARD = 4
+LEVELS = 12
+FORWARD = 16
+BACKWARD = 12
 
 
 def lane_of(shape):
@@ -466,7 +466,7 @@
                 fix[t, side, at, :] = change * (-1.0 / 12.0)
             return carry
 
-        lax.fori_loop(0, rows // SUB, mend, 0, unroll=4)
+        lax.fori_loop(0, rows // SUB, mend, 0, unroll=8)
 
     def plane(msg, p):
         return msg[p * levels : (p + 1) * levels, :]

time: 32.8 us -> 32 us (0.976)
  Pallas kernels: 24.3 us -> 22.9 us
    pallas_call x1, Pallas kernels: 8.17 us -> 7.14 us  [step(): pl.pallas_call(functools.partial(main_kernel, chunk_rows), in_specs=[pl.B...]
    pallas_call x1, Pallas kernels: 6.13 us -> 5.8 us  [interior(): pl.pallas_call(interior_kernel, in_specs=[vmem] * 2 + [hbm] * 2, out_spec...]
    ppermute x1, waiting for transfers between devices: 0.5 us -> 0.83 us  [local(): from_corner = lax.ppermute(corner, ('lat', 'lon'), diagonal())]
where the time goes in v5:
time: 32 us; the launch traced here: 31.8 us
  Pallas kernels  22.9 us (72%)
  starting transfers between devices  7.75 us (24%)
  waiting for transfers between devices  0.84 us (3%)
    pallas_call x1, Pallas kernels, step(): pl.pallas_call(functools.partial(main_kernel, chunk_rows), in_specs=[pl.B...  7.14 us
    pallas_call x1, Pallas kernels, interior(): pl.pallas_call(interior_kernel, in_specs=[vmem] * 2 + [hbm] * 2, out_spec...  5.8 us
    pallas_call x1, Pallas kernels, load(): pl.pallas_call(functools.partial(load_kernel, links), in_specs=[hbm] * 6,...  5.34 us
    pallas_call x2, Pallas kernels, remap(): pl.pallas_call(functools.partial(remap_kernel, links, rows, cols, numbers...  4.65 us
    ppermute x1, starting transfers between devices, local(): from_south = lax.ppermute(to_north, 'lat', ring('lat', 1))  2.64 us
    ppermute x1, starting transfers between devices, local(): from_north = lax.ppermute(to_south, 'lat', ring('lat', -1))  2.31 us
    ppermute x1, starting transfers between devices, local(): from_east = lax.ppermute(to_west, 'lon', ring('lon', -1))  2.3 us
    ppermute x1, waiting for transfers between devices, local(): from_corner = lax.ppermute(corner, ('lat', 'lon'), diagonal())  0.83 us
  transfers between devices with their start and end apart: 5, of which 1 were waited for; matrix products, arithmetic and copies ran while one was open for 0% of the time, Pallas kernels for 33%

profile of v5, /device:TPU:0, one launch (start us, length us, event | category | flops | bytes accessed | tf_op | source)
XLA Modules:
  0.0 31.8 jit_solution(10393705436169127335)
XLA Ops:
  0.0 5.3 %load.1 = (f32[2,48,128,128]{3,2,1,0:T(8,128)S(1)}, f32[48,128,128]{2,1,0:T(8,128)S(1)}, f32[6,128,128]{2,1,0:T(8,128)S(1)}, f32[432,128]{1,0:T(8,128)S(1)}, f32...) custom-call(f32[2,48,128,128]{3,2,1,0:T(8,128)} %tracers.1, ...), custom_call_target="tpu_custom_call" | custom-call | tf_op jit(solution)/shard_map/load/pallas_call | solution.py:178
  5.4 0.5 %collective-permute-start = (f32[432,128]{1,0:T(8,128)S(1)}, f32[432,128]{1,0:T(8,128)S(1)}, u32[]{:S(2)}, u32[]{:S(2)}) collective-permute-start(f32[432,128]{1,0:T(8,128)S(1)} %get-tuple-element.22), channel_id=1, source_target_pairs={{0,1},{1,2},{2,3},{3,4},{4,5},{5,6},{6,7},{7,0},{8,9},{9,10},{10,1... | collective-permute-start | bytes 663560 | tf_op jit(solution)/shard_map/ppermute | solution.py:651
  5.9 2.6 %collective-permute-start.2 = (f32[416,128]{1,0:T(8,128)S(1)}, f32[416,128]{1,0:T(8,128)S(1)}, u32[]{:S(2)}, u32[]{:S(2)}) collective-permute-start(f32[416,128]{1,0:T(8,128)S(1)} %get-tuple-element.25), channel_id=1, source_target_pairs={{0,8},{8,16},{16,24},{24,0},{1,9},{9,17},{17,25},{25,1},{2,10},{10... | collective-permute-start | bytes 638984 | tf_op jit(solution)/shard_map/ppermute | solution.py:649
  8.5 2.3 %collective-permute-start.1 = (f32[256,128]{1,0:T(8,128)S(1)}, f32[256,128]{1,0:T(8,128)S(1)}, u32[]{:S(2)}, u32[]{:S(2)}) collective-permute-start(f32[256,128]{1,0:T(8,128)S(1)} %get-tuple-element.23), channel_id=1, source_target_pairs={{0,7},{1,0},{2,1},{3,2},{4,3},{5,4},{6,5},{7,6},{8,15},{9,8},{10,9... | collective-permute-start | bytes 393224 | tf_op jit(solution)/shard_map/ppermute | solution.py:652
  10.8 2.3 %collective-permute-start.3 = (f32[192,128]{1,0:T(8,128)S(1)}, f32[192,128]{1,0:T(8,128)S(1)}, u32[]{:S(2)}, u32[]{:S(2)}) collective-permute-start(f32[192,128]{1,0:T(8,128)S(1)} %get-tuple-element.26), channel_id=1, source_target_pairs={{0,24},{8,0},{16,8},{24,16},{1,25},{9,1},{17,9},{25,17},{2,26},{10... | collective-permute-start | bytes 294920 | tf_op jit(solution)/shard_map/ppermute | solution.py:650
  13.1 0.0 collective-permute-start.4
  13.1 0.0 copy-start
  13.1 0.0 copy-start.1
  13.1 0.0 copy-start.2
  13.1 5.8 %interior.1 = (f32[2,48,128,128]{3,2,1,0:T(8,128)S(1)}, f32[48,128,128]{2,1,0:T(8,128)S(1)}) custom-call(f32[2,48,128,128]{3,2,1,0:T(8,128)S(1)} %get-tuple-element.17.cells, f32[48,128,128]{2,1,0:T(8,128)S(1)} %get-tuple-element.18.east, f32[48,128,128]{2,1,0:T(8,128)} %north_courant.3, f32[48,128,128]{2,1,0:T(8,128)} %diffusivity.1), custom_call_target="tpu_custom_call" | custom-call | tf_op jit(solution)/shard_map/interior/pallas_call | solution.py:275
  18.9 0.0 collective-permute-done.refs_1_.from_west
  18.9 0.0 copy-done
  18.9 2.3 %remap.2.refs_2_.upper = f32[2,160,256]{2,1,0:T(8,128)S(1)} custom-call(s32[4,6144]{1,0:T(4,128)S(1)} %bitcast.3, f32[176,128]{1,0:T(8,128)S(1)} %get-tuple-element.27.refs_0_, f32[432,128]{1,0:T(8,128)S(1)} %collective-permute-done.refs_1_.from_west), custom_call_target="tpu_custom_call" | custom-call | tf_op jit(solution)/shard_map/remap/pallas_call | solution.py:358
  21.3 0.8 %collective-permute-done.4.refs_1_ = f32[176,128]{1,0:T(8,128)S(1)} collective-permute-done((f32[176,128]{1,0:T(8,128)S(1)}, f32[176,128]{1,0:T(8,128)S(1)}, u32[]{:S(2)}, u32[]{:S(2)}) %collective-permute-start.4) | collective-permute-done | bytes 90144 | tf_op jit(solution)/shard_map/ppermute | solution.py:648
  22.1 0.0 collective-permute-done.2.refs_0_.from_south
  22.1 2.3 %remap.3.lower = f32[2,160,256]{2,1,0:T(8,128)S(1)} custom-call(s32[4,6144]{1,0:T(4,128)S(1)} %bitcast.4, f32[416,128]{1,0:T(8,128)S(1)} %collective-permute-done.2.refs_0_.from_south, f32[176,128]{1,0:T(8,128)S(1)} %collective-permute-done.4.refs_1_, f32[2,160,256]{2,1,0:T(8,128)S(1)} %remap.2.refs_2_.upper), custom_call_target="tpu_custom_call" | custom-call | tf_op jit(solution)/shard_map/remap/pallas_call | solution.py:358
  24.4 0.0 collective-permute-done.3.from_north
  24.5 0.0 collective-permute-done.1.from_east
  24.5 0.0 copy-done.1
  24.5 0.0 copy-done.2
  24.5 7.1 %step.1 = f32[2,48,128,128]{3,2,1,0:T(8,128)} custom-call(f32[2,48]{1,0:T(2,128)S(1)} %copy-done.2, f32[2,48,128,128]{3,2,1,0:T(8,128)S(1)} %get-tuple-element.17.cells, f32[2,48,128,128]{3,2,1,0:T(8,128)S(1)} %get-tuple-element.19.advected, f32[48,128,128]{2,1,0:T(8,128)S(1)} %get-tuple-element.20.diff, s32[128,128]{1,0:T(8,128)S(1)} %copy-done.1, ...), custom_call_target="tpu_custom_call" | custom-call | tf_op jit(solution)/shard_map/step/pallas_call | solution.py:601
Async XLA Ops:
  5.4 13.6 %collective-permute-start = (f32[432,128]{1,0:T(8,128)S(1)}, f32[432,128]{1,0:T(8,128)S(1)}, u32[]{:S(2)}, u32[]{:S(2)}) collective-permute-start(f32[432,128]{1,0:T(8,128)S(1)} %get-tuple-element.22), channel_id=1, source_target_pairs={{0,1},{1,2},{2,3},{3,4},{4,5},{5,6},{6,7},{7,0},{8,9},{9,10},{10,1... | collective-permute-start | bytes 663560 | tf_op jit(solution)/shard_map/ppermute | solution.py:651
  5.9 16.3 %collective-permute-start.2 = (f32[416,128]{1,0:T(8,128)S(1)}, f32[416,128]{1,0:T(8,128)S(1)}, u32[]{:S(2)}, u32[]{:S(2)}) collective-permute-start(f32[416,128]{1,0:T(8,128)S(1)} %get-tuple-element.25), channel_id=1, source_target_pairs={{0,8},{8,16},{16,24},{24,0},{1,9},{9,17},{17,25},{25,1},{2,10},{10... | collective-permute-start | bytes 638984 | tf_op jit(solution)/shard_map/ppermute | solution.py:649
  8.5 16.0 %collective-permute-start.1 = (f32[256,128]{1,0:T(8,128)S(1)}, f32[256,128]{1,0:T(8,128)S(1)}, u32[]{:S(2)}, u32[]{:S(2)}) collective-permute-start(f32[256,128]{1,0:T(8,128)S(1)} %get-tuple-element.23), channel_id=1, source_target_pairs={{0,7},{1,0},{2,1},{3,2},{4,3},{5,4},{6,5},{7,6},{8,15},{9,8},{10,9... | collective-permute-start | bytes 393224 | tf_op jit(solution)/shard_map/ppermute | solution.py:652
  10.8 13.7 %collective-permute-start.3 = (f32[192,128]{1,0:T(8,128)S(1)}, f32[192,128]{1,0:T(8,128)S(1)}, u32[]{:S(2)}, u32[]{:S(2)}) collective-permute-start(f32[192,128]{1,0:T(8,128)S(1)} %get-tuple-element.26), channel_id=1, source_target_pairs={{0,24},{8,0},{16,8},{24,16},{1,25},{9,1},{17,9},{25,17},{2,26},{10... | collective-permute-start | bytes 294920 | tf_op jit(solution)/shard_map/ppermute | solution.py:650
  13.1 9.0 %collective-permute-start.4 = (f32[176,128]{1,0:T(8,128)S(1)}, f32[176,128]{1,0:T(8,128)S(1)}, u32[]{:S(2)}, u32[]{:S(2)}) collective-permute-start(f32[176,128]{1,0:T(8,128)S(1)} %get-tuple-element.28), channel_id=1, source_target_pairs={{0,9},{1,10},{2,11},{3,12},{4,13},{5,14},{6,15},{7,8},{8,17},{9,18... | collective-permute-start | bytes 270344 | tf_op jit(solution)/shard_map/ppermute | solution.py:648
  13.1 5.8 %copy-start = (s32[1,4,6144]{2,1,0:T(4,128)S(1)}, s32[1,4,6144]{2,1,0:T(4,128)}, u32[]{:S(2)}) copy-start(s32[1,4,6144]{2,1,0:T(4,128)} %param.18) | copy-start | bytes 294916
  13.1 11.4 %copy-start.1 = (s32[128,128]{1,0:T(8,128)S(1)}, s32[128,128]{1,0:T(8,128)}, u32[]{:S(2)}) copy-start(s32[128,128]{1,0:T(8,128)} %land.1) | copy-start | bytes 196612
  13.1 11.4 %copy-start.2 = (f32[2,48]{1,0:T(2,128)S(1)}, f32[2,48]{1,0:T(2,128)}, u32[]{:S(2)}) copy-start(f32[2,48]{1,0:T(2,128)} %constant.2.clone.tables) | copy-start | bytes 1156

commit v6 on v5

--- a/solution.py
+++ b/solution.py
@@ -366,67 +366,9 @@
     )(target, *[msg for _, msg, _ in blocks], *after)
 
 
-def main_kernel(
-    chunk_rows,
-    tables,
-    cells,
-    advected,
-    diff,
-    land,
-    own,
-    from_west,
-    from_east,
-    own_rows,
-    from_south,
-    from_north,
-    upper,
-    lower,
-    out,
-    values,
-    gains,
-    surface,
-    fix,
-    row_fix,
-    out_sem,
-):
-    _, levels, rows, cols = cells.shape
-    chunks = rows // chunk_rows
+def column_kernel(levels, own, from_west, from_east, fix):
+    _, rows, _ = own.shape
     lane = lane_of((SUB, LANES))
-
-    def store(c, q):
-        part = pl.ds(c * chunk_rows, chunk_rows)
-        at = pl.ds(q * (levels // PARTS), levels // PARTS)
-        return pltpu.make_async_copy(
-            values.at[:, at, part, :], out.at[:, at, part, :], out_sem.at[c, q]
-        )
-
-    quads = [upper[0], upper[1], lower[0], lower[1]]
-    short = rows // 8
-    for pair in range(2):
-        left = quads[2 * pair + 1]
-        right = quads[2 * pair]
-        for f in range(5):
-            at = 2 * f * short
-            one = left[at : at + short] + left[at + short : at + 2 * short]
-            two = right[at : at + short] + right[at + short : at + 2 * short]
-            for g in range(4):
-                half = slice(g // 2 * LANES, g // 2 * LANES + LANES)
-                a = one[:, half]
-                b = two[:, half]
-                if g % 2:
-                    a = pltpu.roll(a, LANES // 2, 1)
-                else:
-                    b = pltpu.roll(b, LANES // 2, 1)
-                merged = jnp.where(lane_of((short, LANES)) < LANES // 2, a, b)
-                base = (1 - pair) * (rows // 2) + g * short
-                surface[f, base : base + short, :] = merged
-    for rb in range(rows // SUB):
-        at = pl.ds(rb * SUB, SUB)
-        s3 = surface[3, at, :]
-        s4 = surface[4, at, :]
-        surface[3, at, :] = 2.0 * jnp.sqrt(s3 * s3 + s4 * s4)
-
-    half = levels // 2
     place_in_group = lane % 4
     spread = (2 * levels + lane // 4) % LANES
     for side in range(2):
@@ -468,6 +410,79 @@
 
         lax.fori_loop(0, rows // SUB, mend, 0, unroll=8)
 
+
+def column_fix(levels, own, from_west, from_east):
+    _, rows, cols = own.shape
+    vmem = pl.BlockSpec(memory_space=pltpu.VMEM)
+    return pl.pallas_call(
+        functools.partial(column_kernel, levels),
+        in_specs=[vmem] * 3,
+        out_specs=vmem,
+        out_shape=pltpu.VMEM((2, 2, rows, cols), F32),
+        compiler_params=pltpu.CompilerParams(vmem_limit_bytes=16 << 20),
+        name="column_fix",
+    )(own, from_west, from_east)
+
+
+def main_kernel(
+    chunk_rows,
+    tables,
+    cells,
+    advected,
+    diff,
+    land,
+    fix,
+    own_rows,
+    from_south,
+    from_north,
+    upper,
+    lower,
+    out,
+    values,
+    gains,
+    surface,
+    row_fix,
+    out_sem,
+):
+    _, levels, rows, cols = cells.shape
+    chunks = rows // chunk_rows
+    lane = lane_of((SUB, LANES))
+
+    def store(c, q):
+        part = pl.ds(c * chunk_rows, chunk_rows)
+        at = pl.ds(q * (levels // PARTS), levels // PARTS)
+        return pltpu.make_async_copy(
+            values.at[:, at, part, :], out.at[:, at, part, :], out_sem.at[c, q]
+        )
+
+    quads = [upper[0], upper[1], lower[0], lower[1]]
+    short = rows // 8
+    for pair in range(2):
+        left = quads[2 * pair + 1]
+        right = quads[2 * pair]
+        for f in range(5):
+            at = 2 * f * short
+            one = left[at : at + short] + left[at + short : at + 2 * short]
+            two = right[at : at + short] + right[at + short : at + 2 * short]
+            for g in range(4):
+                half = slice(g // 2 * LANES, g // 2 * LANES + LANES)
+                a = one[:, half]
+                b = two[:, half]
+                if g % 2:
+                    a = pltpu.roll(a, LANES // 2, 1)
+                else:
+                    b = pltpu.roll(b, LANES // 2, 1)
+                merged = jnp.where(lane_of((short, LANES)) < LANES // 2, a, b)
+                base = (1 - pair) * (rows // 2) + g * short
+                surface[f, base : base + short, :] = merged
+    for rb in range(rows // SUB):
+        at = pl.ds(rb * SUB, SUB)
+        s3 = surface[3, at, :]
+        s4 = surface[4, at, :]
+        surface[3, at, :] = 2.0 * jnp.sqrt(s3 * s3 + s4 * s4)
+
+    half = levels // 2
+
     def plane(msg, p):
         return msg[p * levels : (p + 1) * levels, :]
 
@@ -607,7 +622,6 @@
             pltpu.VMEM((2, levels, rows, cols), F32),
             pltpu.VMEM((levels, chunk_rows, cols), F32),
             pltpu.VMEM((5, rows, cols), F32),
-            pltpu.VMEM((2, 2, rows, cols), F32),
             pltpu.VMEM((2, 4, levels, cols), F32),
             pltpu.SemaphoreType.DMA((chunks, PARTS)),
         ],
@@ -652,8 +666,9 @@
     from_east = lax.ppermute(to_west, "lon", ring("lon", -1))
     advected, diff = interior(cells, east, north_courant, diffusivity)
     upper = remap(target, [(0, own_links, 0), (1, from_west, 2 * rows)], rows, cols)
-    lower = remap(target, [(2, from_south, 5 * levels), (3, from_corner, 0)], rows, cols, [upper])
-    messages = (own, from_west, from_east, own_rows, from_south, from_north, upper, lower)
+    fix = column_fix(levels, own, from_west, from_east)
+    lower = remap(target, [(2, from_south, 5 * levels), (3, from_corner, 0)], rows, cols, [upper, fix])
+    messages = (fix, own_rows, from_south, from_north, upper, lower)
     return step(cells, advected, diff, land_sea, messages)
 
 

time: 32 us -> 31.1 us (0.972)
  waiting for transfers between devices: 0.84 us -> 0.01 us
    pallas_call x0 -> x1, Pallas kernels: none -> 1.13 us  [column_fix(): pl.pallas_call(functools.partial(column_kernel, levels), in_specs=[vmem]...]
    pallas_call x1, Pallas kernels: 7.14 us -> 6.03 us  [step(): pl.pallas_call(functools.partial(main_kernel, chunk_rows), in_specs=[pl.B...]
    ppermute x1, waiting for transfers between devices: 0.83 us -> 0.01 us  [local(): from_corner = lax.ppermute(corner, ('lat', 'lon'), diagonal())]
  transfers between devices with their start and end apart: 5 -> 5, of which waited for: 1 -> 0; matrix products, arithmetic and copies ran while one was open for 0% -> 0% of each run, Pallas kernels for 33% -> 37%
where the time goes in v6:
time: 31.1 us; the launch traced here: 31 us
  Pallas kernels  23 us (74%)
  starting transfers between devices  7.75 us (25%)
    pallas_call x1, Pallas kernels, step(): pl.pallas_call(functools.partial(main_kernel, chunk_rows), in_specs=[pl.B...  6.03 us
    pallas_call x1, Pallas kernels, interior(): pl.pallas_call(interior_kernel, in_specs=[vmem] * 2 + [hbm] * 2, out_spec...  5.8 us
    pallas_call x1, Pallas kernels, load(): pl.pallas_call(functools.partial(load_kernel, links), in_specs=[hbm] * 6,...  5.34 us
    pallas_call x2, Pallas kernels, remap(): pl.pallas_call(functools.partial(remap_kernel, links, rows, cols, numbers...  4.66 us
    ppermute x1, starting transfers between devices, local(): from_south = lax.ppermute(to_north, 'lat', ring('lat', 1))  2.64 us
    ppermute x1, starting transfers between devices, local(): from_north = lax.ppermute(to_south, 'lat', ring('lat', -1))  2.31 us
    ppermute x1, starting transfers between devices, local(): from_east = lax.ppermute(to_west, 'lon', ring('lon', -1))  2.3 us
    pallas_call x1, Pallas kernels, column_fix(): pl.pallas_call(functools.partial(column_kernel, levels), in_specs=[vmem]...  1.13 us
  transfers between devices with their start and end apart: 5, of which 0 were waited for; matrix products, arithmetic and copies ran while one was open for 0% of the time, Pallas kernels for 37%

profile of v6, /device:TPU:0, one launch (start us, length us, event | category | flops | bytes accessed | tf_op | source)
XLA Modules:
  0.0 31.0 jit_solution(17597839206048229664)
XLA Ops:
  0.0 5.3 %load.1 = (f32[2,48,128,128]{3,2,1,0:T(8,128)S(1)}, f32[48,128,128]{2,1,0:T(8,128)S(1)}, f32[6,128,128]{2,1,0:T(8,128)S(1)}, f32[432,128]{1,0:T(8,128)S(1)}, f32...) custom-call(f32[2,48,128,128]{3,2,1,0:T(8,128)} %tracers.1, ...), custom_call_target="tpu_custom_call" | custom-call | tf_op jit(solution)/shard_map/load/pallas_call | solution.py:178
  5.4 0.5 %collective-permute-start = (f32[432,128]{1,0:T(8,128)S(1)}, f32[432,128]{1,0:T(8,128)S(1)}, u32[]{:S(2)}, u32[]{:S(2)}) collective-permute-start(f32[432,128]{1,0:T(8,128)S(1)} %get-tuple-element.22), channel_id=1, source_target_pairs={{0,1},{1,2},{2,3},{3,4},{4,5},{5,6},{6,7},{7,0},{8,9},{9,10},{10,1... | collective-permute-start | bytes 663560 | tf_op jit(solution)/shard_map/ppermute | solution.py:665
  5.9 2.6 %collective-permute-start.2 = (f32[416,128]{1,0:T(8,128)S(1)}, f32[416,128]{1,0:T(8,128)S(1)}, u32[]{:S(2)}, u32[]{:S(2)}) collective-permute-start(f32[416,128]{1,0:T(8,128)S(1)} %get-tuple-element.25), channel_id=1, source_target_pairs={{0,8},{8,16},{16,24},{24,0},{1,9},{9,17},{17,25},{25,1},{2,10},{10... | collective-permute-start | bytes 638984 | tf_op jit(solution)/shard_map/ppermute | solution.py:663
  8.5 2.3 %collective-permute-start.1 = (f32[256,128]{1,0:T(8,128)S(1)}, f32[256,128]{1,0:T(8,128)S(1)}, u32[]{:S(2)}, u32[]{:S(2)}) collective-permute-start(f32[256,128]{1,0:T(8,128)S(1)} %get-tuple-element.23), channel_id=1, source_target_pairs={{0,7},{1,0},{2,1},{3,2},{4,3},{5,4},{6,5},{7,6},{8,15},{9,8},{10,9... | collective-permute-start | bytes 393224 | tf_op jit(solution)/shard_map/ppermute | solution.py:666
  10.8 2.3 %collective-permute-start.3 = (f32[192,128]{1,0:T(8,128)S(1)}, f32[192,128]{1,0:T(8,128)S(1)}, u32[]{:S(2)}, u32[]{:S(2)}) collective-permute-start(f32[192,128]{1,0:T(8,128)S(1)} %get-tuple-element.26), channel_id=1, source_target_pairs={{0,24},{8,0},{16,8},{24,16},{1,25},{9,1},{17,9},{25,17},{2,26},{10... | collective-permute-start | bytes 294920 | tf_op jit(solution)/shard_map/ppermute | solution.py:664
  13.1 0.0 collective-permute-start.4
  13.1 0.0 copy-start
  13.1 0.0 copy-start.1
  13.1 0.0 copy-start.2
  13.1 5.8 %interior.1 = (f32[2,48,128,128]{3,2,1,0:T(8,128)S(1)}, f32[48,128,128]{2,1,0:T(8,128)S(1)}) custom-call(f32[2,48,128,128]{3,2,1,0:T(8,128)S(1)} %get-tuple-element.17.cells, f32[48,128,128]{2,1,0:T(8,128)S(1)} %get-tuple-element.18.east, f32[48,128,128]{2,1,0:T(8,128)} %north_courant.3, f32[48,128,128]{2,1,0:T(8,128)} %diffusivity.1), custom_call_target="tpu_custom_call" | custom-call | tf_op jit(solution)/shard_map/interior/pallas_call | solution.py:275
  18.9 0.0 collective-permute-done.1.from_east
  18.9 0.0 collective-permute-done.from_west.refs_1_
  18.9 1.1 %column_fix.1.refs_3_.fix = f32[2,2,128,128]{3,2,1,0:T(8,128)S(1)} custom-call(f32[6,128,128]{2,1,0:T(8,128)S(1)} %get-tuple-element.21.own, f32[432,128]{1,0:T(8,128)S(1)} %collective-permute-done.from_west.refs_1_, f32[256,128]{1,0:T(8,128)S(1)} %collective-permute-done.1.from_east), custom_call_target="tpu_custom_call" | custom-call | tf_op jit(solution)/shard_map/column_fix/pallas_call | solution.py:417
  20.1 0.0 copy-done
  20.1 2.3 %remap.2.refs_2_.upper = f32[2,160,256]{2,1,0:T(8,128)S(1)} custom-call(s32[4,6144]{1,0:T(4,128)S(1)} %bitcast.3, f32[176,128]{1,0:T(8,128)S(1)} %get-tuple-element.27.refs_0_, f32[432,128]{1,0:T(8,128)S(1)} %collective-permute-done.from_west.refs_1_), custom_call_target="tpu_custom_call" | custom-call | tf_op jit(solution)/shard_map/remap/pallas_call | solution.py:358
  22.4 0.0 collective-permute-done.4.refs_1_
  22.4 0.0 collective-permute-done.2.refs_0_.from_south
  22.4 2.3 %remap.3.lower = f32[2,160,256]{2,1,0:T(8,128)S(1)} custom-call(s32[4,6144]{1,0:T(4,128)S(1)} %bitcast.4, f32[416,128]{1,0:T(8,128)S(1)} %collective-permute-done.2.refs_0_.from_south, f32[176,128]{1,0:T(8,128)S(1)} %collective-permute-done.4.refs_1_, f32[2,160,256]{2,1,0:T(8,128)S(1)} %remap.2.refs_2_.upper, f32[2,2,128,128]{3,2,1,0:T(8,128)S(1)} %column_fix.1.refs_3_.fix), custom_call_target="tpu_custom_call" | custom-call | tf_op jit(solution)/shard_map/remap/pallas_call | solution.py:358
  24.8 0.0 collective-permute-done.3.from_north
  24.8 0.0 copy-done.1
  24.8 0.0 copy-done.2
  24.8 6.0 %step.1 = f32[2,48,128,128]{3,2,1,0:T(8,128)} custom-call(f32[2,48]{1,0:T(2,128)S(1)} %copy-done.2, f32[2,48,128,128]{3,2,1,0:T(8,128)S(1)} %get-tuple-element.17.cells, f32[2,48,128,128]{3,2,1,0:T(8,128)S(1)} %get-tuple-element.19.advected, f32[48,128,128]{2,1,0:T(8,128)S(1)} %get-tuple-element.20.diff, s32[128,128]{1,0:T(8,128)S(1)} %copy-done.1, ...), custom_call_target="tpu_custom_call" | custom-call | tf_op jit(solution)/shard_map/step/pallas_call | solution.py:616
Async XLA Ops:
  5.4 13.6 %collective-permute-start = (f32[432,128]{1,0:T(8,128)S(1)}, f32[432,128]{1,0:T(8,128)S(1)}, u32[]{:S(2)}, u32[]{:S(2)}) collective-permute-start(f32[432,128]{1,0:T(8,128)S(1)} %get-tuple-element.22), channel_id=1, source_target_pairs={{0,1},{1,2},{2,3},{3,4},{4,5},{5,6},{6,7},{7,0},{8,9},{9,10},{10,1... | collective-permute-start | bytes 663560 | tf_op jit(solution)/shard_map/ppermute | solution.py:665
  5.9 16.6 %collective-permute-start.2 = (f32[416,128]{1,0:T(8,128)S(1)}, f32[416,128]{1,0:T(8,128)S(1)}, u32[]{:S(2)}, u32[]{:S(2)}) collective-permute-start(f32[416,128]{1,0:T(8,128)S(1)} %get-tuple-element.25), channel_id=1, source_target_pairs={{0,8},{8,16},{16,24},{24,0},{1,9},{9,17},{17,25},{25,1},{2,10},{10... | collective-permute-start | bytes 638984 | tf_op jit(solution)/shard_map/ppermute | solution.py:663
  8.5 10.4 %collective-permute-start.1 = (f32[256,128]{1,0:T(8,128)S(1)}, f32[256,128]{1,0:T(8,128)S(1)}, u32[]{:S(2)}, u32[]{:S(2)}) collective-permute-start(f32[256,128]{1,0:T(8,128)S(1)} %get-tuple-element.23), channel_id=1, source_target_pairs={{0,7},{1,0},{2,1},{3,2},{4,3},{5,4},{6,5},{7,6},{8,15},{9,8},{10,9... | collective-permute-start | bytes 393224 | tf_op jit(solution)/shard_map/ppermute | solution.py:666
  10.8 14.0 %collective-permute-start.3 = (f32[192,128]{1,0:T(8,128)S(1)}, f32[192,128]{1,0:T(8,128)S(1)}, u32[]{:S(2)}, u32[]{:S(2)}) collective-permute-start(f32[192,128]{1,0:T(8,128)S(1)} %get-tuple-element.26), channel_id=1, source_target_pairs={{0,24},{8,0},{16,8},{24,16},{1,25},{9,1},{17,9},{25,17},{2,26},{10... | collective-permute-start | bytes 294920 | tf_op jit(solution)/shard_map/ppermute | solution.py:664
  13.1 9.3 %collective-permute-start.4 = (f32[176,128]{1,0:T(8,128)S(1)}, f32[176,128]{1,0:T(8,128)S(1)}, u32[]{:S(2)}, u32[]{:S(2)}) collective-permute-start(f32[176,128]{1,0:T(8,128)S(1)} %get-tuple-element.28), channel_id=1, source_target_pairs={{0,9},{1,10},{2,11},{3,12},{4,13},{5,14},{6,15},{7,8},{8,17},{9,18... | collective-permute-start | bytes 270344 | tf_op jit(solution)/shard_map/ppermute | solution.py:662
  13.1 7.0 %copy-start = (s32[1,4,6144]{2,1,0:T(4,128)S(1)}, s32[1,4,6144]{2,1,0:T(4,128)}, u32[]{:S(2)}) copy-start(s32[1,4,6144]{2,1,0:T(4,128)} %param.18) | copy-start | bytes 294916
  13.1 11.7 %copy-start.1 = (s32[128,128]{1,0:T(8,128)S(1)}, s32[128,128]{1,0:T(8,128)}, u32[]{:S(2)}) copy-start(s32[128,128]{1,0:T(8,128)} %land.1) | copy-start | bytes 196612
  13.1 11.7 %copy-start.2 = (f32[2,48]{1,0:T(2,128)S(1)}, f32[2,48]{1,0:T(2,128)}, u32[]{:S(2)}) copy-start(f32[2,48]{1,0:T(2,128)} %constant.2.clone.tables) | copy-start | bytes 1156

commit v7 on v6

--- a/solution.py
+++ b/solution.py
@@ -150,7 +150,7 @@
             west_msg[place, :] = jnp.where(early, pltpu.roll(first, LANES - 2, 1), second)
         return carry
 
-    lax.fori_loop(0, rows // SUB, messages, 0, unroll=4)
+    lax.fori_loop(0, rows // SUB, messages, 0, unroll=8)
 
 
 def in_hbm(*arrays):
@@ -386,14 +386,18 @@
                 west = from_west[msg_at, :]
                 right = from_east[msg_at, :]
                 if side:
-                    west = pltpu.roll(west, LANES - 2, 1)
+                    west_one = pltpu.roll(west, LANES - 1, 1)
+                    west_two = west
+                    right_before = pltpu.roll(right, LANES - 1, 1)
                     right = pltpu.roll(right, LANES - 2, 1)
+                else:
+                    west_one = pltpu.roll(west, 1, 1)
+                    west_two = pltpu.roll(west, 2, 1)
+                    right_before = pltpu.roll(right, 1, 1)
                 inner = own[2 * t + side, at, :]
                 inner_next = pltpu.roll(inner, LANES - 1, 1)
-                west_one = pltpu.roll(west, 1, 1)
-                west_two = pltpu.roll(west, 2, 1)
                 product = courant * right
-                second = courant * (7.0 * pltpu.roll(right, 1, 1)) - product + pltpu.roll(product, 1, 1)
+                second = courant * (7.0 * right_before) - product + pltpu.roll(product, 1, 1)
                 third = (
                     courant_before * (7.0 * inner - inner_next)
                     - courant * west_one

time: 31.1 us -> 30.8 us (level)
  no operation moved by 1% of the time
where the time goes in v7:
time: 30.8 us; the launch traced here: 30.7 us
  Pallas kernels  22.7 us (74%)
  starting transfers between devices  7.75 us (25%)
    pallas_call x1, Pallas kernels, step(): pl.pallas_call(functools.partial(main_kernel, chunk_rows), in_specs=[pl.B...  6.03 us
    pallas_call x1, Pallas kernels, interior(): pl.pallas_call(interior_kernel, in_specs=[vmem] * 2 + [hbm] * 2, out_spec...  5.8 us
    pallas_call x1, Pallas kernels, load(): pl.pallas_call(functools.partial(load_kernel, links), in_specs=[hbm] * 6,...  5.21 us
    pallas_call x2, Pallas kernels, remap(): pl.pallas_call(functools.partial(remap_kernel, links, rows, cols, numbers...  4.66 us
    ppermute x1, starting transfers between devices, local(): from_south = lax.ppermute(to_north, 'lat', ring('lat', 1))  2.64 us
    ppermute x1, starting transfers between devices, local(): from_north = lax.ppermute(to_south, 'lat', ring('lat', -1))  2.31 us
    ppermute x1, starting transfers between devices, local(): from_east = lax.ppermute(to_west, 'lon', ring('lon', -1))  2.3 us
    pallas_call x1, Pallas kernels, column_fix(): pl.pallas_call(functools.partial(column_kernel, levels), in_specs=[vmem]...  0.96 us
  transfers between devices with their start and end apart: 5, of which 0 were waited for; matrix products, arithmetic and copies ran while one was open for 0% of the time, Pallas kernels for 37%

profile of v7, /device:TPU:0, one launch (start us, length us, event | category | flops | bytes accessed | tf_op | source)
XLA Modules:
  0.0 30.7 jit_solution(6774837993212770423)
XLA Ops:
  0.0 5.2 %load.1 = (f32[2,48,128,128]{3,2,1,0:T(8,128)S(1)}, f32[48,128,128]{2,1,0:T(8,128)S(1)}, f32[6,128,128]{2,1,0:T(8,128)S(1)}, f32[432,128]{1,0:T(8,128)S(1)}, f32...) custom-call(f32[2,48,128,128]{3,2,1,0:T(8,128)} %tracers.1, ...), custom_call_target="tpu_custom_call" | custom-call | tf_op jit(solution)/shard_map/load/pallas_call | solution.py:178
  5.2 0.5 %collective-permute-start = (f32[432,128]{1,0:T(8,128)S(1)}, f32[432,128]{1,0:T(8,128)S(1)}, u32[]{:S(2)}, u32[]{:S(2)}) collective-permute-start(f32[432,128]{1,0:T(8,128)S(1)} %get-tuple-element.22), channel_id=1, source_target_pairs={{0,1},{1,2},{2,3},{3,4},{4,5},{5,6},{6,7},{7,0},{8,9},{9,10},{10,1... | collective-permute-start | bytes 663560 | tf_op jit(solution)/shard_map/ppermute | solution.py:669
  5.7 2.6 %collective-permute-start.2 = (f32[416,128]{1,0:T(8,128)S(1)}, f32[416,128]{1,0:T(8,128)S(1)}, u32[]{:S(2)}, u32[]{:S(2)}) collective-permute-start(f32[416,128]{1,0:T(8,128)S(1)} %get-tuple-element.25), channel_id=1, source_target_pairs={{0,8},{8,16},{16,24},{24,0},{1,9},{9,17},{17,25},{25,1},{2,10},{10... | collective-permute-start | bytes 638984 | tf_op jit(solution)/shard_map/ppermute | solution.py:667
  8.4 2.3 %collective-permute-start.1 = (f32[256,128]{1,0:T(8,128)S(1)}, f32[256,128]{1,0:T(8,128)S(1)}, u32[]{:S(2)}, u32[]{:S(2)}) collective-permute-start(f32[256,128]{1,0:T(8,128)S(1)} %get-tuple-element.23), channel_id=1, source_target_pairs={{0,7},{1,0},{2,1},{3,2},{4,3},{5,4},{6,5},{7,6},{8,15},{9,8},{10,9... | collective-permute-start | bytes 393224 | tf_op jit(solution)/shard_map/ppermute | solution.py:670
  10.7 2.3 %collective-permute-start.3 = (f32[192,128]{1,0:T(8,128)S(1)}, f32[192,128]{1,0:T(8,128)S(1)}, u32[]{:S(2)}, u32[]{:S(2)}) collective-permute-start(f32[192,128]{1,0:T(8,128)S(1)} %get-tuple-element.26), channel_id=1, source_target_pairs={{0,24},{8,0},{16,8},{24,16},{1,25},{9,1},{17,9},{25,17},{2,26},{10... | collective-permute-start | bytes 294920 | tf_op jit(solution)/shard_map/ppermute | solution.py:668
  13.0 0.0 collective-permute-start.4
  13.0 0.0 copy-start
  13.0 0.0 copy-start.1
  13.0 0.0 copy-start.2
  13.0 5.8 %interior.1 = (f32[2,48,128,128]{3,2,1,0:T(8,128)S(1)}, f32[48,128,128]{2,1,0:T(8,128)S(1)}) custom-call(f32[2,48,128,128]{3,2,1,0:T(8,128)S(1)} %get-tuple-element.17.cells, f32[48,128,128]{2,1,0:T(8,128)S(1)} %get-tuple-element.18.east, f32[48,128,128]{2,1,0:T(8,128)} %north_courant.3, f32[48,128,128]{2,1,0:T(8,128)} %diffusivity.1), custom_call_target="tpu_custom_call" | custom-call | tf_op jit(solution)/shard_map/interior/pallas_call | solution.py:275
  18.8 0.0 collective-permute-done.1.from_east
  18.8 0.0 collective-permute-done.from_west.refs_1_
  18.8 1.0 %column_fix.1.refs_3_.fix = f32[2,2,128,128]{3,2,1,0:T(8,128)S(1)} custom-call(f32[6,128,128]{2,1,0:T(8,128)S(1)} %get-tuple-element.21.own, f32[432,128]{1,0:T(8,128)S(1)} %collective-permute-done.from_west.refs_1_, f32[256,128]{1,0:T(8,128)S(1)} %collective-permute-done.1.from_east), custom_call_target="tpu_custom_call" | custom-call | tf_op jit(solution)/shard_map/column_fix/pallas_call | solution.py:421
  19.8 0.0 copy-done
  19.8 2.3 %remap.2.refs_2_.upper = f32[2,160,256]{2,1,0:T(8,128)S(1)} custom-call(s32[4,6144]{1,0:T(4,128)S(1)} %bitcast.3, f32[176,128]{1,0:T(8,128)S(1)} %get-tuple-element.27.refs_0_, f32[432,128]{1,0:T(8,128)S(1)} %collective-permute-done.from_west.refs_1_), custom_call_target="tpu_custom_call" | custom-call | tf_op jit(solution)/shard_map/remap/pallas_call | solution.py:358
  22.1 0.0 collective-permute-done.4.refs_1_
  22.1 0.0 collective-permute-done.2.refs_0_.from_south
  22.1 2.3 %remap.3.lower = f32[2,160,256]{2,1,0:T(8,128)S(1)} custom-call(s32[4,6144]{1,0:T(4,128)S(1)} %bitcast.4, f32[416,128]{1,0:T(8,128)S(1)} %collective-permute-done.2.refs_0_.from_south, f32[176,128]{1,0:T(8,128)S(1)} %collective-permute-done.4.refs_1_, f32[2,160,256]{2,1,0:T(8,128)S(1)} %remap.2.refs_2_.upper, f32[2,2,128,128]{3,2,1,0:T(8,128)S(1)} %column_fix.1.refs_3_.fix), custom_call_target="tpu_custom_call" | custom-call | tf_op jit(solution)/shard_map/remap/pallas_call | solution.py:358
  24.5 0.0 collective-permute-done.3.from_north
  24.5 0.0 copy-done.1
  24.5 0.0 copy-done.2
  24.5 6.0 %step.1 = f32[2,48,128,128]{3,2,1,0:T(8,128)} custom-call(f32[2,48]{1,0:T(2,128)S(1)} %copy-done.2, f32[2,48,128,128]{3,2,1,0:T(8,128)S(1)} %get-tuple-element.17.cells, f32[2,48,128,128]{3,2,1,0:T(8,128)S(1)} %get-tuple-element.19.advected, f32[48,128,128]{2,1,0:T(8,128)S(1)} %get-tuple-element.20.diff, s32[128,128]{1,0:T(8,128)S(1)} %copy-done.1, ...), custom_call_target="tpu_custom_call" | custom-call | tf_op jit(solution)/shard_map/step/pallas_call | solution.py:620
Async XLA Ops:
  5.2 13.6 %collective-permute-start = (f32[432,128]{1,0:T(8,128)S(1)}, f32[432,128]{1,0:T(8,128)S(1)}, u32[]{:S(2)}, u32[]{:S(2)}) collective-permute-start(f32[432,128]{1,0:T(8,128)S(1)} %get-tuple-element.22), channel_id=1, source_target_pairs={{0,1},{1,2},{2,3},{3,4},{4,5},{5,6},{6,7},{7,0},{8,9},{9,10},{10,1... | collective-permute-start | bytes 663560 | tf_op jit(solution)/shard_map/ppermute | solution.py:669
  5.7 16.4 %collective-permute-start.2 = (f32[416,128]{1,0:T(8,128)S(1)}, f32[416,128]{1,0:T(8,128)S(1)}, u32[]{:S(2)}, u32[]{:S(2)}) collective-permute-start(f32[416,128]{1,0:T(8,128)S(1)} %get-tuple-element.25), channel_id=1, source_target_pairs={{0,8},{8,16},{16,24},{24,0},{1,9},{9,17},{17,25},{25,1},{2,10},{10... | collective-permute-start | bytes 638984 | tf_op jit(solution)/shard_map/ppermute | solution.py:667
  8.4 10.4 %collective-permute-start.1 = (f32[256,128]{1,0:T(8,128)S(1)}, f32[256,128]{1,0:T(8,128)S(1)}, u32[]{:S(2)}, u32[]{:S(2)}) collective-permute-start(f32[256,128]{1,0:T(8,128)S(1)} %get-tuple-element.23), channel_id=1, source_target_pairs={{0,7},{1,0},{2,1},{3,2},{4,3},{5,4},{6,5},{7,6},{8,15},{9,8},{10,9... | collective-permute-start | bytes 393224 | tf_op jit(solution)/shard_map/ppermute | solution.py:670
  10.7 13.8 %collective-permute-start.3 = (f32[192,128]{1,0:T(8,128)S(1)}, f32[192,128]{1,0:T(8,128)S(1)}, u32[]{:S(2)}, u32[]{:S(2)}) collective-permute-start(f32[192,128]{1,0:T(8,128)S(1)} %get-tuple-element.26), channel_id=1, source_target_pairs={{0,24},{8,0},{16,8},{24,16},{1,25},{9,1},{17,9},{25,17},{2,26},{10... | collective-permute-start | bytes 294920 | tf_op jit(solution)/shard_map/ppermute | solution.py:668
  13.0 9.2 %collective-permute-start.4 = (f32[176,128]{1,0:T(8,128)S(1)}, f32[176,128]{1,0:T(8,128)S(1)}, u32[]{:S(2)}, u32[]{:S(2)}) collective-permute-start(f32[176,128]{1,0:T(8,128)S(1)} %get-tuple-element.28), channel_id=1, source_target_pairs={{0,9},{1,10},{2,11},{3,12},{4,13},{5,14},{6,15},{7,8},{8,17},{9,18... | collective-permute-start | bytes 270344 | tf_op jit(solution)/shard_map/ppermute | solution.py:666
  13.0 6.8 %copy-start = (s32[1,4,6144]{2,1,0:T(4,128)S(1)}, s32[1,4,6144]{2,1,0:T(4,128)}, u32[]{:S(2)}) copy-start(s32[1,4,6144]{2,1,0:T(4,128)} %param.18) | copy-start | bytes 294916
  13.0 11.5 %copy-start.1 = (s32[128,128]{1,0:T(8,128)S(1)}, s32[128,128]{1,0:T(8,128)}, u32[]{:S(2)}) copy-start(s32[128,128]{1,0:T(8,128)} %land.1) | copy-start | bytes 196612
  13.0 11.5 %copy-start.2 = (f32[2,48]{1,0:T(2,128)S(1)}, f32[2,48]{1,0:T(2,128)}, u32[]{:S(2)}) copy-start(f32[2,48]{1,0:T(2,128)} %constant.2.clone.tables) | copy-start | bytes 1156
